TPU v7x, 32 devices: a whole 2x2x4 slice. The times are simulated.
32 devices in a mesh: tpair: 8 (over z, x), col: 4 (over y, core).
Axes of the slice: x: 2, y: 2, z: 4, core: 2. Of those that a mesh axis runs over, the one named last changes fastest.
Arguments:
- peramb: bfloat16 [8, 2, 2048, 2048], P('tpair', None, None, 'col'), may hold values from -6 to 6
- sink_ops: bfloat16 [8, 2, 2, 512, 512], P('tpair'), may hold values from -0.1875 to 0.1875
- op_table: bfloat16 [2048, 2, 512], P('tpair'), may hold values from -0.1875 to 0.1875
- row_slot: int32 [2048], replicated, may hold values from 0 to 2047, each once
- pair_source: int32 [8], P('tpair'), may hold values from 0 to 1
- op_index: int32 [16, 2], P('tpair'), may hold values from 0 to 1
- listed_rows: int32 [16, 128], P('tpair'), may hold values from 0 to 511
Outputs:
- contracted: bfloat16 [16, 4, 128, 2, 2048], P('tpair', None, 'col')
Inputs may be any that keep to these rules, and one draw needn't show every extreme that they name: `row_slot`: every position of 0 to 2047 appears once.
All inputs are finite; a program needn't handle non-finite values.
Results may differ from a plain program's by a relative error of at most 0.0049.
Values may be sent and summed in bfloat16 or wider, within the bound.
No kernel may reach another device: no remote copies, remote signals or barrier semaphores. Data moves between devices by JAX's collectives and lax.ppermute only.
A program may use at most 64 MiB of HBM per device.

v0:
```python
import functools

import jax
import jax.numpy as jnp
from jax import lax
from jax.experimental import pallas as pl
from jax.experimental.pallas import tpu as pltpu
from jax.sharding import PartitionSpec as P

NS = 4
LANES = 128
VMEM_LIMIT = 24 * 1024 * 1024
BF16, F32 = jnp.bfloat16, jnp.float32


def iota(shape, dim):
    return lax.broadcasted_iota(jnp.int32, shape, dim)


def dot(a, b):
    return jnp.dot(a, b, preferred_element_type=F32)


def column(row):
    wide = jnp.broadcast_to(row, (LANES, LANES)).astype(F32)
    return jnp.transpose(wide).astype(jnp.int32)


def one_hot(col, first, width):
    tiles = [
        jnp.where(col - (first + n) == iota((col.shape[0], LANES), 1), 1.0, 0.0)
        for n in range(0, width, LANES)
    ]
    return jnp.concatenate(tiles, axis=1).astype(BF16)


def mix_kernel(op_ref, listed_ref, sink_ref, peramb_ref, *refs):
    outs, (left, held, sems) = refs[:-3], refs[-3:]
    n_cols = len(outs)
    products, listed = listed_ref.shape
    eigen, local_cols = sink_ref.shape[-1], peramb_ref.shape[-1]
    loads = [
        pltpu.make_async_copy(
            peramb_ref.at[0, :, pl.ds(s * eigen, eigen), :], held.at[s], sems.at[s]
        )
        for s in range(NS)
    ]
    for load in loads:
        load.start()
    own2 = 2 * listed // n_cols
    me = lax.axis_index("col")
    row = iota((2 * listed, 2 * listed), 0)
    wanted = ((row // own2) ^ me) * (own2 // 2) + (row % own2) // 2 + (row % 2) * listed
    order = jnp.where(wanted == iota((2 * listed, 2 * listed), 1), 1.0, 0.0).astype(BF16)
    for k in range(products):
        op = op_ref[k, 0]
        onehot = one_hot(column(listed_ref[k : k + 1, :]), 0, eigen)
        real = dot(onehot, sink_ref[0, op, 0])
        imag = dot(onehot, sink_ref[0, op, 1])
        top = jnp.concatenate([real, -imag], axis=1)
        bottom = jnp.concatenate([imag, real], axis=1)
        both = jnp.concatenate([top, bottom], axis=0).astype(BF16)
        rows = dot(order, both).astype(BF16)
        for j in range(n_cols):
            at = (j * products + k) * own2
            left[at : at + own2, :] = rows[j * own2 : (j + 1) * own2]
    for s in range(NS):
        loads[s].wait()
        mixed = dot(left[...], held[s].reshape(2 * eigen, local_cols)).astype(BF16)
        for j in range(n_cols):
            for k in range(products):
                at = (j * products + k) * own2
                outs[j][k, s] = mixed[at : at + own2]


def mix(op_index, listed_rows, sink_ops, peramb, n_cols):
    products, listed = listed_rows.shape
    eigen = sink_ops.shape[-1]
    local_cols = peramb.shape[3]
    own2 = 2 * listed // n_cols
    block = jax.ShapeDtypeStruct((products, NS, own2, local_cols), BF16)
    vmem = pl.BlockSpec(memory_space=pltpu.VMEM)
    return pl.pallas_call(
        mix_kernel,
        in_specs=[
            pl.BlockSpec(memory_space=pltpu.SMEM), vmem, vmem, pl.BlockSpec(memory_space=pltpu.HBM)
        ],
        out_specs=[vmem] * n_cols,
        out_shape=[block] * n_cols,
        scratch_shapes=[
            pltpu.VMEM((products * 2 * listed, 2 * eigen), BF16),
            pltpu.VMEM((NS, 2, eigen, local_cols), BF16),
            pltpu.SemaphoreType.DMA((NS,)),
        ],
        compiler_params=pltpu.CompilerParams(vmem_limit_bytes=VMEM_LIMIT),
        cost_estimate=pl.CostEstimate(flops=1000, bytes_accessed=1000, transcendentals=0),
        name="mix",
    )(op_index, listed_rows, sink_ops, peramb)


def add_pieces(places, scalars_ref, slot_ref, pieces, products, eigen):
    source_ref, op_ref = scalars_ref
    blocks = eigen // LANES
    nops = slot_ref.shape[0] // blocks // 2
    pair, side = lax.axis_index("tpair"), lax.axis_index("col") % 2
    cols = []
    for k in range(products):
        op = source_ref[0] * nops + op_ref[k, 1]
        cols += [
            column(slot_ref[pl.ds(op * blocks + b, 1), :]) for b in range(blocks)
        ]
    col = jnp.concatenate(cols, axis=0)
    tiles, tables = [], []
    for place, piece in zip(places, pieces):
        height = piece.shape[0]
        first = place
        if isinstance(place, tuple):
            first = (2 * (pair ^ place[0]) + (side ^ place[1])) * height
        tiles.append(one_hot(col, first, height))
        tables.append(piece[...])
    return dot(jnp.concatenate(tiles, axis=1), jnp.concatenate(tables, axis=0))


def assemble_kernel(places, source_ref, op_ref, slot_ref, *refs):
    pieces, out_ref = refs[:-1], refs[-1]
    products, eigen = out_ref.shape[0], out_ref.shape[2]
    total = add_pieces(places, (source_ref, op_ref), slot_ref, pieces, products, eigen)
    total = total.astype(BF16)
    for k in range(products):
        rows = slice(k * eigen, (k + 1) * eigen)
        out_ref[k, :eigen] = total[rows, :eigen]
        out_ref[k, eigen:] = total[rows, eigen:]


def assemble(places, pieces, source, op_index, slots, eigen):
    products = op_index.shape[0]
    vmem = pl.BlockSpec(memory_space=pltpu.VMEM)
    smem = pl.BlockSpec(memory_space=pltpu.SMEM)
    return pl.pallas_call(
        functools.partial(assemble_kernel, places),
        in_specs=[smem, smem] + [vmem] * (1 + len(pieces)),
        out_specs=vmem,
        out_shape=jax.ShapeDtypeStruct((products, 2 * eigen, eigen), BF16),
        compiler_params=pltpu.CompilerParams(vmem_limit_bytes=VMEM_LIMIT),
        cost_estimate=pl.CostEstimate(flops=1000, bytes_accessed=1000, transcendentals=0),
        name="assemble",
    )(source, op_index, slots, *pieces)


def contract_kernel(places, n_cols, source_ref, op_ref, slot_ref, partial_ref, *refs):
    n_pieces = len(places)
    pieces, blocks = refs[:n_pieces], refs[n_pieces : n_pieces + n_cols]
    out_ref, right, done, sems = refs[n_pieces + n_cols :]
    own2, local_cols = blocks[0].shape[2], blocks[0].shape[3]
    products, eigen = right.shape[0], right.shape[2]
    rows = NS * own2
    total = add_pieces(places, (source_ref, op_ref), slot_ref, pieces, products, eigen)
    total = total.astype(BF16)
    for p in range(products):
        some = slice(p * eigen, (p + 1) * eigen)
        right[p, :eigen] = partial_ref[p, :eigen] + total[some, :eigen]
        right[p, eigen:] = partial_ref[p, eigen:] + total[some, eigen:]
    me = lax.axis_index("col")
    per_time = eigen // local_cols
    times = n_cols // per_time
    odd = iota((rows, local_cols), 0) % 2 == 1
    copies = []
    for k in range(products):
        direct, turned = [], []
        for j in range(n_cols):
            x = blocks[j][k].reshape(rows, local_cols)
            wide = x.astype(F32)
            y = jnp.where(odd, pltpu.roll(wide, 1, 0), -pltpu.roll(wide, rows - 1, 0))
            direct.append(x)
            turned.append(y.astype(BF16))
        if per_time == 1:
            lhs = jnp.concatenate(
                [jnp.concatenate(direct, axis=0), jnp.concatenate(turned, axis=0)], axis=1
            )
            result = dot(lhs, right[k])
        else:
            result = []
            for j in range(n_cols):
                first = pl.multiple_of(((me ^ j) % per_time) * local_cols, local_cols)
                second = pl.multiple_of(eigen + first, local_cols)
                part = dot(direct[j], right[k, pl.ds(first, local_cols), :])
                part += dot(turned[j], right[k, pl.ds(second, local_cols), :])
                if j % per_time:
                    result[-1] += part
                else:
                    result.append(part)
            result = jnp.concatenate(result, axis=0)
        result = result.astype(BF16)
        for g in range(times):
            slot = k * times + g
            block = result[g * rows : (g + 1) * rows]
            done[slot] = block.reshape(NS, own2 // 2, 2, eigen)
            at = pl.multiple_of(((me ^ (g * per_time)) // per_time) * eigen, eigen)
            copy = pltpu.make_async_copy(
                done.at[slot], out_ref.at[k, :, :, :, pl.ds(at, eigen)], sems.at[slot]
            )
            copy.start()
            copies.append(copy)
    for copy in copies:
        copy.wait()


def contract(places, pieces, partial, source, op_index, slots, blocks):
    products, _, own2, local_cols = blocks[0].shape
    n_cols = len(blocks)
    eigen = partial.shape[2]
    order = n_cols * local_cols
    times = order // eigen
    vmem = pl.BlockSpec(memory_space=pltpu.VMEM)
    smem = pl.BlockSpec(memory_space=pltpu.SMEM)
    return pl.pallas_call(
        functools.partial(contract_kernel, places, n_cols),
        in_specs=[smem, smem] + [vmem] * (2 + len(pieces) + n_cols),
        out_specs=pl.BlockSpec(memory_space=pl.ANY),
        out_shape=jax.ShapeDtypeStruct((products, NS, own2 // 2, 2, order), BF16),
        scratch_shapes=[
            pltpu.VMEM((products, 2 * eigen, eigen), BF16),
            pltpu.VMEM((products * times, NS, own2 // 2, 2, eigen), BF16),
            pltpu.SemaphoreType.DMA((products * times,)),
        ],
        compiler_params=pltpu.CompilerParams(vmem_limit_bytes=VMEM_LIMIT),
        cost_estimate=pl.CostEstimate(
            flops=4 * products * eigen * NS * own2 * order, bytes_accessed=0, transcendentals=0
        ),
        name="contract",
    )(source, op_index, slots, partial, *pieces, *blocks)


def swap(array, axis, size, mask):
    return lax.ppermute(array, axis, [(i, i ^ mask) for i in range(size)])


def after(array, *others):
    return lax.optimization_barrier((array, *others))[0]


def per_device(peramb, sink_ops, op_table, row_slot, pair_source, op_index, listed_rows):
    n_cols = lax.axis_size("col")
    n_pair = lax.axis_size("tpair")
    rows, _, eigen = op_table.shape
    slots = row_slot.reshape(-1, LANES)

    def across(array, mask):
        return swap(array, "tpair", n_pair, mask)

    def beside(array):
        return swap(array, "col", n_cols, 1)

    if n_cols != 4 or n_pair != 8 or rows % 32:
        own = jnp.concatenate([op_table[:, 0], op_table[:, 1]], axis=1)
        whole = lax.all_gather(own, "tpair", axis=0, tiled=True)
        half = whole.shape[0] // 2
        mixed = mix(op_index, listed_rows, sink_ops, peramb, n_cols)
        blocks = [mixed[0]] + [swap(mixed[j], "col", n_cols, j) for j in range(1, n_cols)]
        partial = assemble([0], [whole[:half]], pair_source, op_index, slots, eigen)
        return contract(
            [half], [whole[half:]], partial, pair_source, op_index, slots, blocks
        )
    half = rows // 2
    own = lax.dynamic_slice_in_dim(op_table, lax.axis_index("col") % 2 * half, half, 0)
    own = jnp.concatenate([own[:, 0], own[:, 1]], axis=1)
    held = {(0, 0): own, (0, 1): beside(own)}
    for mask in (4, 2, 1):
        held[mask, 0] = across(own, mask)
    mixed = mix(op_index, after(listed_rows, held[0, 1]), sink_ops, peramb, n_cols)
    cross = swap(mixed[3], "col", n_cols, 2)
    straight = swap(after(mixed[2], cross), "col", n_cols, 2)
    blocks = [mixed[0], beside(mixed[1]), straight, beside(cross)]
    held[3, 0] = across(after(held[2, 0], mixed[0], held[1, 0]), 1)
    held[6, 0] = across(after(own, mixed[0]), 6)
    held[5, 0] = across(after(held[4, 0], held[3, 0]), 1)
    held[6, 1] = beside(held[6, 0])
    held[7, 0] = across(after(held[6, 0], held[6, 1], held[5, 0]), 1)
    for mask in (1, 2, 3, 4, 5):
        held[mask, 1] = beside(held[mask, 0])
    early = [(mask, side) for mask in range(7) for side in (0, 1)]
    partial = assemble(early, [held[p] for p in early], pair_source, op_index, slots, eigen)
    held[7, 1] = beside(after(held[7, 0], partial))
    late = [(7, 0), (7, 1)]
    return contract(
        late, [held[p] for p in late], partial, pair_source, op_index, slots, blocks
    )


def solution(mesh):
    in_specs = (
        P("tpair", None, None, "col"),
        P("tpair", None, None, None, None),
        P("tpair", None, None),
        P(),
        P("tpair"),
        P("tpair", None),
        P("tpair", None),
    )
    out_specs = P("tpair", None, "col", None, None)
    return jax.shard_map(
        per_device, mesh=mesh, in_specs=in_specs, out_specs=out_specs, check_vma=False
    )
```

profile of v0, /device:TPU:0, one launch (start us, length us, event | category | flops | bytes accessed | tf_op | source)
XLA Modules:
  0.0 53.2 jit_solution(4615332423661449785)
XLA Ops:
  0.0 1.6 %constant_dynamic-slice_fusion = (bf16[128,1,512]{2,1,0:T(2,128)(2,1)S(1)}, bf16[128,1,512]{2,1,0:T(2,128)(2,1)S(1)}) fusion(bf16[256,2,512]{2,1,0:T(2,128)(2,1)} %param.9, s32[]{:T(128)S(6)} %select_n.11, s32[]{:T(128)S(6)} %add.9), kind=kLoop, calls=%fused_computation.3 | loop fusion | bytes 524296 | tf_op jit(solution)/shard_map/slice | solution.py:266
  1.7 0.0 copy-start.2
  1.7 0.5 %collective-permute-start = (bf16[128,1024]{1,0:T(8,128)(2,1)S(1)}, bf16[128,1024]{1,0:T(8,128)(2,1)S(1)}, u32[]{:S(2)}, u32[]{:S(2)}) collective-permute-start(bf16[128,1024]{1,0:T(8,128)(2,1)S(1)} %pad_maximum_fusion.refs_0_), channel_id=1, source_target_pairs={{0,1},{1,0},{2,3},{3,2},{4,5},{5,4},{6,7},{7,6},{8,9},{9,8},{10,11... | collective-permute-start | bytes 786440 | tf_op jit(solution)/shard_map/ppermute | solution.py:235
  2.2 2.6 %collective-permute-start.3 = (bf16[128,1024]{1,0:T(8,128)(2,1)S(1)}, bf16[128,1024]{1,0:T(8,128)(2,1)S(1)}, u32[]{:S(2)}, u32[]{:S(2)}) collective-permute-start(bf16[128,1024]{1,0:T(8,128)(2,1)S(1)} %pad_maximum_fusion.refs_0_), channel_id=1, source_target_pairs={{0,8},{4,12},{8,0},{12,4},{16,24},{20,28},{24,16},{28,20},{1,9},{5... | collective-permute-start | bytes 786440 | tf_op jit(solution)/shard_map/ppermute | solution.py:235
  4.9 1.5 %collective-permute-start.1 = (bf16[128,1024]{1,0:T(8,128)(2,1)S(1)}, bf16[128,1024]{1,0:T(8,128)(2,1)S(1)}, u32[]{:S(2)}, u32[]{:S(2)}) collective-permute-start(bf16[128,1024]{1,0:T(8,128)(2,1)S(1)} %pad_maximum_fusion.refs_0_), channel_id=1, source_target_pairs={{0,4},{4,0},{8,12},{12,8},{16,20},{20,16},{24,28},{28,24},{1,5},{5... | collective-permute-start | bytes 786440 | tf_op jit(solution)/shard_map/ppermute | solution.py:235
  6.4 2.6 %collective-permute-start.7 = (bf16[128,1024]{1,0:T(8,128)(2,1)S(1)}, bf16[128,1024]{1,0:T(8,128)(2,1)S(1)}, u32[]{:S(2)}, u32[]{:S(2)}) collective-permute-start(bf16[128,1024]{1,0:T(8,128)(2,1)S(1)} %pad_maximum_fusion.refs_0_), channel_id=1, source_target_pairs={{0,16},{4,20},{8,24},{12,28},{16,0},{20,4},{24,8},{28,12},{1,17},{... | collective-permute-start | bytes 786440 | tf_op jit(solution)/shard_map/ppermute | solution.py:235
  9.0 0.0 copy-start
  9.0 2.2 %copy-done = bf16[1,2,2048,512]{3,2,1,0:T(8,128)(2,1)S(1)} copy-done((bf16[1,2,2048,512]{3,2,1,0:T(8,128)(2,1)S(1)}, bf16[1,2,2048,512]{3,2,1,0:T(8,128)(2,1)}, u32[]{:S(2)}) %copy-start) | copy-done | bytes 4194328
  11.2 4.7 %mix.1 = (bf16[2,4,64,512]{3,2,1,0:T(8,128)(2,1)S(1)}, bf16[2,4,64,512]{3,2,1,0:T(8,128)(2,1)S(1)}, bf16[2,4,64,512]{3,2,1,0:T(8,128)(2,1)S(1)}, bf16[2,4,64,512]{3,2,1,0:T(8,128)(2,1)S(1)}) custom-call(s32[2,2]{1,0:T(2,128)S(1)} %copy-done.3, s32[2,128]{1,0:T(2,128)S(1)} %copy-done.4, bf16[1,2,2,512,512]{4,3,2,1,0:T(8,128)(2,1)S(1)} %copy-done.1, ...), custom_call_target="tpu_custom_call" | custom-call | flops 1000 | bytes 1000 | tf_op jit(solution)/shard_map/mix/pallas_call | solution.py:83
  15.9 0.1 collective-permute-done.3.refs_4_
  16.1 2.6 %collective-permute-start.5 = (bf16[128,1024]{1,0:T(8,128)(2,1)S(1)}, bf16[128,1024]{1,0:T(8,128)(2,1)S(1)}, u32[]{:S(2)}, u32[]{:S(2)}) collective-permute-start(bf16[128,1024]{1,0:T(8,128)(2,1)S(1)} %collective-permute-done.3.refs_4_), channel_id=1, source_target_pairs={{0,4},{4,0},{8,12},{12,8},{16,20},{20,16},{24,28},{28,24},{1,5},{5... | collective-permute-start | bytes 786440 | tf_op jit(solution)/shard_map/ppermute | solution.py:235
  18.7 2.5 %collective-permute-start.11 = (bf16[128,1024]{1,0:T(8,128)(2,1)S(1)}, bf16[128,1024]{1,0:T(8,128)(2,1)S(1)}, u32[]{:S(2)}, u32[]{:S(2)}) collective-permute-start(bf16[128,1024]{1,0:T(8,128)(2,1)S(1)} %pad_maximum_fusion.refs_0_), channel_id=1, source_target_pairs={{0,24},{4,28},{8,16},{12,20},{16,8},{20,12},{24,0},{28,4},{1,25},{... | collective-permute-start | bytes 786440 | tf_op jit(solution)/shard_map/ppermute | solution.py:235
  21.2 1.5 %collective-permute-start.16 = (bf16[2,4,64,512]{3,2,1,0:T(8,128)(2,1)S(1)}, bf16[2,4,64,512]{3,2,1,0:T(8,128)(2,1)S(1)}, u32[]{:S(2)}, u32[]{:S(2)}) collective-permute-start(bf16[2,4,64,512]{3,2,1,0:T(8,128)(2,1)S(1)} %get-tuple-element.25), channel_id=1, source_target_pairs={{0,2},{1,3},{2,0},{3,1},{4,6},{5,7},{6,4},{7,5},{8,10},{9,11},{10,... | collective-permute-start | bytes 1572872 | tf_op jit(solution)/shard_map/ppermute | solution.py:235
  22.7 0.0 collective-permute-done.7.refs_8_
  22.7 2.1 %collective-permute-done.5.refs_6_ = bf16[128,1024]{1,0:T(8,128)(2,1)S(1)} collective-permute-done((bf16[128,1024]{1,0:T(8,128)(2,1)S(1)}, bf16[128,1024]{1,0:T(8,128)(2,1)S(1)}, u32[]{:S(2)}, u32[]{:S(2)}) %collective-permute-start.5) | collective-permute-done | bytes 262176 | tf_op jit(solution)/shard_map/ppermute | solution.py:235
  24.8 1.7 %collective-permute-start.9 = (bf16[128,1024]{1,0:T(8,128)(2,1)S(1)}, bf16[128,1024]{1,0:T(8,128)(2,1)S(1)}, u32[]{:S(2)}, u32[]{:S(2)}) collective-permute-start(bf16[128,1024]{1,0:T(8,128)(2,1)S(1)} %collective-permute-done.7.refs_8_), channel_id=1, source_target_pairs={{0,4},{4,0},{8,12},{12,8},{16,20},{20,16},{24,28},{28,24},{1,5},{5... | collective-permute-start | bytes 786440 | tf_op jit(solution)/shard_map/ppermute | solution.py:235
  26.6 1.6 %collective-permute-done.11.refs_12_ = bf16[128,1024]{1,0:T(8,128)(2,1)S(1)} collective-permute-done((bf16[128,1024]{1,0:T(8,128)(2,1)S(1)}, bf16[128,1024]{1,0:T(8,128)(2,1)S(1)}, u32[]{:S(2)}, u32[]{:S(2)}) %collective-permute-start.11) | collective-permute-done | bytes 262176 | tf_op jit(solution)/shard_map/ppermute | solution.py:235
  28.2 0.0 collective-permute-start.12
  28.2 0.5 collective-permute-start.8
  28.7 0.0 collective-permute-start.4
  28.7 3.4 %collective-permute-done.9.refs_10_ = bf16[128,1024]{1,0:T(8,128)(2,1)S(1)} collective-permute-done((bf16[128,1024]{1,0:T(8,128)(2,1)S(1)}, bf16[128,1024]{1,0:T(8,128)(2,1)S(1)}, u32[]{:S(2)}, u32[]{:S(2)}) %collective-permute-start.9) | collective-permute-done | bytes 262176 | tf_op jit(solution)/shard_map/ppermute | solution.py:235
  32.1 0.0 collective-permute-start.2
  32.1 0.5 collective-permute-start.6
  32.7 1.5 %collective-permute-done.16 = bf16[2,4,64,512]{3,2,1,0:T(8,128)(2,1)S(1)} collective-permute-done((bf16[2,4,64,512]{3,2,1,0:T(8,128)(2,1)S(1)}, bf16[2,4,64,512]{3,2,1,0:T(8,128)(2,1)S(1)}, u32[]{:S(2)}, u32[]{:S(2)}) %collective-permute-start.16) | collective-permute-done | bytes 524320 | tf_op jit(solution)/shard_map/ppermute | solution.py:235
  34.1 0.3 collective-permute-start.13
  34.4 0.3 collective-permute-start.15
  34.7 1.5 %collective-permute-start.17 = (bf16[2,4,64,512]{3,2,1,0:T(8,128)(2,1)S(1)}, bf16[2,4,64,512]{3,2,1,0:T(8,128)(2,1)S(1)}, u32[]{:S(2)}, u32[]{:S(2)}) collective-permute-start(bf16[2,4,64,512]{3,2,1,0:T(8,128)(2,1)S(1)} %get-tuple-element.26), channel_id=1, source_target_pairs={{0,2},{1,3},{2,0},{3,1},{4,6},{5,7},{6,4},{7,5},{8,10},{9,11},{10,... | collective-permute-start | bytes 1572872 | tf_op jit(solution)/shard_map/ppermute | solution.py:235
  36.9 4.6 %assemble.1.partial_ref = bf16[2,1024,512]{2,1,0:T(8,128)(2,1)S(1)} custom-call(s32[1]{0:T(128)S(6)} %copy.14.source_ref, s32[2,2]{1,0:T(2,128)S(1)} %copy-done.3, s32[16,128]{1,0:T(8,128)S(1)} %bitcast.5, bf16[128,1024]{1,0:T(8,128)(2,1)S(1)} %pad_maximum_fusion.refs_0_, bf16[128,1024]{1,0:T(8,128)(2,1)S(1)} %collective-permute-done.refs_1_, ...), custom_call_target="tpu_custom_call" | custom-call | flops 1000 | bytes 1000 | tf_op jit(solution)/shard_map/assemble/pallas_call | solution.py:139
  41.5 1.4 %collective-permute-done.13.refs_0_ = bf16[128,1024]{1,0:T(8,128)(2,1)S(1)} collective-permute-done((bf16[128,1024]{1,0:T(8,128)(2,1)S(1)}, bf16[128,1024]{1,0:T(8,128)(2,1)S(1)}, u32[]{:S(2)}, u32[]{:S(2)}) %collective-permute-start.13) | collective-permute-done | bytes 262176 | tf_op jit(solution)/shard_map/ppermute | solution.py:235
  42.9 1.5 %collective-permute-done.14.refs_1_ = bf16[128,1024]{1,0:T(8,128)(2,1)S(1)} collective-permute-done((bf16[128,1024]{1,0:T(8,128)(2,1)S(1)}, bf16[128,1024]{1,0:T(8,128)(2,1)S(1)}, u32[]{:S(2)}, u32[]{:S(2)}) %collective-permute-start.14) | collective-permute-done | bytes 262176 | tf_op jit(solution)/shard_map/ppermute | solution.py:235
  44.4 4.4 %collective-permute-done.17.refs_4_ = bf16[2,4,64,512]{3,2,1,0:T(8,128)(2,1)S(1)} collective-permute-done((bf16[2,4,64,512]{3,2,1,0:T(8,128)(2,1)S(1)}, bf16[2,4,64,512]{3,2,1,0:T(8,128)(2,1)S(1)}, u32[]{:S(2)}, u32[]{:S(2)}) %collective-permute-start.17) | collective-permute-done | bytes 524320 | tf_op jit(solution)/shard_map/ppermute | solution.py:235
  48.8 4.4 %contract.1 = bf16[2,4,32,2,2048]{4,3,2,1,0:T(2,128)(2,1)} custom-call(s32[1]{0:T(128)S(6)} %copy.14.source_ref, s32[2,2]{1,0:T(2,128)S(1)} %copy-done.3, s32[16,128]{1,0:T(8,128)S(1)} %bitcast.6, bf16[2,1024,512]{2,1,0:T(8,128)(2,1)S(1)} %assemble.1.partial_ref, bf16[128,1024]{1,0:T(8,128)(2,1)S(1)} %collective-permute-done.13.refs_0_, ...), custom_call_target="tpu_custom_call" | custom-call | flops 2147483648 | tf_op jit(solution)/shard_map/contract/pallas_call | solution.py:216
  (22 shorter events, 0.1 us)
Async XLA Ops:
  0.0 9.0 %copy-start.4 = (s32[2,128]{1,0:T(2,128)S(1)}, s32[2,128]{1,0:T(2,128)}, u32[]{:S(2)}) copy-start(s32[2,128]{1,0:T(2,128)} %listed_ref) | copy-start | bytes 3076
  0.0 9.0 %copy-start.3 = (s32[2,2]{1,0:T(2,128)S(1)}, s32[2,2]{1,0:T(2,128)}, u32[]{:S(2)}) copy-start(s32[2,2]{1,0:T(2,128)} %op_ref.5) | copy-start | bytes 52
  0.0 9.0 %copy-start.1 = (bf16[1,2,2,512,512]{4,3,2,1,0:T(8,128)(2,1)S(1)}, bf16[1,2,2,512,512]{4,3,2,1,0:T(8,128)(2,1)}, u32[]{:S(2)}) copy-start(bf16[1,2,2,512,512]{4,3,2,1,0:T(8,128)(2,1)} %sink_ref.1) | copy-start | bytes 6291460
  1.7 35.2 %copy-start.2 = (s32[2048]{0:T(1024)S(1)}, s32[2048]{0:T(1024)}, u32[]{:S(2)}) copy-start(s32[2048]{0:T(1024)} %param.10) | copy-start | bytes 24580
  1.7 7.3 %collective-permute-start = (bf16[128,1024]{1,0:T(8,128)(2,1)S(1)}, bf16[128,1024]{1,0:T(8,128)(2,1)S(1)}, u32[]{:S(2)}, u32[]{:S(2)}) collective-permute-start(bf16[128,1024]{1,0:T(8,128)(2,1)S(1)} %pad_maximum_fusion.refs_0_), channel_id=1, source_target_pairs={{0,1},{1,0},{2,3},{3,2},{4,5},{5,4},{6,7},{7,6},{8,9},{9,8},{10,11... | collective-permute-start | bytes 786440 | tf_op jit(solution)/shard_map/ppermute | solution.py:235
  2.2 13.8 %collective-permute-start.3 = (bf16[128,1024]{1,0:T(8,128)(2,1)S(1)}, bf16[128,1024]{1,0:T(8,128)(2,1)S(1)}, u32[]{:S(2)}, u32[]{:S(2)}) collective-permute-start(bf16[128,1024]{1,0:T(8,128)(2,1)S(1)} %pad_maximum_fusion.refs_0_), channel_id=1, source_target_pairs={{0,8},{4,12},{8,0},{12,4},{16,24},{20,28},{24,16},{28,20},{1,9},{5... | collective-permute-start | bytes 786440 | tf_op jit(solution)/shard_map/ppermute | solution.py:235
  4.9 11.2 %collective-permute-start.1 = (bf16[128,1024]{1,0:T(8,128)(2,1)S(1)}, bf16[128,1024]{1,0:T(8,128)(2,1)S(1)}, u32[]{:S(2)}, u32[]{:S(2)}) collective-permute-start(bf16[128,1024]{1,0:T(8,128)(2,1)S(1)} %pad_maximum_fusion.refs_0_), channel_id=1, source_target_pairs={{0,4},{4,0},{8,12},{12,8},{16,20},{20,16},{24,28},{28,24},{1,5},{5... | collective-permute-start | bytes 786440 | tf_op jit(solution)/shard_map/ppermute | solution.py:235
  6.4 16.3 %collective-permute-start.7 = (bf16[128,1024]{1,0:T(8,128)(2,1)S(1)}, bf16[128,1024]{1,0:T(8,128)(2,1)S(1)}, u32[]{:S(2)}, u32[]{:S(2)}) collective-permute-start(bf16[128,1024]{1,0:T(8,128)(2,1)S(1)} %pad_maximum_fusion.refs_0_), channel_id=1, source_target_pairs={{0,16},{4,20},{8,24},{12,28},{16,0},{20,4},{24,8},{28,12},{1,17},{... | collective-permute-start | bytes 786440 | tf_op jit(solution)/shard_map/ppermute | solution.py:235
  9.0 2.2 %copy-start = (bf16[1,2,2048,512]{3,2,1,0:T(8,128)(2,1)S(1)}, bf16[1,2,2048,512]{3,2,1,0:T(8,128)(2,1)}, u32[]{:S(2)}) copy-start(bf16[1,2,2048,512]{3,2,1,0:T(8,128)(2,1)} %peramb_ref.1) | copy-start | bytes 12582916
  16.1 8.8 %collective-permute-start.5 = (bf16[128,1024]{1,0:T(8,128)(2,1)S(1)}, bf16[128,1024]{1,0:T(8,128)(2,1)S(1)}, u32[]{:S(2)}, u32[]{:S(2)}) collective-permute-start(bf16[128,1024]{1,0:T(8,128)(2,1)S(1)} %collective-permute-done.3.refs_4_), channel_id=1, source_target_pairs={{0,4},{4,0},{8,12},{12,8},{16,20},{20,16},{24,28},{28,24},{1,5},{5... | collective-permute-start | bytes 786440 | tf_op jit(solution)/shard_map/ppermute | solution.py:235
  18.7 9.5 %collective-permute-start.11 = (bf16[128,1024]{1,0:T(8,128)(2,1)S(1)}, bf16[128,1024]{1,0:T(8,128)(2,1)S(1)}, u32[]{:S(2)}, u32[]{:S(2)}) collective-permute-start(bf16[128,1024]{1,0:T(8,128)(2,1)S(1)} %pad_maximum_fusion.refs_0_), channel_id=1, source_target_pairs={{0,24},{4,28},{8,16},{12,20},{16,8},{20,12},{24,0},{28,4},{1,25},{... | collective-permute-start | bytes 786440 | tf_op jit(solution)/shard_map/ppermute | solution.py:235
  21.2 12.9 %collective-permute-start.16 = (bf16[2,4,64,512]{3,2,1,0:T(8,128)(2,1)S(1)}, bf16[2,4,64,512]{3,2,1,0:T(8,128)(2,1)S(1)}, u32[]{:S(2)}, u32[]{:S(2)}) collective-permute-start(bf16[2,4,64,512]{3,2,1,0:T(8,128)(2,1)S(1)} %get-tuple-element.25), channel_id=1, source_target_pairs={{0,2},{1,3},{2,0},{3,1},{4,6},{5,7},{6,4},{7,5},{8,10},{9,11},{10,... | collective-permute-start | bytes 1572872 | tf_op jit(solution)/shard_map/ppermute | solution.py:235
  24.8 7.3 %collective-permute-start.9 = (bf16[128,1024]{1,0:T(8,128)(2,1)S(1)}, bf16[128,1024]{1,0:T(8,128)(2,1)S(1)}, u32[]{:S(2)}, u32[]{:S(2)}) collective-permute-start(bf16[128,1024]{1,0:T(8,128)(2,1)S(1)} %collective-permute-done.7.refs_8_), channel_id=1, source_target_pairs={{0,4},{4,0},{8,12},{12,8},{16,20},{20,16},{24,28},{28,24},{1,5},{5... | collective-permute-start | bytes 786440 | tf_op jit(solution)/shard_map/ppermute | solution.py:235
  28.2 3.9 %collective-permute-start.12 = (bf16[128,1024]{1,0:T(8,128)(2,1)S(1)}, bf16[128,1024]{1,0:T(8,128)(2,1)S(1)}, u32[]{:S(2)}, u32[]{:S(2)}) collective-permute-start(bf16[128,1024]{1,0:T(8,128)(2,1)S(1)} %collective-permute-done.11.refs_12_), channel_id=1, source_target_pairs={{0,1},{1,0},{2,3},{3,2},{4,5},{5,4},{6,7},{7,6},{8,9},{9,8},{10,11... | collective-permute-start | bytes 786440 | tf_op jit(solution)/shard_map/ppermute | solution.py:235
  28.2 5.9 %collective-permute-start.8 = (bf16[128,1024]{1,0:T(8,128)(2,1)S(1)}, bf16[128,1024]{1,0:T(8,128)(2,1)S(1)}, u32[]{:S(2)}, u32[]{:S(2)}) collective-permute-start(bf16[128,1024]{1,0:T(8,128)(2,1)S(1)} %collective-permute-done.7.refs_8_), channel_id=1, source_target_pairs={{0,1},{1,0},{2,3},{3,2},{4,5},{5,4},{6,7},{7,6},{8,9},{9,8},{10,11... | collective-permute-start | bytes 786440 | tf_op jit(solution)/shard_map/ppermute | solution.py:235
  28.7 5.7 %collective-permute-start.4 = (bf16[128,1024]{1,0:T(8,128)(2,1)S(1)}, bf16[128,1024]{1,0:T(8,128)(2,1)S(1)}, u32[]{:S(2)}, u32[]{:S(2)}) collective-permute-start(bf16[128,1024]{1,0:T(8,128)(2,1)S(1)} %collective-permute-done.3.refs_4_), channel_id=1, source_target_pairs={{0,1},{1,0},{2,3},{3,2},{4,5},{5,4},{6,7},{7,6},{8,9},{9,8},{10,11... | collective-permute-start | bytes 786440 | tf_op jit(solution)/shard_map/ppermute | solution.py:235
  32.1 2.6 %collective-permute-start.2 = (bf16[128,1024]{1,0:T(8,128)(2,1)S(1)}, bf16[128,1024]{1,0:T(8,128)(2,1)S(1)}, u32[]{:S(2)}, u32[]{:S(2)}) collective-permute-start(bf16[128,1024]{1,0:T(8,128)(2,1)S(1)} %collective-permute-done.1.refs_2_), channel_id=1, source_target_pairs={{0,1},{1,0},{2,3},{3,2},{4,5},{5,4},{6,7},{7,6},{8,9},{9,8},{10,11... | collective-permute-start | bytes 786440 | tf_op jit(solution)/shard_map/ppermute | solution.py:235
  32.1 4.1 %collective-permute-start.6 = (bf16[128,1024]{1,0:T(8,128)(2,1)S(1)}, bf16[128,1024]{1,0:T(8,128)(2,1)S(1)}, u32[]{:S(2)}, u32[]{:S(2)}) collective-permute-start(bf16[128,1024]{1,0:T(8,128)(2,1)S(1)} %collective-permute-done.5.refs_6_), channel_id=1, source_target_pairs={{0,1},{1,0},{2,3},{3,2},{4,5},{5,4},{6,7},{7,6},{8,9},{9,8},{10,11... | collective-permute-start | bytes 786440 | tf_op jit(solution)/shard_map/ppermute | solution.py:235
  34.1 2.8 %collective-permute-start.10 = (bf16[128,1024]{1,0:T(8,128)(2,1)S(1)}, bf16[128,1024]{1,0:T(8,128)(2,1)S(1)}, u32[]{:S(2)}, u32[]{:S(2)}) collective-permute-start(bf16[128,1024]{1,0:T(8,128)(2,1)S(1)} %collective-permute-done.9.refs_10_), channel_id=1, source_target_pairs={{0,1},{1,0},{2,3},{3,2},{4,5},{5,4},{6,7},{7,6},{8,9},{9,8},{10,11... | collective-permute-start | bytes 786440 | tf_op jit(solution)/shard_map/ppermute | solution.py:235
  34.1 8.7 %collective-permute-start.13 = (bf16[128,1024]{1,0:T(8,128)(2,1)S(1)}, bf16[128,1024]{1,0:T(8,128)(2,1)S(1)}, u32[]{:S(2)}, u32[]{:S(2)}) collective-permute-start(bf16[128,1024]{1,0:T(8,128)(2,1)S(1)} %collective-permute-done.11.refs_12_), channel_id=1, source_target_pairs={{0,4},{4,0},{8,12},{12,8},{16,20},{20,16},{24,28},{28,24},{1,5},{5... | collective-permute-start | bytes 786440 | tf_op jit(solution)/shard_map/ppermute | solution.py:235
  34.4 8.4 %collective-permute-start.15 = (bf16[2,4,64,512]{3,2,1,0:T(8,128)(2,1)S(1)}, bf16[2,4,64,512]{3,2,1,0:T(8,128)(2,1)S(1)}, u32[]{:S(2)}, u32[]{:S(2)}) collective-permute-start(bf16[2,4,64,512]{3,2,1,0:T(8,128)(2,1)S(1)} %get-tuple-element.23), channel_id=1, source_target_pairs={{0,1},{1,0},{2,3},{3,2},{4,5},{5,4},{6,7},{7,6},{8,9},{9,8},{10,11... | collective-permute-start | bytes 1572872 | tf_op jit(solution)/shard_map/ppermute | solution.py:235
  34.7 14.0 %collective-permute-start.17 = (bf16[2,4,64,512]{3,2,1,0:T(8,128)(2,1)S(1)}, bf16[2,4,64,512]{3,2,1,0:T(8,128)(2,1)S(1)}, u32[]{:S(2)}, u32[]{:S(2)}) collective-permute-start(bf16[2,4,64,512]{3,2,1,0:T(8,128)(2,1)S(1)} %get-tuple-element.26), channel_id=1, source_target_pairs={{0,2},{1,3},{2,0},{3,1},{4,6},{5,7},{6,4},{7,5},{8,10},{9,11},{10,... | collective-permute-start | bytes 1572872 | tf_op jit(solution)/shard_map/ppermute | solution.py:235
  36.2 12.5 %collective-permute-start.18 = (bf16[2,4,64,512]{3,2,1,0:T(8,128)(2,1)S(1)}, bf16[2,4,64,512]{3,2,1,0:T(8,128)(2,1)S(1)}, u32[]{:S(2)}, u32[]{:S(2)}) collective-permute-start(bf16[2,4,64,512]{3,2,1,0:T(8,128)(2,1)S(1)} %collective-permute-done.16), channel_id=1, source_target_pairs={{0,1},{1,0},{2,3},{3,2},{4,5},{5,4},{6,7},{7,6},{8,9},{9,8},{10,11... | collective-permute-start | bytes 1572872 | tf_op jit(solution)/shard_map/ppermute | solution.py:235
  42.8 1.5 %collective-permute-start.14 = (bf16[128,1024]{1,0:T(8,128)(2,1)S(1)}, bf16[128,1024]{1,0:T(8,128)(2,1)S(1)}, u32[]{:S(2)}, u32[]{:S(2)}) collective-permute-start(bf16[128,1024]{1,0:T(8,128)(2,1)S(1)} %collective-permute-done.13.refs_0_), channel_id=1, source_target_pairs={{0,1},{1,0},{2,3},{3,2},{4,5},{5,4},{6,7},{7,6},{8,9},{9,8},{10,11... | collective-permute-start | bytes 786440 | tf_op jit(solution)/shard_map/ppermute | solution.py:235
where the time goes:
time: 53.3 us; the launch traced here: 53.2 us
  starting transfers between devices  18.8 us (35%)
  waiting for transfers between devices  16.1 us (30%)
  Pallas kernels  13.7 us (26%)
  local copies, waits for them, and re-layouts  3.84 us (7%)
  between operations  0.75 us (1%)
    ppermute x19, starting transfers between devices, swap(): return lax.ppermute(array, axis, [(i, i ^ mask) for i in range(size)])  18.8 us
    ppermute x19, waiting for transfers between devices, swap(): return lax.ppermute(array, axis, [(i, i ^ mask) for i in range(size)])  16.1 us
    pallas_call x1, Pallas kernels, mix(): pl.pallas_call(mix_kernel, in_specs=[pl.BlockSpec(memory_space=pltpu.SMEM...  4.74 us
    pallas_call x1, Pallas kernels, assemble(): pl.pallas_call(functools.partial(assemble_kernel, places), in_specs=[smem...  4.56 us
    pallas_call x1, Pallas kernels, contract(): pl.pallas_call(functools.partial(contract_kernel, places, n_cols), in_spe...  4.41 us
    unnamed x10, local copies, waits for them, and re-layouts  2.2 us
    slice x1, local copies, waits for them, and re-layouts, per_device(): own = jnp.concatenate([own[:, 0], own[:, 1]], axis=1)  1.6 us
  transfers between devices with their start and end apart: 19, of which 8 were waited for; matrix products, arithmetic and copies ran while one was open for 0% of the time, Pallas kernels for 17%

commit v1 on v0

--- a/solution.py
+++ b/solution.py
@@ -36,7 +36,7 @@
 
 def mix_kernel(op_ref, listed_ref, sink_ref, peramb_ref, *refs):
     outs, (left, held, sems) = refs[:-3], refs[-3:]
-    n_cols = len(outs)
+    n_cols = sum(out.shape[0] for out in outs)
     products, listed = listed_ref.shape
     eigen, local_cols = sink_ref.shape[-1], peramb_ref.shape[-1]
     loads = [
@@ -67,26 +67,31 @@
     for s in range(NS):
         loads[s].wait()
         mixed = dot(left[...], held[s].reshape(2 * eigen, local_cols)).astype(BF16)
-        for j in range(n_cols):
-            for k in range(products):
-                at = (j * products + k) * own2
-                outs[j][k, s] = mixed[at : at + own2]
-
-
-def mix(op_index, listed_rows, sink_ops, peramb, n_cols):
+        j = 0
+        for out in outs:
+            for n in range(out.shape[0]):
+                for k in range(products):
+                    at = (j * products + k) * own2
+                    out[n, k, s] = mixed[at : at + own2]
+                j += 1
+
+
+def mix(op_index, listed_rows, sink_ops, peramb, groups):
     products, listed = listed_rows.shape
     eigen = sink_ops.shape[-1]
     local_cols = peramb.shape[3]
-    own2 = 2 * listed // n_cols
-    block = jax.ShapeDtypeStruct((products, NS, own2, local_cols), BF16)
+    own2 = 2 * listed // sum(groups)
+    blocks = [
+        jax.ShapeDtypeStruct((group, products, NS, own2, local_cols), BF16) for group in groups
+    ]
     vmem = pl.BlockSpec(memory_space=pltpu.VMEM)
     return pl.pallas_call(
         mix_kernel,
         in_specs=[
             pl.BlockSpec(memory_space=pltpu.SMEM), vmem, vmem, pl.BlockSpec(memory_space=pltpu.HBM)
         ],
-        out_specs=[vmem] * n_cols,
-        out_shape=[block] * n_cols,
+        out_specs=[vmem] * len(groups),
+        out_shape=blocks,
         scratch_shapes=[
             pltpu.VMEM((products * 2 * listed, 2 * eigen), BF16),
             pltpu.VMEM((NS, 2, eigen, local_cols), BF16),
@@ -95,7 +100,7 @@
         compiler_params=pltpu.CompilerParams(vmem_limit_bytes=VMEM_LIMIT),
         cost_estimate=pl.CostEstimate(flops=1000, bytes_accessed=1000, transcendentals=0),
         name="mix",
-    )(op_index, listed_rows, sink_ops, peramb)
+    )(op_index, listed_rows, sink_ops, pltpu.with_memory_space_constraint(peramb, pltpu.HBM))
 
 
 def add_pieces(places, scalars_ref, slot_ref, pieces, products, eigen):
@@ -151,7 +156,7 @@
     n_pieces = len(places)
     pieces, blocks = refs[:n_pieces], refs[n_pieces : n_pieces + n_cols]
     out_ref, right, done, sems = refs[n_pieces + n_cols :]
-    own2, local_cols = blocks[0].shape[2], blocks[0].shape[3]
+    own2, local_cols = blocks[0].shape[3], blocks[0].shape[4]
     products, eigen = right.shape[0], right.shape[2]
     rows = NS * own2
     total = add_pieces(places, (source_ref, op_ref), slot_ref, pieces, products, eigen)
@@ -168,7 +173,7 @@
     for k in range(products):
         direct, turned = [], []
         for j in range(n_cols):
-            x = blocks[j][k].reshape(rows, local_cols)
+            x = blocks[j][0, k].reshape(rows, local_cols)
             wide = x.astype(F32)
             y = jnp.where(odd, pltpu.roll(wide, 1, 0), -pltpu.roll(wide, rows - 1, 0))
             direct.append(x)
@@ -206,7 +211,7 @@
 
 
 def contract(places, pieces, partial, source, op_index, slots, blocks):
-    products, _, own2, local_cols = blocks[0].shape
+    _, products, _, own2, local_cols = blocks[0].shape
     n_cols = len(blocks)
     eigen = partial.shape[2]
     order = n_cols * local_cols
@@ -255,7 +260,7 @@
         own = jnp.concatenate([op_table[:, 0], op_table[:, 1]], axis=1)
         whole = lax.all_gather(own, "tpair", axis=0, tiled=True)
         half = whole.shape[0] // 2
-        mixed = mix(op_index, listed_rows, sink_ops, peramb, n_cols)
+        mixed = mix(op_index, listed_rows, sink_ops, peramb, [1] * n_cols)
         blocks = [mixed[0]] + [swap(mixed[j], "col", n_cols, j) for j in range(1, n_cols)]
         partial = assemble([0], [whole[:half]], pair_source, op_index, slots, eigen)
         return contract(
@@ -267,10 +272,9 @@
     held = {(0, 0): own, (0, 1): beside(own)}
     for mask in (4, 2, 1):
         held[mask, 0] = across(own, mask)
-    mixed = mix(op_index, after(listed_rows, held[0, 1]), sink_ops, peramb, n_cols)
-    cross = swap(mixed[3], "col", n_cols, 2)
-    straight = swap(after(mixed[2], cross), "col", n_cols, 2)
-    blocks = [mixed[0], beside(mixed[1]), straight, beside(cross)]
+    mixed = mix(op_index, after(listed_rows, held[0, 1]), sink_ops, peramb, [1, 1, 2])
+    crossed = swap(mixed[2], "col", n_cols, 2)
+    blocks = [mixed[0], beside(mixed[1]), crossed, beside(crossed[1:])]
     held[3, 0] = across(after(held[2, 0], mixed[0], held[1, 0]), 1)
     held[6, 0] = across(after(own, mixed[0]), 6)
     held[5, 0] = across(after(held[4, 0], held[3, 0]), 1)

time: 53.3 us -> 56.5 us (1.060)
  waiting for transfers between devices: 16.1 us -> 26.3 us
  starting transfers between devices: 18.8 us -> 13.6 us
  local copies, waits for them, and re-layouts: 3.84 us -> 1.69 us
    ppermute x19 -> x18, waiting for transfers between devices: 16.1 us -> 26.3 us  [swap(): return lax.ppermute(array, axis, [(i, i ^ mask) for i in range(size)])]
    ppermute x19 -> x18, starting transfers between devices: 18.8 us -> 13.6 us  [swap(): return lax.ppermute(array, axis, [(i, i ^ mask) for i in range(size)])]
    unnamed x10 -> x8, local copies, waits for them, and re-layouts: 2.2 us -> 0.02 us
  transfers between devices with their start and end apart: 19 -> 18, of which waited for: 8 -> 5; matrix products, arithmetic and copies ran while one was open for 0% -> 0% of each run, Pallas kernels for 17% -> 17%
where the time goes in v1:
time: 56.5 us; the launch traced here: 56.4 us
  waiting for transfers between devices  26.3 us (47%)
  Pallas kernels  14 us (25%)
  starting transfers between devices  13.6 us (24%)
  local copies, waits for them, and re-layouts  1.69 us (3%)
  between operations  0.76 us (1%)
    ppermute x18, waiting for transfers between devices, swap(): return lax.ppermute(array, axis, [(i, i ^ mask) for i in range(size)])  26.3 us
    ppermute x18, starting transfers between devices, swap(): return lax.ppermute(array, axis, [(i, i ^ mask) for i in range(size)])  13.6 us
    pallas_call x1, Pallas kernels, mix(): pl.pallas_call(mix_kernel, in_specs=[pl.BlockSpec(memory_space=pltpu.SMEM...  4.99 us
    pallas_call x1, Pallas kernels, assemble(): pl.pallas_call(functools.partial(assemble_kernel, places), in_specs=[smem...  4.56 us
    pallas_call x1, Pallas kernels, contract(): pl.pallas_call(functools.partial(contract_kernel, places, n_cols), in_spe...  4.42 us
    slice x1, local copies, waits for them, and re-layouts, per_device(): own = jnp.concatenate([own[:, 0], own[:, 1]], axis=1)  1.6 us
  transfers between devices with their start and end apart: 18, of which 5 were waited for; matrix products, arithmetic and copies ran while one was open for 0% of the time, Pallas kernels for 17%

profile of v1, /device:TPU:0, one launch (start us, length us, event | category | flops | bytes accessed | tf_op | source)
XLA Modules:
  0.0 56.4 jit_solution(16998398174270090954)
XLA Ops:
  0.0 1.6 %constant_dynamic-slice_fusion = (bf16[128,1,512]{2,1,0:T(2,128)(2,1)S(1)}, bf16[128,1,512]{2,1,0:T(2,128)(2,1)S(1)}) fusion(bf16[256,2,512]{2,1,0:T(2,128)(2,1)} %param.9, s32[]{:T(128)S(6)} %select_n.11, s32[]{:T(128)S(6)} %add.9), kind=kLoop, calls=%fused_computation.3 | loop fusion | bytes 524296 | tf_op jit(solution)/shard_map/slice | solution.py:271
  1.7 0.0 copy-start.1
  1.7 0.5 collective-permute-start
  2.2 2.6 %collective-permute-start.3 = (bf16[128,1024]{1,0:T(8,128)(2,1)S(1)}, bf16[128,1024]{1,0:T(8,128)(2,1)S(1)}, u32[]{:S(2)}, u32[]{:S(2)}) collective-permute-start(bf16[128,1024]{1,0:T(8,128)(2,1)S(1)} %pad_maximum_fusion.refs_0_), channel_id=1, source_target_pairs={{0,8},{4,12},{8,0},{12,4},{16,24},{20,28},{24,16},{28,20},{1,9},{5... | collective-permute-start | bytes 786440 | tf_op jit(solution)/shard_map/ppermute | solution.py:240
  4.9 1.5 %collective-permute-start.1 = (bf16[128,1024]{1,0:T(8,128)(2,1)S(1)}, bf16[128,1024]{1,0:T(8,128)(2,1)S(1)}, u32[]{:S(2)}, u32[]{:S(2)}) collective-permute-start(bf16[128,1024]{1,0:T(8,128)(2,1)S(1)} %pad_maximum_fusion.refs_0_), channel_id=1, source_target_pairs={{0,4},{4,0},{8,12},{12,8},{16,20},{20,16},{24,28},{28,24},{1,5},{5... | collective-permute-start | bytes 786440 | tf_op jit(solution)/shard_map/ppermute | solution.py:240
  6.4 5.0 %mix.1 = (bf16[1,2,4,64,512]{4,3,2,1,0:T(8,128)(2,1)S(1)}, bf16[1,2,4,64,512]{4,3,2,1,0:T(8,128)(2,1)S(1)}, bf16[2,2,4,64,512]{4,3,2,1,0:T(8,128)(2,1)S(1)}) custom-call(s32[2,2]{1,0:T(2,128)S(1)} %copy-done.2, s32[2,128]{1,0:T(2,128)S(1)} %copy-done.3, bf16[1,2,2,512,512]{4,3,2,1,0:T(8,128)(2,1)S(1)} %copy-done, bf16[1,2,2048,512]{3,2,1,0:T(8,128)(2,1)} %peramb_ref.1), custom_call_target="tpu_custom_call" | custom-call | flops 1000 | bytes 1000 | tf_op jit(solution)/shard_map/mix/pallas_call | solution.py:88
  11.4 1.6 %collective-permute-start.16 = (bf16[2,2,4,64,512]{4,3,2,1,0:T(8,128)(2,1)S(1)}, bf16[2,2,4,64,512]{4,3,2,1,0:T(8,128)(2,1)S(1)}, u32[]{:S(2)}, u32[]{:S(2)}) collective-permute-start(bf16[2,2,4,64,512]{4,3,2,1,0:T(8,128)(2,1)S(1)} %get-tuple-element.22), channel_id=1, source_target_pairs={{0,2},{1,3},{2,0},{3,1},{4,6},{5,7},{6,4},{7,5},{8,10},{9,11},{10,... | collective-permute-start | bytes 3145736 | tf_op jit(solution)/shard_map/ppermute | solution.py:240
  13.0 2.6 %collective-permute-start.7 = (bf16[128,1024]{1,0:T(8,128)(2,1)S(1)}, bf16[128,1024]{1,0:T(8,128)(2,1)S(1)}, u32[]{:S(2)}, u32[]{:S(2)}) collective-permute-start(bf16[128,1024]{1,0:T(8,128)(2,1)S(1)} %pad_maximum_fusion.refs_0_), channel_id=1, source_target_pairs={{0,16},{4,20},{8,24},{12,28},{16,0},{20,4},{24,8},{28,12},{1,17},{... | collective-permute-start | bytes 786440 | tf_op jit(solution)/shard_map/ppermute | solution.py:240
  15.6 0.0 collective-permute-done.3.refs_4_
  15.6 0.0 collective-permute-done.1.refs_2_
  15.6 0.5 collective-permute-start.5
  16.1 1.1 %collective-permute-start.11 = (bf16[128,1024]{1,0:T(8,128)(2,1)S(1)}, bf16[128,1024]{1,0:T(8,128)(2,1)S(1)}, u32[]{:S(2)}, u32[]{:S(2)}) collective-permute-start(bf16[128,1024]{1,0:T(8,128)(2,1)S(1)} %pad_maximum_fusion.refs_0_), channel_id=1, source_target_pairs={{0,24},{4,28},{8,16},{12,20},{16,8},{20,12},{24,0},{28,4},{1,25},{... | collective-permute-start | bytes 786440 | tf_op jit(solution)/shard_map/ppermute | solution.py:240
  17.2 15.7 %collective-permute-done.7.refs_8_ = bf16[128,1024]{1,0:T(8,128)(2,1)S(1)} collective-permute-done((bf16[128,1024]{1,0:T(8,128)(2,1)S(1)}, bf16[128,1024]{1,0:T(8,128)(2,1)S(1)}, u32[]{:S(2)}, u32[]{:S(2)}) %collective-permute-start.7) | collective-permute-done | bytes 262176 | tf_op jit(solution)/shard_map/ppermute | solution.py:240
  32.9 1.3 %collective-permute-start.9 = (bf16[128,1024]{1,0:T(8,128)(2,1)S(1)}, bf16[128,1024]{1,0:T(8,128)(2,1)S(1)}, u32[]{:S(2)}, u32[]{:S(2)}) collective-permute-start(bf16[128,1024]{1,0:T(8,128)(2,1)S(1)} %collective-permute-done.7.refs_8_), channel_id=1, source_target_pairs={{0,4},{4,0},{8,12},{12,8},{16,20},{20,16},{24,28},{28,24},{1,5},{5... | collective-permute-start | bytes 786440 | tf_op jit(solution)/shard_map/ppermute | solution.py:240
  34.2 0.5 collective-permute-start.8
  34.7 0.0 collective-permute-start.4
  34.7 6.3 %collective-permute-done.9.refs_10_ = bf16[128,1024]{1,0:T(8,128)(2,1)S(1)} collective-permute-done((bf16[128,1024]{1,0:T(8,128)(2,1)S(1)}, bf16[128,1024]{1,0:T(8,128)(2,1)S(1)}, u32[]{:S(2)}, u32[]{:S(2)}) %collective-permute-start.9) | collective-permute-done | bytes 262176 | tf_op jit(solution)/shard_map/ppermute | solution.py:240
  41.1 0.0 collective-permute-start.2
  41.1 0.0 collective-permute-done.12.refs_13_
  41.1 0.5 collective-permute-start.6
  41.6 0.0 collective-permute-done.16.refs_4_
  41.6 0.1 collective-permute-start.10
  41.7 0.0 collective-permute-done.8.refs_9_
  41.7 0.3 collective-permute-start.13
  42.0 0.2 collective-permute-start.15
  42.3 0.3 collective-permute-done.2.refs_3_
  42.6 0.1 collective-permute-start.17
  43.4 0.0 collective-permute-done.6.refs_7_
  43.4 4.6 %assemble.1.partial_ref = bf16[2,1024,512]{2,1,0:T(8,128)(2,1)S(1)} custom-call(s32[1]{0:T(128)S(6)} %copy.14.source_ref, s32[2,2]{1,0:T(2,128)S(1)} %copy-done.2, s32[16,128]{1,0:T(8,128)S(1)} %bitcast.5, bf16[128,1024]{1,0:T(8,128)(2,1)S(1)} %pad_maximum_fusion.refs_0_, bf16[128,1024]{1,0:T(8,128)(2,1)S(1)} %collective-permute-done.refs_1_, ...), custom_call_target="tpu_custom_call" | custom-call | flops 1000 | bytes 1000 | tf_op jit(solution)/shard_map/assemble/pallas_call | solution.py:144
  48.0 2.4 %collective-permute-done.13.refs_0_ = bf16[128,1024]{1,0:T(8,128)(2,1)S(1)} collective-permute-done((bf16[128,1024]{1,0:T(8,128)(2,1)S(1)}, bf16[128,1024]{1,0:T(8,128)(2,1)S(1)}, u32[]{:S(2)}, u32[]{:S(2)}) %collective-permute-start.13) | collective-permute-done | bytes 262176 | tf_op jit(solution)/shard_map/ppermute | solution.py:240
  50.4 1.5 %collective-permute-done.14.refs_1_ = bf16[128,1024]{1,0:T(8,128)(2,1)S(1)} collective-permute-done((bf16[128,1024]{1,0:T(8,128)(2,1)S(1)}, bf16[128,1024]{1,0:T(8,128)(2,1)S(1)}, u32[]{:S(2)}, u32[]{:S(2)}) %collective-permute-start.14) | collective-permute-done | bytes 262176 | tf_op jit(solution)/shard_map/ppermute | solution.py:240
  52.0 4.4 %contract.1 = bf16[2,4,32,2,2048]{4,3,2,1,0:T(2,128)(2,1)} custom-call(s32[1]{0:T(128)S(6)} %copy.14.source_ref, s32[2,2]{1,0:T(2,128)S(1)} %copy-done.2, s32[16,128]{1,0:T(8,128)S(1)} %bitcast.6, bf16[2,1024,512]{2,1,0:T(8,128)(2,1)S(1)} %assemble.1.partial_ref, bf16[128,1024]{1,0:T(8,128)(2,1)S(1)} %collective-permute-done.13.refs_0_, ...), custom_call_target="tpu_custom_call" | custom-call | flops 2147483648 | tf_op jit(solution)/shard_map/contract/pallas_call | solution.py:221
  (19 shorter events, 0.1 us)
Async XLA Ops:
  0.0 6.4 %copy-start.3 = (s32[2,128]{1,0:T(2,128)S(1)}, s32[2,128]{1,0:T(2,128)}, u32[]{:S(2)}) copy-start(s32[2,128]{1,0:T(2,128)} %listed_ref) | copy-start | bytes 3076
  0.0 6.4 %copy-start.2 = (s32[2,2]{1,0:T(2,128)S(1)}, s32[2,2]{1,0:T(2,128)}, u32[]{:S(2)}) copy-start(s32[2,2]{1,0:T(2,128)} %op_ref.5) | copy-start | bytes 52
  0.0 6.4 %copy-start = (bf16[1,2,2,512,512]{4,3,2,1,0:T(8,128)(2,1)S(1)}, bf16[1,2,2,512,512]{4,3,2,1,0:T(8,128)(2,1)}, u32[]{:S(2)}) copy-start(bf16[1,2,2,512,512]{4,3,2,1,0:T(8,128)(2,1)} %sink_ref.1) | copy-start | bytes 6291460
  1.7 41.7 %copy-start.1 = (s32[2048]{0:T(1024)S(1)}, s32[2048]{0:T(1024)}, u32[]{:S(2)}) copy-start(s32[2048]{0:T(1024)} %param.10) | copy-start | bytes 24580
  1.7 4.7 %collective-permute-start = (bf16[128,1024]{1,0:T(8,128)(2,1)S(1)}, bf16[128,1024]{1,0:T(8,128)(2,1)S(1)}, u32[]{:S(2)}, u32[]{:S(2)}) collective-permute-start(bf16[128,1024]{1,0:T(8,128)(2,1)S(1)} %pad_maximum_fusion.refs_0_), channel_id=1, source_target_pairs={{0,1},{1,0},{2,3},{3,2},{4,5},{5,4},{6,7},{7,6},{8,9},{9,8},{10,11... | collective-permute-start | bytes 786440 | tf_op jit(solution)/shard_map/ppermute | solution.py:240
  2.2 13.3 %collective-permute-start.3 = (bf16[128,1024]{1,0:T(8,128)(2,1)S(1)}, bf16[128,1024]{1,0:T(8,128)(2,1)S(1)}, u32[]{:S(2)}, u32[]{:S(2)}) collective-permute-start(bf16[128,1024]{1,0:T(8,128)(2,1)S(1)} %pad_maximum_fusion.refs_0_), channel_id=1, source_target_pairs={{0,8},{4,12},{8,0},{12,4},{16,24},{20,28},{24,16},{28,20},{1,9},{5... | collective-permute-start | bytes 786440 | tf_op jit(solution)/shard_map/ppermute | solution.py:240
  4.9 10.7 %collective-permute-start.1 = (bf16[128,1024]{1,0:T(8,128)(2,1)S(1)}, bf16[128,1024]{1,0:T(8,128)(2,1)S(1)}, u32[]{:S(2)}, u32[]{:S(2)}) collective-permute-start(bf16[128,1024]{1,0:T(8,128)(2,1)S(1)} %pad_maximum_fusion.refs_0_), channel_id=1, source_target_pairs={{0,4},{4,0},{8,12},{12,8},{16,20},{20,16},{24,28},{28,24},{1,5},{5... | collective-permute-start | bytes 786440 | tf_op jit(solution)/shard_map/ppermute | solution.py:240
  11.4 30.2 %collective-permute-start.16 = (bf16[2,2,4,64,512]{4,3,2,1,0:T(8,128)(2,1)S(1)}, bf16[2,2,4,64,512]{4,3,2,1,0:T(8,128)(2,1)S(1)}, u32[]{:S(2)}, u32[]{:S(2)}) collective-permute-start(bf16[2,2,4,64,512]{4,3,2,1,0:T(8,128)(2,1)S(1)} %get-tuple-element.22), channel_id=1, source_target_pairs={{0,2},{1,3},{2,0},{3,1},{4,6},{5,7},{6,4},{7,5},{8,10},{9,11},{10,... | collective-permute-start | bytes 3145736 | tf_op jit(solution)/shard_map/ppermute | solution.py:240
  13.0 19.9 %collective-permute-start.7 = (bf16[128,1024]{1,0:T(8,128)(2,1)S(1)}, bf16[128,1024]{1,0:T(8,128)(2,1)S(1)}, u32[]{:S(2)}, u32[]{:S(2)}) collective-permute-start(bf16[128,1024]{1,0:T(8,128)(2,1)S(1)} %pad_maximum_fusion.refs_0_), channel_id=1, source_target_pairs={{0,16},{4,20},{8,24},{12,28},{16,0},{20,4},{24,8},{28,12},{1,17},{... | collective-permute-start | bytes 786440 | tf_op jit(solution)/shard_map/ppermute | solution.py:240
  15.6 17.3 %collective-permute-start.5 = (bf16[128,1024]{1,0:T(8,128)(2,1)S(1)}, bf16[128,1024]{1,0:T(8,128)(2,1)S(1)}, u32[]{:S(2)}, u32[]{:S(2)}) collective-permute-start(bf16[128,1024]{1,0:T(8,128)(2,1)S(1)} %collective-permute-done.3.refs_4_), channel_id=1, source_target_pairs={{0,4},{4,0},{8,12},{12,8},{16,20},{20,16},{24,28},{28,24},{1,5},{5... | collective-permute-start | bytes 786440 | tf_op jit(solution)/shard_map/ppermute | solution.py:240
  16.1 18.1 %collective-permute-start.11 = (bf16[128,1024]{1,0:T(8,128)(2,1)S(1)}, bf16[128,1024]{1,0:T(8,128)(2,1)S(1)}, u32[]{:S(2)}, u32[]{:S(2)}) collective-permute-start(bf16[128,1024]{1,0:T(8,128)(2,1)S(1)} %pad_maximum_fusion.refs_0_), channel_id=1, source_target_pairs={{0,24},{4,28},{8,16},{12,20},{16,8},{20,12},{24,0},{28,4},{1,25},{... | collective-permute-start | bytes 786440 | tf_op jit(solution)/shard_map/ppermute | solution.py:240
  32.9 8.1 %collective-permute-start.9 = (bf16[128,1024]{1,0:T(8,128)(2,1)S(1)}, bf16[128,1024]{1,0:T(8,128)(2,1)S(1)}, u32[]{:S(2)}, u32[]{:S(2)}) collective-permute-start(bf16[128,1024]{1,0:T(8,128)(2,1)S(1)} %collective-permute-done.7.refs_8_), channel_id=1, source_target_pairs={{0,4},{4,0},{8,12},{12,8},{16,20},{20,16},{24,28},{28,24},{1,5},{5... | collective-permute-start | bytes 786440 | tf_op jit(solution)/shard_map/ppermute | solution.py:240
  34.2 6.8 %collective-permute-start.12 = (bf16[128,1024]{1,0:T(8,128)(2,1)S(1)}, bf16[128,1024]{1,0:T(8,128)(2,1)S(1)}, u32[]{:S(2)}, u32[]{:S(2)}) collective-permute-start(bf16[128,1024]{1,0:T(8,128)(2,1)S(1)} %collective-permute-done.11.refs_12_), channel_id=1, source_target_pairs={{0,1},{1,0},{2,3},{3,2},{4,5},{5,4},{6,7},{7,6},{8,9},{9,8},{10,11... | collective-permute-start | bytes 786440 | tf_op jit(solution)/shard_map/ppermute | solution.py:240
  34.2 7.5 %collective-permute-start.8 = (bf16[128,1024]{1,0:T(8,128)(2,1)S(1)}, bf16[128,1024]{1,0:T(8,128)(2,1)S(1)}, u32[]{:S(2)}, u32[]{:S(2)}) collective-permute-start(bf16[128,1024]{1,0:T(8,128)(2,1)S(1)} %collective-permute-done.7.refs_8_), channel_id=1, source_target_pairs={{0,1},{1,0},{2,3},{3,2},{4,5},{5,4},{6,7},{7,6},{8,9},{9,8},{10,11... | collective-permute-start | bytes 786440 | tf_op jit(solution)/shard_map/ppermute | solution.py:240
  34.7 7.3 %collective-permute-start.4 = (bf16[128,1024]{1,0:T(8,128)(2,1)S(1)}, bf16[128,1024]{1,0:T(8,128)(2,1)S(1)}, u32[]{:S(2)}, u32[]{:S(2)}) collective-permute-start(bf16[128,1024]{1,0:T(8,128)(2,1)S(1)} %collective-permute-done.3.refs_4_), channel_id=1, source_target_pairs={{0,1},{1,0},{2,3},{3,2},{4,5},{5,4},{6,7},{7,6},{8,9},{9,8},{10,11... | collective-permute-start | bytes 786440 | tf_op jit(solution)/shard_map/ppermute | solution.py:240
  41.1 1.5 %collective-permute-start.2 = (bf16[128,1024]{1,0:T(8,128)(2,1)S(1)}, bf16[128,1024]{1,0:T(8,128)(2,1)S(1)}, u32[]{:S(2)}, u32[]{:S(2)}) collective-permute-start(bf16[128,1024]{1,0:T(8,128)(2,1)S(1)} %collective-permute-done.1.refs_2_), channel_id=1, source_target_pairs={{0,1},{1,0},{2,3},{3,2},{4,5},{5,4},{6,7},{7,6},{8,9},{9,8},{10,11... | collective-permute-start | bytes 786440 | tf_op jit(solution)/shard_map/ppermute | solution.py:240
  41.1 2.3 %collective-permute-start.6 = (bf16[128,1024]{1,0:T(8,128)(2,1)S(1)}, bf16[128,1024]{1,0:T(8,128)(2,1)S(1)}, u32[]{:S(2)}, u32[]{:S(2)}) collective-permute-start(bf16[128,1024]{1,0:T(8,128)(2,1)S(1)} %collective-permute-done.5.refs_6_), channel_id=1, source_target_pairs={{0,1},{1,0},{2,3},{3,2},{4,5},{5,4},{6,7},{7,6},{8,9},{9,8},{10,11... | collective-permute-start | bytes 786440 | tf_op jit(solution)/shard_map/ppermute | solution.py:240
  41.6 1.8 %collective-permute-start.10 = (bf16[128,1024]{1,0:T(8,128)(2,1)S(1)}, bf16[128,1024]{1,0:T(8,128)(2,1)S(1)}, u32[]{:S(2)}, u32[]{:S(2)}) collective-permute-start(bf16[128,1024]{1,0:T(8,128)(2,1)S(1)} %collective-permute-done.9.refs_10_), channel_id=1, source_target_pairs={{0,1},{1,0},{2,3},{3,2},{4,5},{5,4},{6,7},{7,6},{8,9},{9,8},{10,11... | collective-permute-start | bytes 786440 | tf_op jit(solution)/shard_map/ppermute | solution.py:240
  41.7 8.7 %collective-permute-start.13 = (bf16[128,1024]{1,0:T(8,128)(2,1)S(1)}, bf16[128,1024]{1,0:T(8,128)(2,1)S(1)}, u32[]{:S(2)}, u32[]{:S(2)}) collective-permute-start(bf16[128,1024]{1,0:T(8,128)(2,1)S(1)} %collective-permute-done.11.refs_12_), channel_id=1, source_target_pairs={{0,4},{4,0},{8,12},{12,8},{16,20},{20,16},{24,28},{28,24},{1,5},{5... | collective-permute-start | bytes 786440 | tf_op jit(solution)/shard_map/ppermute | solution.py:240
  42.0 8.4 %collective-permute-start.15 = (bf16[1,2,4,64,512]{4,3,2,1,0:T(8,128)(2,1)S(1)}, bf16[1,2,4,64,512]{4,3,2,1,0:T(8,128)(2,1)S(1)}, u32[]{:S(2)}, u32[]{:S(2)}) collective-permute-start(bf16[1,2,4,64,512]{4,3,2,1,0:T(8,128)(2,1)S(1)} %get-tuple-element.21), channel_id=1, source_target_pairs={{0,1},{1,0},{2,3},{3,2},{4,5},{5,4},{6,7},{7,6},{8,9},{9,8},{10,11... | collective-permute-start | bytes 1572872 | tf_op jit(solution)/shard_map/ppermute | solution.py:240
  42.6 9.4 %collective-permute-start.17 = (bf16[1,2,4,64,512]{4,3,2,1,0:T(8,128)(2,1)S(1)}, bf16[1,2,4,64,512]{4,3,2,1,0:T(8,128)(2,1)S(1)}, u32[]{:S(2)}, u32[]{:S(2)}) collective-permute-start(bf16[1,2,4,64,512]{4,3,2,1,0:T(8,128)(2,1)S(1)} %slice.12), channel_id=1, source_target_pairs={{0,1},{1,0},{2,3},{3,2},{4,5},{5,4},{6,7},{7,6},{8,9},{9,8},{10,11... | collective-permute-start | bytes 1572872 | tf_op jit(solution)/shard_map/ppermute | solution.py:240
  50.4 1.5 %collective-permute-start.14 = (bf16[128,1024]{1,0:T(8,128)(2,1)S(1)}, bf16[128,1024]{1,0:T(8,128)(2,1)S(1)}, u32[]{:S(2)}, u32[]{:S(2)}) collective-permute-start(bf16[128,1024]{1,0:T(8,128)(2,1)S(1)} %collective-permute-done.13.refs_0_), channel_id=1, source_target_pairs={{0,1},{1,0},{2,3},{3,2},{4,5},{5,4},{6,7},{7,6},{8,9},{9,8},{10,11... | collective-permute-start | bytes 786440 | tf_op jit(solution)/shard_map/ppermute | solution.py:240

commit v2 on v1

--- a/solution.py
+++ b/solution.py
@@ -269,18 +269,20 @@
     half = rows // 2
     own = lax.dynamic_slice_in_dim(op_table, lax.axis_index("col") % 2 * half, half, 0)
     own = jnp.concatenate([own[:, 0], own[:, 1]], axis=1)
-    held = {(0, 0): own, (0, 1): beside(own)}
+    held = {(0, 0): own}
     for mask in (4, 2, 1):
         held[mask, 0] = across(own, mask)
-    mixed = mix(op_index, after(listed_rows, held[0, 1]), sink_ops, peramb, [1, 1, 2])
-    crossed = swap(mixed[2], "col", n_cols, 2)
-    blocks = [mixed[0], beside(mixed[1]), crossed, beside(crossed[1:])]
-    held[3, 0] = across(after(held[2, 0], mixed[0], held[1, 0]), 1)
+    mixed = mix(op_index, listed_rows, sink_ops, peramb, [1] * n_cols)
+    for mask in (0, 1, 2, 4):
+        held[mask, 1] = beside(after(held[mask, 0], mixed[0]))
+    cross = swap(mixed[3], "col", n_cols, 2)
+    straight = swap(after(mixed[2], cross), "col", n_cols, 2)
+    blocks = [mixed[0], beside(mixed[1]), straight, beside(cross)]
+    held[3, 0] = across(after(held[2, 0], mixed[0], held[2, 1], held[1, 1]), 1)
     held[6, 0] = across(after(own, mixed[0]), 6)
-    held[5, 0] = across(after(held[4, 0], held[3, 0]), 1)
-    held[6, 1] = beside(held[6, 0])
-    held[7, 0] = across(after(held[6, 0], held[6, 1], held[5, 0]), 1)
-    for mask in (1, 2, 3, 4, 5):
+    held[5, 0] = across(after(held[4, 0], mixed[0], held[4, 1]), 1)
+    held[7, 0] = across(after(held[6, 0], held[5, 0]), 1)
+    for mask in (3, 5, 6):
         held[mask, 1] = beside(held[mask, 0])
     early = [(mask, side) for mask in range(7) for side in (0, 1)]
     partial = assemble(early, [held[p] for p in early], pair_source, op_index, slots, eigen)

time: 56.5 us -> 56.1 us (level)
  waiting for transfers between devices: 26.3 us -> 24 us
  starting transfers between devices: 13.6 us -> 15.5 us
    ppermute x18 -> x19, waiting for transfers between devices: 26.3 us -> 24 us  [swap(): return lax.ppermute(array, axis, [(i, i ^ mask) for i in range(size)])]
    ppermute x18 -> x19, starting transfers between devices: 13.6 us -> 15.5 us  [swap(): return lax.ppermute(array, axis, [(i, i ^ mask) for i in range(size)])]
  transfers between devices with their start and end apart: 18 -> 19, of which waited for: 5 -> 8; matrix products, arithmetic and copies ran while one was open for 0% -> 0% of each run, Pallas kernels for 17% -> 17%
where the time goes in v2:
time: 56.1 us; the launch traced here: 55.9 us
  waiting for transfers between devices  24 us (43%)
  starting transfers between devices  15.5 us (28%)
  Pallas kernels  14 us (25%)
  local copies, waits for them, and re-layouts  1.66 us (3%)
  between operations  0.75 us (1%)
    ppermute x19, waiting for transfers between devices, swap(): return lax.ppermute(array, axis, [(i, i ^ mask) for i in range(size)])  24 us
    ppermute x19, starting transfers between devices, swap(): return lax.ppermute(array, axis, [(i, i ^ mask) for i in range(size)])  15.5 us
    pallas_call x1, Pallas kernels, mix(): pl.pallas_call(mix_kernel, in_specs=[pl.BlockSpec(memory_space=pltpu.SMEM...  4.99 us
    pallas_call x1, Pallas kernels, assemble(): pl.pallas_call(functools.partial(assemble_kernel, places), in_specs=[smem...  4.56 us
    pallas_call x1, Pallas kernels, contract(): pl.pallas_call(functools.partial(contract_kernel, places, n_cols), in_spe...  4.43 us
    slice x1, local copies, waits for them, and re-layouts, per_device(): own = jnp.concatenate([own[:, 0], own[:, 1]], axis=1)  1.6 us
  transfers between devices with their start and end apart: 19, of which 8 were waited for; matrix products, arithmetic and copies ran while one was open for 0% of the time, Pallas kernels for 17%

profile of v2, /device:TPU:0, one launch (start us, length us, event | category | flops | bytes accessed | tf_op | source)
XLA Modules:
  0.0 55.9 jit_solution(7928351349560235791)
XLA Ops:
  0.0 1.6 %constant_dynamic-slice_fusion = (bf16[128,1,512]{2,1,0:T(2,128)(2,1)S(1)}, bf16[128,1,512]{2,1,0:T(2,128)(2,1)S(1)}) fusion(bf16[256,2,512]{2,1,0:T(2,128)(2,1)} %param.9, s32[]{:T(128)S(6)} %select_n.11, s32[]{:T(128)S(6)} %add.9), kind=kLoop, calls=%fused_computation.3 | loop fusion | bytes 524296 | tf_op jit(solution)/shard_map/slice | solution.py:271
  1.7 0.0 copy-start.1
  1.7 3.0 %collective-permute-start.1 = (bf16[128,1024]{1,0:T(8,128)(2,1)S(1)}, bf16[128,1024]{1,0:T(8,128)(2,1)S(1)}, u32[]{:S(2)}, u32[]{:S(2)}) collective-permute-start(bf16[128,1024]{1,0:T(8,128)(2,1)S(1)} %pad_maximum_fusion.refs_0_), channel_id=1, source_target_pairs={{0,4},{4,0},{8,12},{12,8},{16,20},{20,16},{24,28},{28,24},{1,5},{5... | collective-permute-start | bytes 786440 | tf_op jit(solution)/shard_map/ppermute | solution.py:240
  4.7 1.6 %collective-permute-start.3 = (bf16[128,1024]{1,0:T(8,128)(2,1)S(1)}, bf16[128,1024]{1,0:T(8,128)(2,1)S(1)}, u32[]{:S(2)}, u32[]{:S(2)}) collective-permute-start(bf16[128,1024]{1,0:T(8,128)(2,1)S(1)} %pad_maximum_fusion.refs_0_), channel_id=1, source_target_pairs={{0,8},{4,12},{8,0},{12,4},{16,24},{20,28},{24,16},{28,20},{1,9},{5... | collective-permute-start | bytes 786440 | tf_op jit(solution)/shard_map/ppermute | solution.py:240
  6.3 2.6 %collective-permute-start.7 = (bf16[128,1024]{1,0:T(8,128)(2,1)S(1)}, bf16[128,1024]{1,0:T(8,128)(2,1)S(1)}, u32[]{:S(2)}, u32[]{:S(2)}) collective-permute-start(bf16[128,1024]{1,0:T(8,128)(2,1)S(1)} %pad_maximum_fusion.refs_0_), channel_id=1, source_target_pairs={{0,16},{4,20},{8,24},{12,28},{16,0},{20,4},{24,8},{28,12},{1,17},{... | collective-permute-start | bytes 786440 | tf_op jit(solution)/shard_map/ppermute | solution.py:240
  8.9 5.0 %mix.1 = (bf16[1,2,4,64,512]{4,3,2,1,0:T(8,128)(2,1)S(1)}, bf16[1,2,4,64,512]{4,3,2,1,0:T(8,128)(2,1)S(1)}, bf16[1,2,4,64,512]{4,3,2,1,0:T(8,128)(2,1)S(1)}, bf16[1,2,4,64,512]{4,3,2,1,0:T(8,128)(2,1)S(1)}) custom-call(s32[2,2]{1,0:T(2,128)S(1)} %copy-done.2, s32[2,128]{1,0:T(2,128)S(1)} %copy-done.3, bf16[1,2,2,512,512]{4,3,2,1,0:T(8,128)(2,1)S(1)} %copy-done, ...), custom_call_target="tpu_custom_call" | custom-call | flops 1000 | bytes 1000 | tf_op jit(solution)/shard_map/mix/pallas_call | solution.py:88
  13.9 0.0 collective-permute-done.1.refs_2_
  13.9 0.1 collective-permute-start.2
  14.0 4.0 %collective-permute-done.3.refs_4_ = bf16[128,1024]{1,0:T(8,128)(2,1)S(1)} collective-permute-done((bf16[128,1024]{1,0:T(8,128)(2,1)S(1)}, bf16[128,1024]{1,0:T(8,128)(2,1)S(1)}, u32[]{:S(2)}, u32[]{:S(2)}) %collective-permute-start.3) | collective-permute-done | bytes 262176 | tf_op jit(solution)/shard_map/ppermute | solution.py:240
  18.0 1.5 %collective-permute-start.16 = (bf16[1,2,4,64,512]{4,3,2,1,0:T(8,128)(2,1)S(1)}, bf16[1,2,4,64,512]{4,3,2,1,0:T(8,128)(2,1)S(1)}, u32[]{:S(2)}, u32[]{:S(2)}) collective-permute-start(bf16[1,2,4,64,512]{4,3,2,1,0:T(8,128)(2,1)S(1)} %get-tuple-element.29), channel_id=1, source_target_pairs={{0,2},{1,3},{2,0},{3,1},{4,6},{5,7},{6,4},{7,5},{8,10},{9,11},{10,... | collective-permute-start | bytes 1572872 | tf_op jit(solution)/shard_map/ppermute | solution.py:240
  19.5 0.8 %collective-permute-done.7.refs_8_ = bf16[128,1024]{1,0:T(8,128)(2,1)S(1)} collective-permute-done((bf16[128,1024]{1,0:T(8,128)(2,1)S(1)}, bf16[128,1024]{1,0:T(8,128)(2,1)S(1)}, u32[]{:S(2)}, u32[]{:S(2)}) %collective-permute-start.7) | collective-permute-done | bytes 262176 | tf_op jit(solution)/shard_map/ppermute | solution.py:240
  20.4 2.5 %collective-permute-start.11 = (bf16[128,1024]{1,0:T(8,128)(2,1)S(1)}, bf16[128,1024]{1,0:T(8,128)(2,1)S(1)}, u32[]{:S(2)}, u32[]{:S(2)}) collective-permute-start(bf16[128,1024]{1,0:T(8,128)(2,1)S(1)} %pad_maximum_fusion.refs_0_), channel_id=1, source_target_pairs={{0,24},{4,28},{8,16},{12,20},{16,8},{20,12},{24,0},{28,4},{1,25},{... | collective-permute-start | bytes 786440 | tf_op jit(solution)/shard_map/ppermute | solution.py:240
  22.8 0.0 collective-permute-done.2.refs_3_
  22.8 0.0 collective-permute-done.4.refs_5_
  22.8 0.5 collective-permute-start.5
  23.4 0.0 collective-permute-done.8.refs_9_
  23.4 1.5 %collective-permute-start.9 = (bf16[128,1024]{1,0:T(8,128)(2,1)S(1)}, bf16[128,1024]{1,0:T(8,128)(2,1)S(1)}, u32[]{:S(2)}, u32[]{:S(2)}) collective-permute-start(bf16[128,1024]{1,0:T(8,128)(2,1)S(1)} %collective-permute-done.7.refs_8_), channel_id=1, source_target_pairs={{0,4},{4,0},{8,12},{12,8},{16,20},{20,16},{24,28},{28,24},{1,5},{5... | collective-permute-start | bytes 786440 | tf_op jit(solution)/shard_map/ppermute | solution.py:240
  24.9 0.0 collective-permute-start
  24.9 6.1 %collective-permute-done.11.refs_12_ = bf16[128,1024]{1,0:T(8,128)(2,1)S(1)} collective-permute-done((bf16[128,1024]{1,0:T(8,128)(2,1)S(1)}, bf16[128,1024]{1,0:T(8,128)(2,1)S(1)}, u32[]{:S(2)}, u32[]{:S(2)}) %collective-permute-start.11) | collective-permute-done | bytes 262176 | tf_op jit(solution)/shard_map/ppermute | solution.py:240
  31.0 0.0 collective-permute-start.12
  31.0 1.0 %collective-permute-done.5.refs_6_ = bf16[128,1024]{1,0:T(8,128)(2,1)S(1)} collective-permute-done((bf16[128,1024]{1,0:T(8,128)(2,1)S(1)}, bf16[128,1024]{1,0:T(8,128)(2,1)S(1)}, u32[]{:S(2)}, u32[]{:S(2)}) %collective-permute-start.5) | collective-permute-done | bytes 262176 | tf_op jit(solution)/shard_map/ppermute | solution.py:240
  32.0 0.0 collective-permute-start.6
  32.0 0.4 collective-permute-done.16
  32.3 0.2 collective-permute-start.15
  32.5 4.4 %collective-permute-done.9.refs_10_ = bf16[128,1024]{1,0:T(8,128)(2,1)S(1)} collective-permute-done((bf16[128,1024]{1,0:T(8,128)(2,1)S(1)}, bf16[128,1024]{1,0:T(8,128)(2,1)S(1)}, u32[]{:S(2)}, u32[]{:S(2)}) %collective-permute-start.9) | collective-permute-done | bytes 262176 | tf_op jit(solution)/shard_map/ppermute | solution.py:240
  36.9 0.5 collective-permute-start.13
  37.4 1.5 %collective-permute-start.17 = (bf16[1,2,4,64,512]{4,3,2,1,0:T(8,128)(2,1)S(1)}, bf16[1,2,4,64,512]{4,3,2,1,0:T(8,128)(2,1)S(1)}, u32[]{:S(2)}, u32[]{:S(2)}) collective-permute-start(bf16[1,2,4,64,512]{4,3,2,1,0:T(8,128)(2,1)S(1)} %get-tuple-element.30), channel_id=1, source_target_pairs={{0,2},{1,3},{2,0},{3,1},{4,6},{5,7},{6,4},{7,5},{8,10},{9,11},{10,... | collective-permute-start | bytes 1572872 | tf_op jit(solution)/shard_map/ppermute | solution.py:240
  39.6 0.0 collective-permute-done.10.refs_11_
  39.6 4.6 %assemble.1.partial_ref = bf16[2,1024,512]{2,1,0:T(8,128)(2,1)S(1)} custom-call(s32[1]{0:T(128)S(6)} %copy.14.source_ref, s32[2,2]{1,0:T(2,128)S(1)} %copy-done.2, s32[16,128]{1,0:T(8,128)S(1)} %bitcast.5, bf16[128,1024]{1,0:T(8,128)(2,1)S(1)} %pad_maximum_fusion.refs_0_, bf16[128,1024]{1,0:T(8,128)(2,1)S(1)} %collective-permute-done.refs_1_, ...), custom_call_target="tpu_custom_call" | custom-call | flops 1000 | bytes 1000 | tf_op jit(solution)/shard_map/assemble/pallas_call | solution.py:144
  44.2 1.4 %collective-permute-done.13.refs_0_ = bf16[128,1024]{1,0:T(8,128)(2,1)S(1)} collective-permute-done((bf16[128,1024]{1,0:T(8,128)(2,1)S(1)}, bf16[128,1024]{1,0:T(8,128)(2,1)S(1)}, u32[]{:S(2)}, u32[]{:S(2)}) %collective-permute-start.13) | collective-permute-done | bytes 262176 | tf_op jit(solution)/shard_map/ppermute | solution.py:240
  45.6 5.9 %collective-permute-done.17.refs_4_ = bf16[1,2,4,64,512]{4,3,2,1,0:T(8,128)(2,1)S(1)} collective-permute-done((bf16[1,2,4,64,512]{4,3,2,1,0:T(8,128)(2,1)S(1)}, bf16[1,2,4,64,512]{4,3,2,1,0:T(8,128)(2,1)S(1)}, u32[]{:S(2)}, u32[]{:S(2)}) %collective-permute-start.17) | collective-permute-done | bytes 524320 | tf_op jit(solution)/shard_map/ppermute | solution.py:240
  51.5 4.4 %contract.1 = bf16[2,4,32,2,2048]{4,3,2,1,0:T(2,128)(2,1)} custom-call(s32[1]{0:T(128)S(6)} %copy.14.source_ref, s32[2,2]{1,0:T(2,128)S(1)} %copy-done.2, s32[16,128]{1,0:T(8,128)S(1)} %bitcast.6, bf16[2,1024,512]{2,1,0:T(8,128)(2,1)S(1)} %assemble.1.partial_ref, bf16[128,1024]{1,0:T(8,128)(2,1)S(1)} %collective-permute-done.13.refs_0_, ...), custom_call_target="tpu_custom_call" | custom-call | flops 2147483648 | tf_op jit(solution)/shard_map/contract/pallas_call | solution.py:221
  (20 shorter events, 0.1 us)
Async XLA Ops:
  0.0 8.9 %copy-start.2 = (s32[2,2]{1,0:T(2,128)S(1)}, s32[2,2]{1,0:T(2,128)}, u32[]{:S(2)}) copy-start(s32[2,2]{1,0:T(2,128)} %op_ref.5) | copy-start | bytes 52
  0.0 8.9 %copy-start.3 = (s32[2,128]{1,0:T(2,128)S(1)}, s32[2,128]{1,0:T(2,128)}, u32[]{:S(2)}) copy-start(s32[2,128]{1,0:T(2,128)} %listed_ref.1) | copy-start | bytes 3076
  0.0 8.9 %copy-start = (bf16[1,2,2,512,512]{4,3,2,1,0:T(8,128)(2,1)S(1)}, bf16[1,2,2,512,512]{4,3,2,1,0:T(8,128)(2,1)}, u32[]{:S(2)}) copy-start(bf16[1,2,2,512,512]{4,3,2,1,0:T(8,128)(2,1)} %sink_ref.1) | copy-start | bytes 6291460
  1.7 37.9 %copy-start.1 = (s32[2048]{0:T(1024)S(1)}, s32[2048]{0:T(1024)}, u32[]{:S(2)}) copy-start(s32[2048]{0:T(1024)} %param.10) | copy-start | bytes 24580
  1.7 12.2 %collective-permute-start.1 = (bf16[128,1024]{1,0:T(8,128)(2,1)S(1)}, bf16[128,1024]{1,0:T(8,128)(2,1)S(1)}, u32[]{:S(2)}, u32[]{:S(2)}) collective-permute-start(bf16[128,1024]{1,0:T(8,128)(2,1)S(1)} %pad_maximum_fusion.refs_0_), channel_id=1, source_target_pairs={{0,4},{4,0},{8,12},{12,8},{16,20},{20,16},{24,28},{28,24},{1,5},{5... | collective-permute-start | bytes 786440 | tf_op jit(solution)/shard_map/ppermute | solution.py:240
  4.7 13.3 %collective-permute-start.3 = (bf16[128,1024]{1,0:T(8,128)(2,1)S(1)}, bf16[128,1024]{1,0:T(8,128)(2,1)S(1)}, u32[]{:S(2)}, u32[]{:S(2)}) collective-permute-start(bf16[128,1024]{1,0:T(8,128)(2,1)S(1)} %pad_maximum_fusion.refs_0_), channel_id=1, source_target_pairs={{0,8},{4,12},{8,0},{12,4},{16,24},{20,28},{24,16},{28,20},{1,9},{5... | collective-permute-start | bytes 786440 | tf_op jit(solution)/shard_map/ppermute | solution.py:240
  6.3 14.0 %collective-permute-start.7 = (bf16[128,1024]{1,0:T(8,128)(2,1)S(1)}, bf16[128,1024]{1,0:T(8,128)(2,1)S(1)}, u32[]{:S(2)}, u32[]{:S(2)}) collective-permute-start(bf16[128,1024]{1,0:T(8,128)(2,1)S(1)} %pad_maximum_fusion.refs_0_), channel_id=1, source_target_pairs={{0,16},{4,20},{8,24},{12,28},{16,0},{20,4},{24,8},{28,12},{1,17},{... | collective-permute-start | bytes 786440 | tf_op jit(solution)/shard_map/ppermute | solution.py:240
  13.9 8.9 %collective-permute-start.2 = (bf16[128,1024]{1,0:T(8,128)(2,1)S(1)}, bf16[128,1024]{1,0:T(8,128)(2,1)S(1)}, u32[]{:S(2)}, u32[]{:S(2)}) collective-permute-start(bf16[128,1024]{1,0:T(8,128)(2,1)S(1)} %collective-permute-done.1.refs_2_), channel_id=1, source_target_pairs={{0,1},{1,0},{2,3},{3,2},{4,5},{5,4},{6,7},{7,6},{8,9},{9,8},{10,11... | collective-permute-start | bytes 786440 | tf_op jit(solution)/shard_map/ppermute | solution.py:240
  18.0 4.8 %collective-permute-start.4 = (bf16[128,1024]{1,0:T(8,128)(2,1)S(1)}, bf16[128,1024]{1,0:T(8,128)(2,1)S(1)}, u32[]{:S(2)}, u32[]{:S(2)}) collective-permute-start(bf16[128,1024]{1,0:T(8,128)(2,1)S(1)} %collective-permute-done.3.refs_4_), channel_id=1, source_target_pairs={{0,1},{1,0},{2,3},{3,2},{4,5},{5,4},{6,7},{7,6},{8,9},{9,8},{10,11... | collective-permute-start | bytes 786440 | tf_op jit(solution)/shard_map/ppermute | solution.py:240
  18.0 14.3 %collective-permute-start.16 = (bf16[1,2,4,64,512]{4,3,2,1,0:T(8,128)(2,1)S(1)}, bf16[1,2,4,64,512]{4,3,2,1,0:T(8,128)(2,1)S(1)}, u32[]{:S(2)}, u32[]{:S(2)}) collective-permute-start(bf16[1,2,4,64,512]{4,3,2,1,0:T(8,128)(2,1)S(1)} %get-tuple-element.29), channel_id=1, source_target_pairs={{0,2},{1,3},{2,0},{3,1},{4,6},{5,7},{6,4},{7,5},{8,10},{9,11},{10,... | collective-permute-start | bytes 1572872 | tf_op jit(solution)/shard_map/ppermute | solution.py:240
  20.4 3.0 %collective-permute-start.8 = (bf16[128,1024]{1,0:T(8,128)(2,1)S(1)}, bf16[128,1024]{1,0:T(8,128)(2,1)S(1)}, u32[]{:S(2)}, u32[]{:S(2)}) collective-permute-start(bf16[128,1024]{1,0:T(8,128)(2,1)S(1)} %collective-permute-done.7.refs_8_), channel_id=1, source_target_pairs={{0,1},{1,0},{2,3},{3,2},{4,5},{5,4},{6,7},{7,6},{8,9},{9,8},{10,11... | collective-permute-start | bytes 786440 | tf_op jit(solution)/shard_map/ppermute | solution.py:240
  20.4 10.6 %collective-permute-start.11 = (bf16[128,1024]{1,0:T(8,128)(2,1)S(1)}, bf16[128,1024]{1,0:T(8,128)(2,1)S(1)}, u32[]{:S(2)}, u32[]{:S(2)}) collective-permute-start(bf16[128,1024]{1,0:T(8,128)(2,1)S(1)} %pad_maximum_fusion.refs_0_), channel_id=1, source_target_pairs={{0,24},{4,28},{8,16},{12,20},{16,8},{20,12},{24,0},{28,4},{1,25},{... | collective-permute-start | bytes 786440 | tf_op jit(solution)/shard_map/ppermute | solution.py:240
  22.8 9.1 %collective-permute-start.5 = (bf16[128,1024]{1,0:T(8,128)(2,1)S(1)}, bf16[128,1024]{1,0:T(8,128)(2,1)S(1)}, u32[]{:S(2)}, u32[]{:S(2)}) collective-permute-start(bf16[128,1024]{1,0:T(8,128)(2,1)S(1)} %collective-permute-done.3.refs_4_), channel_id=1, source_target_pairs={{0,4},{4,0},{8,12},{12,8},{16,20},{20,16},{24,28},{28,24},{1,5},{5... | collective-permute-start | bytes 786440 | tf_op jit(solution)/shard_map/ppermute | solution.py:240
  23.4 13.5 %collective-permute-start.9 = (bf16[128,1024]{1,0:T(8,128)(2,1)S(1)}, bf16[128,1024]{1,0:T(8,128)(2,1)S(1)}, u32[]{:S(2)}, u32[]{:S(2)}) collective-permute-start(bf16[128,1024]{1,0:T(8,128)(2,1)S(1)} %collective-permute-done.7.refs_8_), channel_id=1, source_target_pairs={{0,4},{4,0},{8,12},{12,8},{16,20},{20,16},{24,28},{28,24},{1,5},{5... | collective-permute-start | bytes 786440 | tf_op jit(solution)/shard_map/ppermute | solution.py:240
  24.9 12.0 %collective-permute-start = (bf16[128,1024]{1,0:T(8,128)(2,1)S(1)}, bf16[128,1024]{1,0:T(8,128)(2,1)S(1)}, u32[]{:S(2)}, u32[]{:S(2)}) collective-permute-start(bf16[128,1024]{1,0:T(8,128)(2,1)S(1)} %pad_maximum_fusion.refs_0_), channel_id=1, source_target_pairs={{0,1},{1,0},{2,3},{3,2},{4,5},{5,4},{6,7},{7,6},{8,9},{9,8},{10,11... | collective-permute-start | bytes 786440 | tf_op jit(solution)/shard_map/ppermute | solution.py:240
  31.0 6.5 %collective-permute-start.12 = (bf16[128,1024]{1,0:T(8,128)(2,1)S(1)}, bf16[128,1024]{1,0:T(8,128)(2,1)S(1)}, u32[]{:S(2)}, u32[]{:S(2)}) collective-permute-start(bf16[128,1024]{1,0:T(8,128)(2,1)S(1)} %collective-permute-done.11.refs_12_), channel_id=1, source_target_pairs={{0,1},{1,0},{2,3},{3,2},{4,5},{5,4},{6,7},{7,6},{8,9},{9,8},{10,11... | collective-permute-start | bytes 786440 | tf_op jit(solution)/shard_map/ppermute | solution.py:240
  32.0 7.0 %collective-permute-start.6 = (bf16[128,1024]{1,0:T(8,128)(2,1)S(1)}, bf16[128,1024]{1,0:T(8,128)(2,1)S(1)}, u32[]{:S(2)}, u32[]{:S(2)}) collective-permute-start(bf16[128,1024]{1,0:T(8,128)(2,1)S(1)} %collective-permute-done.5.refs_6_), channel_id=1, source_target_pairs={{0,1},{1,0},{2,3},{3,2},{4,5},{5,4},{6,7},{7,6},{8,9},{9,8},{10,11... | collective-permute-start | bytes 786440 | tf_op jit(solution)/shard_map/ppermute | solution.py:240
  32.3 13.3 %collective-permute-start.15 = (bf16[1,2,4,64,512]{4,3,2,1,0:T(8,128)(2,1)S(1)}, bf16[1,2,4,64,512]{4,3,2,1,0:T(8,128)(2,1)S(1)}, u32[]{:S(2)}, u32[]{:S(2)}) collective-permute-start(bf16[1,2,4,64,512]{4,3,2,1,0:T(8,128)(2,1)S(1)} %get-tuple-element.27), channel_id=1, source_target_pairs={{0,1},{1,0},{2,3},{3,2},{4,5},{5,4},{6,7},{7,6},{8,9},{9,8},{10,11... | collective-permute-start | bytes 1572872 | tf_op jit(solution)/shard_map/ppermute | solution.py:240
  36.9 2.7 %collective-permute-start.10 = (bf16[128,1024]{1,0:T(8,128)(2,1)S(1)}, bf16[128,1024]{1,0:T(8,128)(2,1)S(1)}, u32[]{:S(2)}, u32[]{:S(2)}) collective-permute-start(bf16[128,1024]{1,0:T(8,128)(2,1)S(1)} %collective-permute-done.9.refs_10_), channel_id=1, source_target_pairs={{0,1},{1,0},{2,3},{3,2},{4,5},{5,4},{6,7},{7,6},{8,9},{9,8},{10,11... | collective-permute-start | bytes 786440 | tf_op jit(solution)/shard_map/ppermute | solution.py:240
  36.9 8.7 %collective-permute-start.13 = (bf16[128,1024]{1,0:T(8,128)(2,1)S(1)}, bf16[128,1024]{1,0:T(8,128)(2,1)S(1)}, u32[]{:S(2)}, u32[]{:S(2)}) collective-permute-start(bf16[128,1024]{1,0:T(8,128)(2,1)S(1)} %collective-permute-done.11.refs_12_), channel_id=1, source_target_pairs={{0,4},{4,0},{8,12},{12,8},{16,20},{20,16},{24,28},{28,24},{1,5},{5... | collective-permute-start | bytes 786440 | tf_op jit(solution)/shard_map/ppermute | solution.py:240
  37.4 14.1 %collective-permute-start.17 = (bf16[1,2,4,64,512]{4,3,2,1,0:T(8,128)(2,1)S(1)}, bf16[1,2,4,64,512]{4,3,2,1,0:T(8,128)(2,1)S(1)}, u32[]{:S(2)}, u32[]{:S(2)}) collective-permute-start(bf16[1,2,4,64,512]{4,3,2,1,0:T(8,128)(2,1)S(1)} %get-tuple-element.30), channel_id=1, source_target_pairs={{0,2},{1,3},{2,0},{3,1},{4,6},{5,7},{6,4},{7,5},{8,10},{9,11},{10,... | collective-permute-start | bytes 1572872 | tf_op jit(solution)/shard_map/ppermute | solution.py:240
  39.0 12.5 %collective-permute-start.18 = (bf16[1,2,4,64,512]{4,3,2,1,0:T(8,128)(2,1)S(1)}, bf16[1,2,4,64,512]{4,3,2,1,0:T(8,128)(2,1)S(1)}, u32[]{:S(2)}, u32[]{:S(2)}) collective-permute-start(bf16[1,2,4,64,512]{4,3,2,1,0:T(8,128)(2,1)S(1)} %collective-permute-done.16), channel_id=1, source_target_pairs={{0,1},{1,0},{2,3},{3,2},{4,5},{5,4},{6,7},{7,6},{8,9},{9,8},{10,11... | collective-permute-start | bytes 1572872 | tf_op jit(solution)/shard_map/ppermute | solution.py:240
  45.6 5.9 %collective-permute-start.14 = (bf16[128,1024]{1,0:T(8,128)(2,1)S(1)}, bf16[128,1024]{1,0:T(8,128)(2,1)S(1)}, u32[]{:S(2)}, u32[]{:S(2)}) collective-permute-start(bf16[128,1024]{1,0:T(8,128)(2,1)S(1)} %collective-permute-done.13.refs_0_), channel_id=1, source_target_pairs={{0,1},{1,0},{2,3},{3,2},{4,5},{5,4},{6,7},{7,6},{8,9},{9,8},{10,11... | collective-permute-start | bytes 786440 | tf_op jit(solution)/shard_map/ppermute | solution.py:240

commit v3 on v1

--- a/solution.py
+++ b/solution.py
@@ -152,11 +152,25 @@
     )(source, op_index, slots, *pieces)
 
 
-def contract_kernel(places, n_cols, source_ref, op_ref, slot_ref, partial_ref, *refs):
+def block_rows(parts, k):
+    if len(parts) == 1:
+        found = [parts[0][0, k]]
+    else:
+        per = NS // parts[0].shape[2]
+        found = [part[0, 0] for part in parts[k * per : (k + 1) * per]]
+    return jnp.concatenate([f.reshape(-1, f.shape[-1]) for f in found], axis=0)
+
+
+def contract_kernel(places, counts, source_ref, op_ref, slot_ref, partial_ref, *refs):
     n_pieces = len(places)
-    pieces, blocks = refs[:n_pieces], refs[n_pieces : n_pieces + n_cols]
-    out_ref, right, done, sems = refs[n_pieces + n_cols :]
-    own2, local_cols = blocks[0].shape[3], blocks[0].shape[4]
+    pieces, refs = refs[:n_pieces], refs[n_pieces:]
+    blocks = []
+    for count in counts:
+        blocks.append(refs[:count])
+        refs = refs[count:]
+    n_cols = len(blocks)
+    out_ref, right, done, sems = refs
+    own2, local_cols = blocks[0][0].shape[3:]
     products, eigen = right.shape[0], right.shape[2]
     rows = NS * own2
     total = add_pieces(places, (source_ref, op_ref), slot_ref, pieces, products, eigen)
@@ -173,7 +187,7 @@
     for k in range(products):
         direct, turned = [], []
         for j in range(n_cols):
-            x = blocks[j][0, k].reshape(rows, local_cols)
+            x = block_rows(blocks[j], k)
             wide = x.astype(F32)
             y = jnp.where(odd, pltpu.roll(wide, 1, 0), -pltpu.roll(wide, rows - 1, 0))
             direct.append(x)
@@ -211,16 +225,17 @@
 
 
 def contract(places, pieces, partial, source, op_index, slots, blocks):
-    _, products, _, own2, local_cols = blocks[0].shape
+    _, products, _, own2, local_cols = blocks[0][0].shape
     n_cols = len(blocks)
+    parts = [part for block in blocks for part in block]
     eigen = partial.shape[2]
     order = n_cols * local_cols
     times = order // eigen
     vmem = pl.BlockSpec(memory_space=pltpu.VMEM)
     smem = pl.BlockSpec(memory_space=pltpu.SMEM)
     return pl.pallas_call(
-        functools.partial(contract_kernel, places, n_cols),
-        in_specs=[smem, smem] + [vmem] * (2 + len(pieces) + n_cols),
+        functools.partial(contract_kernel, places, [len(block) for block in blocks]),
+        in_specs=[smem, smem] + [vmem] * (2 + len(pieces) + len(parts)),
         out_specs=pl.BlockSpec(memory_space=pl.ANY),
         out_shape=jax.ShapeDtypeStruct((products, NS, own2 // 2, 2, order), BF16),
         scratch_shapes=[
@@ -233,7 +248,7 @@
             flops=4 * products * eigen * NS * own2 * order, bytes_accessed=0, transcendentals=0
         ),
         name="contract",
-    )(source, op_index, slots, partial, *pieces, *blocks)
+    )(source, op_index, slots, partial, *pieces, *parts)
 
 
 def swap(array, axis, size, mask):
@@ -261,7 +276,7 @@
         whole = lax.all_gather(own, "tpair", axis=0, tiled=True)
         half = whole.shape[0] // 2
         mixed = mix(op_index, listed_rows, sink_ops, peramb, [1] * n_cols)
-        blocks = [mixed[0]] + [swap(mixed[j], "col", n_cols, j) for j in range(1, n_cols)]
+        blocks = [[mixed[0]]] + [[swap(mixed[j], "col", n_cols, j)] for j in range(1, n_cols)]
         partial = assemble([0], [whole[:half]], pair_source, op_index, slots, eigen)
         return contract(
             [half], [whole[half:]], partial, pair_source, op_index, slots, blocks
@@ -269,18 +284,25 @@
     half = rows // 2
     own = lax.dynamic_slice_in_dim(op_table, lax.axis_index("col") % 2 * half, half, 0)
     own = jnp.concatenate([own[:, 0], own[:, 1]], axis=1)
-    held = {(0, 0): own, (0, 1): beside(own)}
+    held = {(0, 0): own}
     for mask in (4, 2, 1):
         held[mask, 0] = across(own, mask)
-    mixed = mix(op_index, after(listed_rows, held[0, 1]), sink_ops, peramb, [1, 1, 2])
+    mixed = mix(op_index, listed_rows, sink_ops, peramb, [1, 1, 2])
     crossed = swap(mixed[2], "col", n_cols, 2)
-    blocks = [mixed[0], beside(mixed[1]), crossed, beside(crossed[1:])]
+    halves = [
+        beside(crossed[1:, k : k + 1, s : s + NS // 2])
+        for k in range(mixed[2].shape[1])
+        for s in (0, NS // 2)
+    ]
+    blocks = [[mixed[0]], [beside(mixed[1])], [crossed], halves]
+    for mask in (0, 1, 2, 4):
+        held[mask, 1] = beside(after(held[mask, 0], mixed[0]))
     held[3, 0] = across(after(held[2, 0], mixed[0], held[1, 0]), 1)
     held[6, 0] = across(after(own, mixed[0]), 6)
-    held[5, 0] = across(after(held[4, 0], held[3, 0]), 1)
     held[6, 1] = beside(held[6, 0])
+    held[5, 0] = across(after(held[4, 0], held[4, 1], held[3, 0]), 1)
     held[7, 0] = across(after(held[6, 0], held[6, 1], held[5, 0]), 1)
-    for mask in (1, 2, 3, 4, 5):
+    for mask in (3, 5):
         held[mask, 1] = beside(held[mask, 0])
     early = [(mask, side) for mask in range(7) for side in (0, 1)]
     partial = assemble(early, [held[p] for p in early], pair_source, op_index, slots, eigen)

time: 56.5 us -> 54.6 us (0.966)
  the two profiles are of different devices: /device:TPU:0 before, /device:TPU:13 now
where the time goes in v3:
time: 54.6 us; the launch traced here: 54.4 us
  waiting for transfers between devices  19.6 us (36%)
  starting transfers between devices  18.3 us (34%)
  Pallas kernels  14 us (26%)
  local copies, waits for them, and re-layouts  1.7 us (3%)
  between operations  0.75 us (1%)
    ppermute x21, waiting for transfers between devices, swap(): return lax.ppermute(array, axis, [(i, i ^ mask) for i in range(size)])  19.6 us
    ppermute x21, starting transfers between devices, swap(): return lax.ppermute(array, axis, [(i, i ^ mask) for i in range(size)])  18.3 us
    pallas_call x1, Pallas kernels, mix(): pl.pallas_call(mix_kernel, in_specs=[pl.BlockSpec(memory_space=pltpu.SMEM...  4.99 us
    pallas_call x1, Pallas kernels, assemble(): pl.pallas_call(functools.partial(assemble_kernel, places), in_specs=[smem...  4.56 us
    pallas_call x1, Pallas kernels, contract(): pl.pallas_call(functools.partial(contract_kernel, places, [len(block) for...  4.47 us
    slice x1, local copies, waits for them, and re-layouts, per_device(): own = jnp.concatenate([own[:, 0], own[:, 1]], axis=1)  1.61 us
  transfers between devices with their start and end apart: 21, of which 12 were waited for; matrix products, arithmetic and copies ran while one was open for 0% of the time, Pallas kernels for 18%

profile of v3, /device:TPU:13, one launch (start us, length us, event | category | flops | bytes accessed | tf_op | source)
XLA Modules:
  0.0 54.4 jit_solution(14857690352559258800)
XLA Ops:
  0.0 1.6 %constant_dynamic-slice_fusion = (bf16[128,1,512]{2,1,0:T(2,128)(2,1)S(1)}, bf16[128,1,512]{2,1,0:T(2,128)(2,1)S(1)}) fusion(bf16[256,2,512]{2,1,0:T(2,128)(2,1)} %param.9, s32[]{:T(128)S(6)} %select_n.11, s32[]{:T(128)S(6)} %add.9), kind=kLoop, calls=%fused_computation.3 | loop fusion | bytes 524296 | tf_op jit(solution)/shard_map/slice | solution.py:286
  1.7 1.3 %collective-permute-start.1 = (bf16[128,1024]{1,0:T(8,128)(2,1)S(1)}, bf16[128,1024]{1,0:T(8,128)(2,1)S(1)}, u32[]{:S(2)}, u32[]{:S(2)}) collective-permute-start(bf16[128,1024]{1,0:T(8,128)(2,1)S(1)} %pad_maximum_fusion.refs_0_), channel_id=1, source_target_pairs={{0,4},{4,0},{8,12},{12,8},{16,20},{20,16},{24,28},{28,24},{1,5},{5... | collective-permute-start | bytes 786440 | tf_op jit(solution)/shard_map/ppermute | solution.py:255
  3.2 2.3 %collective-permute-start.7 = (bf16[128,1024]{1,0:T(8,128)(2,1)S(1)}, bf16[128,1024]{1,0:T(8,128)(2,1)S(1)}, u32[]{:S(2)}, u32[]{:S(2)}) collective-permute-start(bf16[128,1024]{1,0:T(8,128)(2,1)S(1)} %pad_maximum_fusion.refs_0_), channel_id=1, source_target_pairs={{0,16},{4,20},{8,24},{12,28},{16,0},{20,4},{24,8},{28,12},{1,17},{... | collective-permute-start | bytes 786440 | tf_op jit(solution)/shard_map/ppermute | solution.py:255
  5.5 5.0 %mix.1 = (bf16[1,2,4,64,512]{4,3,2,1,0:T(8,128)(2,1)S(1)}, bf16[1,2,4,64,512]{4,3,2,1,0:T(8,128)(2,1)S(1)}, bf16[2,2,4,64,512]{4,3,2,1,0:T(8,128)(2,1)S(1)}) custom-call(s32[2,2]{1,0:T(2,128)S(1)} %copy-done.2, s32[2,128]{1,0:T(2,128)S(1)} %copy-done.3, bf16[1,2,2,512,512]{4,3,2,1,0:T(8,128)(2,1)S(1)} %copy-done, bf16[1,2,2048,512]{3,2,1,0:T(8,128)(2,1)} %peramb_ref.1), custom_call_target="tpu_custom_call" | custom-call | flops 1000 | bytes 1000 | tf_op jit(solution)/shard_map/mix/pallas_call | solution.py:88
  10.5 0.2 collective-permute-start.11
  10.7 0.2 collective-permute-start.16
  10.9 2.0 %collective-permute-done.3.refs_4_ = bf16[128,1024]{1,0:T(8,128)(2,1)S(1)} collective-permute-done((bf16[128,1024]{1,0:T(8,128)(2,1)S(1)}, bf16[128,1024]{1,0:T(8,128)(2,1)S(1)}, u32[]{:S(2)}, u32[]{:S(2)}) %collective-permute-start.3) | collective-permute-done | bytes 262176 | tf_op jit(solution)/shard_map/ppermute | solution.py:255
  13.0 0.3 collective-permute-start.5
  13.2 3.3 %collective-permute-done.7.refs_8_ = bf16[128,1024]{1,0:T(8,128)(2,1)S(1)} collective-permute-done((bf16[128,1024]{1,0:T(8,128)(2,1)S(1)}, bf16[128,1024]{1,0:T(8,128)(2,1)S(1)}, u32[]{:S(2)}, u32[]{:S(2)}) %collective-permute-start.7) | collective-permute-done | bytes 262176 | tf_op jit(solution)/shard_map/ppermute | solution.py:255
  16.5 8.3 %collective-permute-start.8 = (bf16[128,1024]{1,0:T(8,128)(2,1)S(1)}, bf16[128,1024]{1,0:T(8,128)(2,1)S(1)}, u32[]{:S(2)}, u32[]{:S(2)}) collective-permute-start(bf16[128,1024]{1,0:T(8,128)(2,1)S(1)} %collective-permute-done.7.refs_8_), channel_id=1, source_target_pairs={{0,1},{1,0},{2,3},{3,2},{4,5},{5,4},{6,7},{7,6},{8,9},{9,8},{10,11... | collective-permute-start | bytes 786440 | tf_op jit(solution)/shard_map/ppermute | solution.py:255
  24.8 4.2 %collective-permute-done.11.refs_12_ = bf16[128,1024]{1,0:T(8,128)(2,1)S(1)} collective-permute-done((bf16[128,1024]{1,0:T(8,128)(2,1)S(1)}, bf16[128,1024]{1,0:T(8,128)(2,1)S(1)}, u32[]{:S(2)}, u32[]{:S(2)}) %collective-permute-start.11) | collective-permute-done | bytes 262176 | tf_op jit(solution)/shard_map/ppermute | solution.py:255
  29.0 0.8 %collective-permute-start.12 = (bf16[128,1024]{1,0:T(8,128)(2,1)S(1)}, bf16[128,1024]{1,0:T(8,128)(2,1)S(1)}, u32[]{:S(2)}, u32[]{:S(2)}) collective-permute-start(bf16[128,1024]{1,0:T(8,128)(2,1)S(1)} %collective-permute-done.11.refs_12_), channel_id=1, source_target_pairs={{0,1},{1,0},{2,3},{3,2},{4,5},{5,4},{6,7},{7,6},{8,9},{9,8},{10,11... | collective-permute-start | bytes 786440 | tf_op jit(solution)/shard_map/ppermute | solution.py:255
  29.8 0.3 collective-permute-start.9
  30.1 0.3 collective-permute-start
  30.6 0.4 collective-permute-done.12.refs_13_
  31.0 0.4 collective-permute-start.4
  31.3 6.3 %collective-permute-done.9.refs_10_ = bf16[128,1024]{1,0:T(8,128)(2,1)S(1)} collective-permute-done((bf16[128,1024]{1,0:T(8,128)(2,1)S(1)}, bf16[128,1024]{1,0:T(8,128)(2,1)S(1)}, u32[]{:S(2)}, u32[]{:S(2)}) %collective-permute-start.9) | collective-permute-done | bytes 262176 | tf_op jit(solution)/shard_map/ppermute | solution.py:255
  37.7 0.9 %collective-permute-start.15 = (bf16[1,2,4,64,512]{4,3,2,1,0:T(8,128)(2,1)S(1)}, bf16[1,2,4,64,512]{4,3,2,1,0:T(8,128)(2,1)S(1)}, u32[]{:S(2)}, u32[]{:S(2)}) collective-permute-start(bf16[1,2,4,64,512]{4,3,2,1,0:T(8,128)(2,1)S(1)} %get-tuple-element.25), channel_id=1, source_target_pairs={{0,1},{1,0},{2,3},{3,2},{4,5},{5,4},{6,7},{7,6},{8,9},{9,8},{10,11... | collective-permute-start | bytes 1572872 | tf_op jit(solution)/shard_map/ppermute | solution.py:255
  38.5 0.5 collective-permute-start.10
  39.1 0.3 collective-permute-start.13
  40.0 0.5 collective-permute-done.6.refs_7_
  40.4 0.4 collective-permute-done.10.refs_11_
  40.8 4.6 %assemble.1.partial_ref = bf16[2,1024,512]{2,1,0:T(8,128)(2,1)S(1)} custom-call(s32[1]{0:T(128)S(6)} %copy.14.source_ref, s32[2,2]{1,0:T(2,128)S(1)} %copy-done.2, s32[16,128]{1,0:T(8,128)S(1)} %bitcast.5, bf16[128,1024]{1,0:T(8,128)(2,1)S(1)} %pad_maximum_fusion.refs_0_, bf16[128,1024]{1,0:T(8,128)(2,1)S(1)} %collective-permute-done.refs_1_, ...), custom_call_target="tpu_custom_call" | custom-call | flops 1000 | bytes 1000 | tf_op jit(solution)/shard_map/assemble/pallas_call | solution.py:144
  45.4 1.5 %collective-permute-done.13.refs_0_ = bf16[128,1024]{1,0:T(8,128)(2,1)S(1)} collective-permute-done((bf16[128,1024]{1,0:T(8,128)(2,1)S(1)}, bf16[128,1024]{1,0:T(8,128)(2,1)S(1)}, u32[]{:S(2)}, u32[]{:S(2)}) %collective-permute-start.13) | collective-permute-done | bytes 262176 | tf_op jit(solution)/shard_map/ppermute | solution.py:255
  46.9 0.9 %collective-permute-start.14 = (bf16[128,1024]{1,0:T(8,128)(2,1)S(1)}, bf16[128,1024]{1,0:T(8,128)(2,1)S(1)}, u32[]{:S(2)}, u32[]{:S(2)}) collective-permute-start(bf16[128,1024]{1,0:T(8,128)(2,1)S(1)} %collective-permute-done.13.refs_0_), channel_id=1, source_target_pairs={{0,1},{1,0},{2,3},{3,2},{4,5},{5,4},{6,7},{7,6},{8,9},{9,8},{10,11... | collective-permute-start | bytes 786440 | tf_op jit(solution)/shard_map/ppermute | solution.py:255
  47.9 0.5 collective-permute-start.18
  48.5 0.4 collective-permute-start.20
  48.9 0.3 collective-permute-done.17.refs_5_
  49.2 0.2 collective-permute-done.18.refs_6_
  49.4 0.3 collective-permute-done.19.refs_7_
  49.7 0.2 collective-permute-done.20.refs_8_
  49.9 4.5 %contract.1 = bf16[2,4,32,2,2048]{4,3,2,1,0:T(2,128)(2,1)} custom-call(s32[1]{0:T(128)S(6)} %copy.14.source_ref, s32[2,2]{1,0:T(2,128)S(1)} %copy-done.2, s32[16,128]{1,0:T(8,128)S(1)} %bitcast.6, bf16[2,1024,512]{2,1,0:T(8,128)(2,1)S(1)} %assemble.1.partial_ref, bf16[128,1024]{1,0:T(8,128)(2,1)S(1)} %collective-permute-done.13.refs_0_, ...), custom_call_target="tpu_custom_call" | custom-call | flops 2147483648 | tf_op jit(solution)/shard_map/contract/pallas_call | solution.py:236
  (25 shorter events, 0.6 us)
Async XLA Ops:
  0.0 5.5 %copy-start.2 = (s32[2,2]{1,0:T(2,128)S(1)}, s32[2,2]{1,0:T(2,128)}, u32[]{:S(2)}) copy-start(s32[2,2]{1,0:T(2,128)} %op_ref.5) | copy-start | bytes 52
  0.0 5.5 %copy-start.3 = (s32[2,128]{1,0:T(2,128)S(1)}, s32[2,128]{1,0:T(2,128)}, u32[]{:S(2)}) copy-start(s32[2,128]{1,0:T(2,128)} %listed_ref.1) | copy-start | bytes 3076
  0.0 5.5 %copy-start = (bf16[1,2,2,512,512]{4,3,2,1,0:T(8,128)(2,1)S(1)}, bf16[1,2,2,512,512]{4,3,2,1,0:T(8,128)(2,1)}, u32[]{:S(2)}) copy-start(bf16[1,2,2,512,512]{4,3,2,1,0:T(8,128)(2,1)} %sink_ref.1) | copy-start | bytes 6291460
  1.7 39.1 %copy-start.1 = (s32[2048]{0:T(1024)S(1)}, s32[2048]{0:T(1024)}, u32[]{:S(2)}) copy-start(s32[2048]{0:T(1024)} %param.10) | copy-start | bytes 24580
  1.7 9.2 %collective-permute-start.1 = (bf16[128,1024]{1,0:T(8,128)(2,1)S(1)}, bf16[128,1024]{1,0:T(8,128)(2,1)S(1)}, u32[]{:S(2)}, u32[]{:S(2)}) collective-permute-start(bf16[128,1024]{1,0:T(8,128)(2,1)S(1)} %pad_maximum_fusion.refs_0_), channel_id=1, source_target_pairs={{0,4},{4,0},{8,12},{12,8},{16,20},{20,16},{24,28},{28,24},{1,5},{5... | collective-permute-start | bytes 786440 | tf_op jit(solution)/shard_map/ppermute | solution.py:255
  3.0 10.0 %collective-permute-start.3 = (bf16[128,1024]{1,0:T(8,128)(2,1)S(1)}, bf16[128,1024]{1,0:T(8,128)(2,1)S(1)}, u32[]{:S(2)}, u32[]{:S(2)}) collective-permute-start(bf16[128,1024]{1,0:T(8,128)(2,1)S(1)} %pad_maximum_fusion.refs_0_), channel_id=1, source_target_pairs={{0,8},{4,12},{8,0},{12,4},{16,24},{20,28},{24,16},{28,20},{1,9},{5... | collective-permute-start | bytes 786440 | tf_op jit(solution)/shard_map/ppermute | solution.py:255
  3.2 13.4 %collective-permute-start.7 = (bf16[128,1024]{1,0:T(8,128)(2,1)S(1)}, bf16[128,1024]{1,0:T(8,128)(2,1)S(1)}, u32[]{:S(2)}, u32[]{:S(2)}) collective-permute-start(bf16[128,1024]{1,0:T(8,128)(2,1)S(1)} %pad_maximum_fusion.refs_0_), channel_id=1, source_target_pairs={{0,16},{4,20},{8,24},{12,28},{16,0},{20,4},{24,8},{28,12},{1,17},{... | collective-permute-start | bytes 786440 | tf_op jit(solution)/shard_map/ppermute | solution.py:255
  10.5 18.5 %collective-permute-start.11 = (bf16[128,1024]{1,0:T(8,128)(2,1)S(1)}, bf16[128,1024]{1,0:T(8,128)(2,1)S(1)}, u32[]{:S(2)}, u32[]{:S(2)}) collective-permute-start(bf16[128,1024]{1,0:T(8,128)(2,1)S(1)} %pad_maximum_fusion.refs_0_), channel_id=1, source_target_pairs={{0,24},{4,28},{8,16},{12,20},{16,8},{20,12},{24,0},{28,4},{1,25},{... | collective-permute-start | bytes 786440 | tf_op jit(solution)/shard_map/ppermute | solution.py:255
  10.7 37.1 %collective-permute-start.16 = (bf16[2,2,4,64,512]{4,3,2,1,0:T(8,128)(2,1)S(1)}, bf16[2,2,4,64,512]{4,3,2,1,0:T(8,128)(2,1)S(1)}, u32[]{:S(2)}, u32[]{:S(2)}) collective-permute-start(bf16[2,2,4,64,512]{4,3,2,1,0:T(8,128)(2,1)S(1)} %get-tuple-element.26), channel_id=1, source_target_pairs={{0,2},{1,3},{2,0},{3,1},{4,6},{5,7},{6,4},{7,5},{8,10},{9,11},{10,... | collective-permute-start | bytes 3145736 | tf_op jit(solution)/shard_map/ppermute | solution.py:255
  13.0 16.8 %collective-permute-start.5 = (bf16[128,1024]{1,0:T(8,128)(2,1)S(1)}, bf16[128,1024]{1,0:T(8,128)(2,1)S(1)}, u32[]{:S(2)}, u32[]{:S(2)}) collective-permute-start(bf16[128,1024]{1,0:T(8,128)(2,1)S(1)} %collective-permute-done.3.refs_4_), channel_id=1, source_target_pairs={{0,4},{4,0},{8,12},{12,8},{16,20},{20,16},{24,28},{28,24},{1,5},{5... | collective-permute-start | bytes 786440 | tf_op jit(solution)/shard_map/ppermute | solution.py:255
  16.5 13.3 %collective-permute-start.8 = (bf16[128,1024]{1,0:T(8,128)(2,1)S(1)}, bf16[128,1024]{1,0:T(8,128)(2,1)S(1)}, u32[]{:S(2)}, u32[]{:S(2)}) collective-permute-start(bf16[128,1024]{1,0:T(8,128)(2,1)S(1)} %collective-permute-done.7.refs_8_), channel_id=1, source_target_pairs={{0,1},{1,0},{2,3},{3,2},{4,5},{5,4},{6,7},{7,6},{8,9},{9,8},{10,11... | collective-permute-start | bytes 786440 | tf_op jit(solution)/shard_map/ppermute | solution.py:255
  29.0 2.0 %collective-permute-start.12 = (bf16[128,1024]{1,0:T(8,128)(2,1)S(1)}, bf16[128,1024]{1,0:T(8,128)(2,1)S(1)}, u32[]{:S(2)}, u32[]{:S(2)}) collective-permute-start(bf16[128,1024]{1,0:T(8,128)(2,1)S(1)} %collective-permute-done.11.refs_12_), channel_id=1, source_target_pairs={{0,1},{1,0},{2,3},{3,2},{4,5},{5,4},{6,7},{7,6},{8,9},{9,8},{10,11... | collective-permute-start | bytes 786440 | tf_op jit(solution)/shard_map/ppermute | solution.py:255
  29.8 7.9 %collective-permute-start.9 = (bf16[128,1024]{1,0:T(8,128)(2,1)S(1)}, bf16[128,1024]{1,0:T(8,128)(2,1)S(1)}, u32[]{:S(2)}, u32[]{:S(2)}) collective-permute-start(bf16[128,1024]{1,0:T(8,128)(2,1)S(1)} %collective-permute-done.7.refs_8_), channel_id=1, source_target_pairs={{0,4},{4,0},{8,12},{12,8},{16,20},{20,16},{24,28},{28,24},{1,5},{5... | collective-permute-start | bytes 786440 | tf_op jit(solution)/shard_map/ppermute | solution.py:255
  30.1 8.5 %collective-permute-start = (bf16[128,1024]{1,0:T(8,128)(2,1)S(1)}, bf16[128,1024]{1,0:T(8,128)(2,1)S(1)}, u32[]{:S(2)}, u32[]{:S(2)}) collective-permute-start(bf16[128,1024]{1,0:T(8,128)(2,1)S(1)} %pad_maximum_fusion.refs_0_), channel_id=1, source_target_pairs={{0,1},{1,0},{2,3},{3,2},{4,5},{5,4},{6,7},{7,6},{8,9},{9,8},{10,11... | collective-permute-start | bytes 786440 | tf_op jit(solution)/shard_map/ppermute | solution.py:255
  30.4 8.1 %collective-permute-start.2 = (bf16[128,1024]{1,0:T(8,128)(2,1)S(1)}, bf16[128,1024]{1,0:T(8,128)(2,1)S(1)}, u32[]{:S(2)}, u32[]{:S(2)}) collective-permute-start(bf16[128,1024]{1,0:T(8,128)(2,1)S(1)} %collective-permute-done.1.refs_2_), channel_id=1, source_target_pairs={{0,1},{1,0},{2,3},{3,2},{4,5},{5,4},{6,7},{7,6},{8,9},{9,8},{10,11... | collective-permute-start | bytes 786440 | tf_op jit(solution)/shard_map/ppermute | solution.py:255
  31.0 8.1 %collective-permute-start.4 = (bf16[128,1024]{1,0:T(8,128)(2,1)S(1)}, bf16[128,1024]{1,0:T(8,128)(2,1)S(1)}, u32[]{:S(2)}, u32[]{:S(2)}) collective-permute-start(bf16[128,1024]{1,0:T(8,128)(2,1)S(1)} %collective-permute-done.3.refs_4_), channel_id=1, source_target_pairs={{0,1},{1,0},{2,3},{3,2},{4,5},{5,4},{6,7},{7,6},{8,9},{9,8},{10,11... | collective-permute-start | bytes 786440 | tf_op jit(solution)/shard_map/ppermute | solution.py:255
  37.7 10.8 %collective-permute-start.15 = (bf16[1,2,4,64,512]{4,3,2,1,0:T(8,128)(2,1)S(1)}, bf16[1,2,4,64,512]{4,3,2,1,0:T(8,128)(2,1)S(1)}, u32[]{:S(2)}, u32[]{:S(2)}) collective-permute-start(bf16[1,2,4,64,512]{4,3,2,1,0:T(8,128)(2,1)S(1)} %get-tuple-element.25), channel_id=1, source_target_pairs={{0,1},{1,0},{2,3},{3,2},{4,5},{5,4},{6,7},{7,6},{8,9},{9,8},{10,11... | collective-permute-start | bytes 1572872 | tf_op jit(solution)/shard_map/ppermute | solution.py:255
  38.5 1.9 %collective-permute-start.6 = (bf16[128,1024]{1,0:T(8,128)(2,1)S(1)}, bf16[128,1024]{1,0:T(8,128)(2,1)S(1)}, u32[]{:S(2)}, u32[]{:S(2)}) collective-permute-start(bf16[128,1024]{1,0:T(8,128)(2,1)S(1)} %collective-permute-done.5.refs_6_), channel_id=1, source_target_pairs={{0,1},{1,0},{2,3},{3,2},{4,5},{5,4},{6,7},{7,6},{8,9},{9,8},{10,11... | collective-permute-start | bytes 786440 | tf_op jit(solution)/shard_map/ppermute | solution.py:255
  38.5 2.3 %collective-permute-start.10 = (bf16[128,1024]{1,0:T(8,128)(2,1)S(1)}, bf16[128,1024]{1,0:T(8,128)(2,1)S(1)}, u32[]{:S(2)}, u32[]{:S(2)}) collective-permute-start(bf16[128,1024]{1,0:T(8,128)(2,1)S(1)} %collective-permute-done.9.refs_10_), channel_id=1, source_target_pairs={{0,1},{1,0},{2,3},{3,2},{4,5},{5,4},{6,7},{7,6},{8,9},{9,8},{10,11... | collective-permute-start | bytes 786440 | tf_op jit(solution)/shard_map/ppermute | solution.py:255
  39.1 7.9 %collective-permute-start.13 = (bf16[128,1024]{1,0:T(8,128)(2,1)S(1)}, bf16[128,1024]{1,0:T(8,128)(2,1)S(1)}, u32[]{:S(2)}, u32[]{:S(2)}) collective-permute-start(bf16[128,1024]{1,0:T(8,128)(2,1)S(1)} %collective-permute-done.11.refs_12_), channel_id=1, source_target_pairs={{0,4},{4,0},{8,12},{12,8},{16,20},{20,16},{24,28},{28,24},{1,5},{5... | collective-permute-start | bytes 786440 | tf_op jit(solution)/shard_map/ppermute | solution.py:255
  46.9 3.0 %collective-permute-start.14 = (bf16[128,1024]{1,0:T(8,128)(2,1)S(1)}, bf16[128,1024]{1,0:T(8,128)(2,1)S(1)}, u32[]{:S(2)}, u32[]{:S(2)}) collective-permute-start(bf16[128,1024]{1,0:T(8,128)(2,1)S(1)} %collective-permute-done.13.refs_0_), channel_id=1, source_target_pairs={{0,1},{1,0},{2,3},{3,2},{4,5},{5,4},{6,7},{7,6},{8,9},{9,8},{10,11... | collective-permute-start | bytes 786440 | tf_op jit(solution)/shard_map/ppermute | solution.py:255
  47.8 1.4 %collective-permute-start.17 = (bf16[1,1,2,64,512]{4,3,2,1,0:T(8,128)(2,1)S(1)}, bf16[1,1,2,64,512]{4,3,2,1,0:T(8,128)(2,1)S(1)}, u32[]{:S(2)}, u32[]{:S(2)}) collective-permute-start(bf16[1,1,2,64,512]{4,3,2,1,0:T(8,128)(2,1)S(1)} %get-tuple-element.30), channel_id=1, source_target_pairs={{0,1},{1,0},{2,3},{3,2},{4,5},{5,4},{6,7},{7,6},{8,9},{9,8},{10,11... | collective-permute-start | bytes 393224 | tf_op jit(solution)/shard_map/ppermute | solution.py:255
  47.9 1.5 %collective-permute-start.18 = (bf16[1,1,2,64,512]{4,3,2,1,0:T(8,128)(2,1)S(1)}, bf16[1,1,2,64,512]{4,3,2,1,0:T(8,128)(2,1)S(1)}, u32[]{:S(2)}, u32[]{:S(2)}) collective-permute-start(bf16[1,1,2,64,512]{4,3,2,1,0:T(8,128)(2,1)S(1)} %get-tuple-element.29), channel_id=1, source_target_pairs={{0,1},{1,0},{2,3},{3,2},{4,5},{5,4},{6,7},{7,6},{8,9},{9,8},{10,11... | collective-permute-start | bytes 393224 | tf_op jit(solution)/shard_map/ppermute | solution.py:255
  48.4 1.3 %collective-permute-start.19 = (bf16[1,1,2,64,512]{4,3,2,1,0:T(8,128)(2,1)S(1)}, bf16[1,1,2,64,512]{4,3,2,1,0:T(8,128)(2,1)S(1)}, u32[]{:S(2)}, u32[]{:S(2)}) collective-permute-start(bf16[1,1,2,64,512]{4,3,2,1,0:T(8,128)(2,1)S(1)} %get-tuple-element.28), channel_id=1, source_target_pairs={{0,1},{1,0},{2,3},{3,2},{4,5},{5,4},{6,7},{7,6},{8,9},{9,8},{10,11... | collective-permute-start | bytes 393224 | tf_op jit(solution)/shard_map/ppermute | solution.py:255
  48.5 1.5 %collective-permute-start.20 = (bf16[1,1,2,64,512]{4,3,2,1,0:T(8,128)(2,1)S(1)}, bf16[1,1,2,64,512]{4,3,2,1,0:T(8,128)(2,1)S(1)}, u32[]{:S(2)}, u32[]{:S(2)}) collective-permute-start(bf16[1,1,2,64,512]{4,3,2,1,0:T(8,128)(2,1)S(1)} %get-tuple-element.27), channel_id=1, source_target_pairs={{0,1},{1,0},{2,3},{3,2},{4,5},{5,4},{6,7},{7,6},{8,9},{9,8},{10,11... | collective-permute-start | bytes 393224 | tf_op jit(solution)/shard_map/ppermute | solution.py:255

commit v4 on v3

--- a/solution.py
+++ b/solution.py
@@ -116,18 +116,26 @@
         ]
     col = jnp.concatenate(cols, axis=0)
     tiles, tables = [], []
-    for place, piece in zip(places, pieces):
-        height = piece.shape[0]
+    for place, parts in zip(places, pieces):
+        height = sum(part.shape[0] for part in parts)
         first = place
         if isinstance(place, tuple):
             first = (2 * (pair ^ place[0]) + (side ^ place[1])) * height
         tiles.append(one_hot(col, first, height))
-        tables.append(piece[...])
+        tables += [part[...] for part in parts]
     return dot(jnp.concatenate(tiles, axis=1), jnp.concatenate(tables, axis=0))
 
 
-def assemble_kernel(places, source_ref, op_ref, slot_ref, *refs):
-    pieces, out_ref = refs[:-1], refs[-1]
+def grouped(counts, refs):
+    groups = []
+    for count in counts:
+        groups.append(refs[:count])
+        refs = refs[count:]
+    return groups, refs
+
+
+def assemble_kernel(places, counts, source_ref, op_ref, slot_ref, *refs):
+    pieces, (out_ref,) = grouped(counts, refs)
     products, eigen = out_ref.shape[0], out_ref.shape[2]
     total = add_pieces(places, (source_ref, op_ref), slot_ref, pieces, products, eigen)
     total = total.astype(BF16)
@@ -142,14 +150,14 @@
     vmem = pl.BlockSpec(memory_space=pltpu.VMEM)
     smem = pl.BlockSpec(memory_space=pltpu.SMEM)
     return pl.pallas_call(
-        functools.partial(assemble_kernel, places),
-        in_specs=[smem, smem] + [vmem] * (1 + len(pieces)),
+        functools.partial(assemble_kernel, places, [len(group) for group in pieces]),
+        in_specs=[smem, smem] + [vmem] * (1 + sum(len(group) for group in pieces)),
         out_specs=vmem,
         out_shape=jax.ShapeDtypeStruct((products, 2 * eigen, eigen), BF16),
         compiler_params=pltpu.CompilerParams(vmem_limit_bytes=VMEM_LIMIT),
         cost_estimate=pl.CostEstimate(flops=1000, bytes_accessed=1000, transcendentals=0),
         name="assemble",
-    )(source, op_index, slots, *pieces)
+    )(source, op_index, slots, *[part for group in pieces for part in group])
 
 
 def block_rows(parts, k):
@@ -162,14 +170,9 @@
 
 
 def contract_kernel(places, counts, source_ref, op_ref, slot_ref, partial_ref, *refs):
-    n_pieces = len(places)
-    pieces, refs = refs[:n_pieces], refs[n_pieces:]
-    blocks = []
-    for count in counts:
-        blocks.append(refs[:count])
-        refs = refs[count:]
+    groups, (out_ref, right, done, sems) = grouped(counts, refs)
+    pieces, blocks = groups[: len(places)], groups[len(places) :]
     n_cols = len(blocks)
-    out_ref, right, done, sems = refs
     own2, local_cols = blocks[0][0].shape[3:]
     products, eigen = right.shape[0], right.shape[2]
     rows = NS * own2
@@ -227,15 +230,16 @@
 def contract(places, pieces, partial, source, op_index, slots, blocks):
     _, products, _, own2, local_cols = blocks[0][0].shape
     n_cols = len(blocks)
-    parts = [part for block in blocks for part in block]
+    groups = pieces + blocks
+    parts = [part for group in groups for part in group]
     eigen = partial.shape[2]
     order = n_cols * local_cols
     times = order // eigen
     vmem = pl.BlockSpec(memory_space=pltpu.VMEM)
     smem = pl.BlockSpec(memory_space=pltpu.SMEM)
     return pl.pallas_call(
-        functools.partial(contract_kernel, places, [len(block) for block in blocks]),
-        in_specs=[smem, smem] + [vmem] * (2 + len(pieces) + len(parts)),
+        functools.partial(contract_kernel, places, [len(group) for group in groups]),
+        in_specs=[smem, smem] + [vmem] * (2 + len(parts)),
         out_specs=pl.BlockSpec(memory_space=pl.ANY),
         out_shape=jax.ShapeDtypeStruct((products, NS, own2 // 2, 2, order), BF16),
         scratch_shapes=[
@@ -248,7 +252,7 @@
             flops=4 * products * eigen * NS * own2 * order, bytes_accessed=0, transcendentals=0
         ),
         name="contract",
-    )(source, op_index, slots, partial, *pieces, *parts)
+    )(source, op_index, slots, partial, *parts)
 
 
 def swap(array, axis, size, mask):
@@ -277,9 +281,9 @@
         half = whole.shape[0] // 2
         mixed = mix(op_index, listed_rows, sink_ops, peramb, [1] * n_cols)
         blocks = [[mixed[0]]] + [[swap(mixed[j], "col", n_cols, j)] for j in range(1, n_cols)]
-        partial = assemble([0], [whole[:half]], pair_source, op_index, slots, eigen)
+        partial = assemble([0], [[whole[:half]]], pair_source, op_index, slots, eigen)
         return contract(
-            [half], [whole[half:]], partial, pair_source, op_index, slots, blocks
+            [half], [[whole[half:]]], partial, pair_source, op_index, slots, blocks
         )
     half = rows // 2
     own = lax.dynamic_slice_in_dim(op_table, lax.axis_index("col") % 2 * half, half, 0)
@@ -289,11 +293,7 @@
         held[mask, 0] = across(own, mask)
     mixed = mix(op_index, listed_rows, sink_ops, peramb, [1, 1, 2])
     crossed = swap(mixed[2], "col", n_cols, 2)
-    halves = [
-        beside(crossed[1:, k : k + 1, s : s + NS // 2])
-        for k in range(mixed[2].shape[1])
-        for s in (0, NS // 2)
-    ]
+    halves = [beside(crossed[1:, k : k + 1]) for k in range(mixed[2].shape[1])]
     blocks = [[mixed[0]], [beside(mixed[1])], [crossed], halves]
     for mask in (0, 1, 2, 4):
         held[mask, 1] = beside(after(held[mask, 0], mixed[0]))
@@ -301,12 +301,13 @@
     held[6, 0] = across(after(own, mixed[0]), 6)
     held[6, 1] = beside(held[6, 0])
     held[5, 0] = across(after(held[4, 0], held[4, 1], held[3, 0]), 1)
-    held[7, 0] = across(after(held[6, 0], held[6, 1], held[5, 0]), 1)
+    held[7, 0] = across(after(held[6, 0], held[5, 0]), 1)
     for mask in (3, 5):
         held[mask, 1] = beside(held[mask, 0])
     early = [(mask, side) for mask in range(7) for side in (0, 1)]
+    held = {p: pieces if isinstance(pieces, list) else [pieces] for p, pieces in held.items()}
     partial = assemble(early, [held[p] for p in early], pair_source, op_index, slots, eigen)
-    held[7, 1] = beside(after(held[7, 0], partial))
+    held[7, 1] = [beside(after(held[7, 0][0], partial))]
     late = [(7, 0), (7, 1)]
     return contract(
         late, [held[p] for p in late], partial, pair_source, op_index, slots, blocks

time: 54.6 us -> 49.3 us (0.903)
  the two profiles are of different devices: /device:TPU:13 before, /device:TPU:9 now
where the time goes in v4:
time: 49.3 us; the launch traced here: 49.1 us
  waiting for transfers between devices  18.2 us (37%)
  starting transfers between devices  14.5 us (29%)
  Pallas kernels  14 us (28%)
  local copies, waits for them, and re-layouts  1.7 us (3%)
  between operations  0.77 us (2%)
    ppermute x19, waiting for transfers between devices, swap(): return lax.ppermute(array, axis, [(i, i ^ mask) for i in range(size)])  18.2 us
    ppermute x19, starting transfers between devices, swap(): return lax.ppermute(array, axis, [(i, i ^ mask) for i in range(size)])  14.5 us
    pallas_call x1, Pallas kernels, mix(): pl.pallas_call(mix_kernel, in_specs=[pl.BlockSpec(memory_space=pltpu.SMEM...  4.99 us
    pallas_call x1, Pallas kernels, assemble(): pl.pallas_call(functools.partial(assemble_kernel, places, [len(group) for...  4.56 us
    pallas_call x1, Pallas kernels, contract(): pl.pallas_call(functools.partial(contract_kernel, places, [len(group) for...  4.42 us
    slice x1, local copies, waits for them, and re-layouts, per_device(): own = jnp.concatenate([own[:, 0], own[:, 1]], axis=1)  1.61 us
  transfers between devices with their start and end apart: 19, of which 11 were waited for; matrix products, arithmetic and copies ran while one was open for 0% of the time, Pallas kernels for 19%

profile of v4, /device:TPU:9, one launch (start us, length us, event | category | flops | bytes accessed | tf_op | source)
XLA Modules:
  0.0 49.1 jit_solution(14875024794637259948)
XLA Ops:
  0.0 1.6 %constant_dynamic-slice_fusion = (bf16[128,1,512]{2,1,0:T(2,128)(2,1)S(1)}, bf16[128,1,512]{2,1,0:T(2,128)(2,1)S(1)}) fusion(bf16[256,2,512]{2,1,0:T(2,128)(2,1)} %param.9, s32[]{:T(128)S(6)} %select_n.11, s32[]{:T(128)S(6)} %add.9), kind=kLoop, calls=%fused_computation.3 | loop fusion | bytes 524296 | tf_op jit(solution)/shard_map/slice | solution.py:290
  1.7 1.3 %collective-permute-start.1 = (bf16[128,1024]{1,0:T(8,128)(2,1)S(1)}, bf16[128,1024]{1,0:T(8,128)(2,1)S(1)}, u32[]{:S(2)}, u32[]{:S(2)}) collective-permute-start(bf16[128,1024]{1,0:T(8,128)(2,1)S(1)} %pad_maximum_fusion.refs_0_), channel_id=1, source_target_pairs={{0,4},{4,0},{8,12},{12,8},{16,20},{20,16},{24,28},{28,24},{1,5},{5... | collective-permute-start | bytes 786440 | tf_op jit(solution)/shard_map/ppermute | solution.py:259
  3.0 0.2 collective-permute-start.3
  3.2 2.3 %collective-permute-start.7 = (bf16[128,1024]{1,0:T(8,128)(2,1)S(1)}, bf16[128,1024]{1,0:T(8,128)(2,1)S(1)}, u32[]{:S(2)}, u32[]{:S(2)}) collective-permute-start(bf16[128,1024]{1,0:T(8,128)(2,1)S(1)} %pad_maximum_fusion.refs_0_), channel_id=1, source_target_pairs={{0,16},{4,20},{8,24},{12,28},{16,0},{20,4},{24,8},{28,12},{1,17},{... | collective-permute-start | bytes 786440 | tf_op jit(solution)/shard_map/ppermute | solution.py:259
  5.5 5.0 %mix.1 = (bf16[1,2,4,64,512]{4,3,2,1,0:T(8,128)(2,1)S(1)}, bf16[1,2,4,64,512]{4,3,2,1,0:T(8,128)(2,1)S(1)}, bf16[2,2,4,64,512]{4,3,2,1,0:T(8,128)(2,1)S(1)}) custom-call(s32[2,2]{1,0:T(2,128)S(1)} %copy-done.2, s32[2,128]{1,0:T(2,128)S(1)} %copy-done.3, bf16[1,2,2,512,512]{4,3,2,1,0:T(8,128)(2,1)S(1)} %copy-done, bf16[1,2,2048,512]{3,2,1,0:T(8,128)(2,1)} %peramb_ref.1), custom_call_target="tpu_custom_call" | custom-call | flops 1000 | bytes 1000 | tf_op jit(solution)/shard_map/mix/pallas_call | solution.py:88
  10.5 1.3 %collective-permute-start.16 = (bf16[2,2,4,64,512]{4,3,2,1,0:T(8,128)(2,1)S(1)}, bf16[2,2,4,64,512]{4,3,2,1,0:T(8,128)(2,1)S(1)}, u32[]{:S(2)}, u32[]{:S(2)}) collective-permute-start(bf16[2,2,4,64,512]{4,3,2,1,0:T(8,128)(2,1)S(1)} %get-tuple-element.26), channel_id=1, source_target_pairs={{0,2},{1,3},{2,0},{3,1},{4,6},{5,7},{6,4},{7,5},{8,10},{9,11},{10,... | collective-permute-start | bytes 3145736 | tf_op jit(solution)/shard_map/ppermute | solution.py:259
  11.8 1.4 %collective-permute-done.3.refs_4_ = bf16[128,1024]{1,0:T(8,128)(2,1)S(1)} collective-permute-done((bf16[128,1024]{1,0:T(8,128)(2,1)S(1)}, bf16[128,1024]{1,0:T(8,128)(2,1)S(1)}, u32[]{:S(2)}, u32[]{:S(2)}) %collective-permute-start.3) | collective-permute-done | bytes 262176 | tf_op jit(solution)/shard_map/ppermute | solution.py:259
  13.2 0.4 collective-permute-start.5
  13.6 2.9 %collective-permute-done.7.refs_8_ = bf16[128,1024]{1,0:T(8,128)(2,1)S(1)} collective-permute-done((bf16[128,1024]{1,0:T(8,128)(2,1)S(1)}, bf16[128,1024]{1,0:T(8,128)(2,1)S(1)}, u32[]{:S(2)}, u32[]{:S(2)}) %collective-permute-start.7) | collective-permute-done | bytes 262176 | tf_op jit(solution)/shard_map/ppermute | solution.py:259
  16.5 1.9 %collective-permute-start.8 = (bf16[128,1024]{1,0:T(8,128)(2,1)S(1)}, bf16[128,1024]{1,0:T(8,128)(2,1)S(1)}, u32[]{:S(2)}, u32[]{:S(2)}) collective-permute-start(bf16[128,1024]{1,0:T(8,128)(2,1)S(1)} %collective-permute-done.7.refs_8_), channel_id=1, source_target_pairs={{0,1},{1,0},{2,3},{3,2},{4,5},{5,4},{6,7},{7,6},{8,9},{9,8},{10,11... | collective-permute-start | bytes 786440 | tf_op jit(solution)/shard_map/ppermute | solution.py:259
  18.5 0.2 collective-permute-start.11
  18.6 0.4 collective-permute-done.5.refs_6_
  19.0 0.6 %collective-permute-done.8.refs_9_ = bf16[128,1024]{1,0:T(8,128)(2,1)S(1)} collective-permute-done((bf16[128,1024]{1,0:T(8,128)(2,1)S(1)}, bf16[128,1024]{1,0:T(8,128)(2,1)S(1)}, u32[]{:S(2)}, u32[]{:S(2)}) %collective-permute-start.8) | collective-permute-done | bytes 262176 | tf_op jit(solution)/shard_map/ppermute | solution.py:259
  19.6 0.3 collective-permute-start.9
  19.9 2.7 %collective-permute-start = (bf16[128,1024]{1,0:T(8,128)(2,1)S(1)}, bf16[128,1024]{1,0:T(8,128)(2,1)S(1)}, u32[]{:S(2)}, u32[]{:S(2)}) collective-permute-start(bf16[128,1024]{1,0:T(8,128)(2,1)S(1)} %pad_maximum_fusion.refs_0_), channel_id=1, source_target_pairs={{0,1},{1,0},{2,3},{3,2},{4,5},{5,4},{6,7},{7,6},{8,9},{9,8},{10,11... | collective-permute-start | bytes 786440 | tf_op jit(solution)/shard_map/ppermute | solution.py:259
  22.6 9.4 %collective-permute-done.11.refs_12_ = bf16[128,1024]{1,0:T(8,128)(2,1)S(1)} collective-permute-done((bf16[128,1024]{1,0:T(8,128)(2,1)S(1)}, bf16[128,1024]{1,0:T(8,128)(2,1)S(1)}, u32[]{:S(2)}, u32[]{:S(2)}) %collective-permute-start.11) | collective-permute-done | bytes 262176 | tf_op jit(solution)/shard_map/ppermute | solution.py:259
  32.0 0.8 %collective-permute-start.4 = (bf16[128,1024]{1,0:T(8,128)(2,1)S(1)}, bf16[128,1024]{1,0:T(8,128)(2,1)S(1)}, u32[]{:S(2)}, u32[]{:S(2)}) collective-permute-start(bf16[128,1024]{1,0:T(8,128)(2,1)S(1)} %collective-permute-done.3.refs_4_), channel_id=1, source_target_pairs={{0,1},{1,0},{2,3},{3,2},{4,5},{5,4},{6,7},{7,6},{8,9},{9,8},{10,11... | collective-permute-start | bytes 786440 | tf_op jit(solution)/shard_map/ppermute | solution.py:259
  32.8 0.5 %collective-permute-start.6 = (bf16[128,1024]{1,0:T(8,128)(2,1)S(1)}, bf16[128,1024]{1,0:T(8,128)(2,1)S(1)}, u32[]{:S(2)}, u32[]{:S(2)}) collective-permute-start(bf16[128,1024]{1,0:T(8,128)(2,1)S(1)} %collective-permute-done.5.refs_6_), channel_id=1, source_target_pairs={{0,1},{1,0},{2,3},{3,2},{4,5},{5,4},{6,7},{7,6},{8,9},{9,8},{10,11... | collective-permute-start | bytes 786440 | tf_op jit(solution)/shard_map/ppermute | solution.py:259
  33.3 0.1 collective-permute-start.10
  33.4 0.6 %collective-permute-done.4.refs_5_ = bf16[128,1024]{1,0:T(8,128)(2,1)S(1)} collective-permute-done((bf16[128,1024]{1,0:T(8,128)(2,1)S(1)}, bf16[128,1024]{1,0:T(8,128)(2,1)S(1)}, u32[]{:S(2)}, u32[]{:S(2)}) %collective-permute-start.4) | collective-permute-done | bytes 262176 | tf_op jit(solution)/shard_map/ppermute | solution.py:259
  34.0 0.3 collective-permute-start.13
  34.2 0.1 collective-permute-done.12.refs_13_
  34.3 0.5 %collective-permute-start.15 = (bf16[1,2,4,64,512]{4,3,2,1,0:T(8,128)(2,1)S(1)}, bf16[1,2,4,64,512]{4,3,2,1,0:T(8,128)(2,1)S(1)}, u32[]{:S(2)}, u32[]{:S(2)}) collective-permute-start(bf16[1,2,4,64,512]{4,3,2,1,0:T(8,128)(2,1)S(1)} %get-tuple-element.25), channel_id=1, source_target_pairs={{0,1},{1,0},{2,3},{3,2},{4,5},{5,4},{6,7},{7,6},{8,9},{9,8},{10,11... | collective-permute-start | bytes 1572872 | tf_op jit(solution)/shard_map/ppermute | solution.py:259
  35.5 4.6 %assemble.1.partial_ref = bf16[2,1024,512]{2,1,0:T(8,128)(2,1)S(1)} custom-call(s32[1]{0:T(128)S(6)} %copy.14.source_ref, s32[2,2]{1,0:T(2,128)S(1)} %copy-done.2, s32[16,128]{1,0:T(8,128)S(1)} %bitcast.5, bf16[128,1024]{1,0:T(8,128)(2,1)S(1)} %pad_maximum_fusion.refs_0_, bf16[128,1024]{1,0:T(8,128)(2,1)S(1)} %collective-permute-done.refs_1_, ...), custom_call_target="tpu_custom_call" | custom-call | flops 1000 | bytes 1000 | tf_op jit(solution)/shard_map/assemble/pallas_call | solution.py:152
  40.1 1.4 %collective-permute-done.13.refs_0_ = bf16[128,1024]{1,0:T(8,128)(2,1)S(1)} collective-permute-done((bf16[128,1024]{1,0:T(8,128)(2,1)S(1)}, bf16[128,1024]{1,0:T(8,128)(2,1)S(1)}, u32[]{:S(2)}, u32[]{:S(2)}) %collective-permute-start.13) | collective-permute-done | bytes 262176 | tf_op jit(solution)/shard_map/ppermute | solution.py:259
  41.5 1.2 %collective-permute-start.14 = (bf16[128,1024]{1,0:T(8,128)(2,1)S(1)}, bf16[128,1024]{1,0:T(8,128)(2,1)S(1)}, u32[]{:S(2)}, u32[]{:S(2)}) collective-permute-start(bf16[128,1024]{1,0:T(8,128)(2,1)S(1)} %collective-permute-done.13.refs_0_), channel_id=1, source_target_pairs={{0,1},{1,0},{2,3},{3,2},{4,5},{5,4},{6,7},{7,6},{8,9},{9,8},{10,11... | collective-permute-start | bytes 786440 | tf_op jit(solution)/shard_map/ppermute | solution.py:259
  42.7 0.1 collective-permute-start.17
  42.8 0.5 %collective-permute-start.18 = (bf16[1,1,4,64,512]{4,3,2,1,0:T(8,128)(2,1)S(1)}, bf16[1,1,4,64,512]{4,3,2,1,0:T(8,128)(2,1)S(1)}, u32[]{:S(2)}, u32[]{:S(2)}) collective-permute-start(bf16[1,1,4,64,512]{4,3,2,1,0:T(8,128)(2,1)S(1)} %get-tuple-element.27), channel_id=1, source_target_pairs={{0,1},{1,0},{2,3},{3,2},{4,5},{5,4},{6,7},{7,6},{8,9},{9,8},{10,11... | collective-permute-start | bytes 786440 | tf_op jit(solution)/shard_map/ppermute | solution.py:259
  43.3 0.5 %collective-permute-done.14.refs_1_ = bf16[128,1024]{1,0:T(8,128)(2,1)S(1)} collective-permute-done((bf16[128,1024]{1,0:T(8,128)(2,1)S(1)}, bf16[128,1024]{1,0:T(8,128)(2,1)S(1)}, u32[]{:S(2)}, u32[]{:S(2)}) %collective-permute-start.14) | collective-permute-done | bytes 262176 | tf_op jit(solution)/shard_map/ppermute | solution.py:259
  43.8 0.5 collective-permute-done.17.refs_5_
  44.3 0.4 collective-permute-done.18.refs_6_
  44.7 4.4 %contract.1 = bf16[2,4,32,2,2048]{4,3,2,1,0:T(2,128)(2,1)} custom-call(s32[1]{0:T(128)S(6)} %copy.14.source_ref, s32[2,2]{1,0:T(2,128)S(1)} %copy-done.2, s32[16,128]{1,0:T(8,128)S(1)} %bitcast.6, bf16[2,1024,512]{2,1,0:T(8,128)(2,1)S(1)} %assemble.1.partial_ref, bf16[128,1024]{1,0:T(8,128)(2,1)S(1)} %collective-permute-done.13.refs_0_, ...), custom_call_target="tpu_custom_call" | custom-call | flops 2147483648 | tf_op jit(solution)/shard_map/contract/pallas_call | solution.py:240
  (21 shorter events, 0.1 us)
Async XLA Ops:
  0.0 5.5 %copy-start.2 = (s32[2,2]{1,0:T(2,128)S(1)}, s32[2,2]{1,0:T(2,128)}, u32[]{:S(2)}) copy-start(s32[2,2]{1,0:T(2,128)} %op_ref.5) | copy-start | bytes 52
  0.0 5.5 %copy-start.3 = (s32[2,128]{1,0:T(2,128)S(1)}, s32[2,128]{1,0:T(2,128)}, u32[]{:S(2)}) copy-start(s32[2,128]{1,0:T(2,128)} %listed_ref.1) | copy-start | bytes 3076
  0.0 5.5 %copy-start = (bf16[1,2,2,512,512]{4,3,2,1,0:T(8,128)(2,1)S(1)}, bf16[1,2,2,512,512]{4,3,2,1,0:T(8,128)(2,1)}, u32[]{:S(2)}) copy-start(bf16[1,2,2,512,512]{4,3,2,1,0:T(8,128)(2,1)} %sink_ref.1) | copy-start | bytes 6291460
  1.7 33.8 %copy-start.1 = (s32[2048]{0:T(1024)S(1)}, s32[2048]{0:T(1024)}, u32[]{:S(2)}) copy-start(s32[2048]{0:T(1024)} %param.10) | copy-start | bytes 24580
  1.7 10.1 %collective-permute-start.1 = (bf16[128,1024]{1,0:T(8,128)(2,1)S(1)}, bf16[128,1024]{1,0:T(8,128)(2,1)S(1)}, u32[]{:S(2)}, u32[]{:S(2)}) collective-permute-start(bf16[128,1024]{1,0:T(8,128)(2,1)S(1)} %pad_maximum_fusion.refs_0_), channel_id=1, source_target_pairs={{0,4},{4,0},{8,12},{12,8},{16,20},{20,16},{24,28},{28,24},{1,5},{5... | collective-permute-start | bytes 786440 | tf_op jit(solution)/shard_map/ppermute | solution.py:259
  3.0 10.2 %collective-permute-start.3 = (bf16[128,1024]{1,0:T(8,128)(2,1)S(1)}, bf16[128,1024]{1,0:T(8,128)(2,1)S(1)}, u32[]{:S(2)}, u32[]{:S(2)}) collective-permute-start(bf16[128,1024]{1,0:T(8,128)(2,1)S(1)} %pad_maximum_fusion.refs_0_), channel_id=1, source_target_pairs={{0,8},{4,12},{8,0},{12,4},{16,24},{20,28},{24,16},{28,20},{1,9},{5... | collective-permute-start | bytes 786440 | tf_op jit(solution)/shard_map/ppermute | solution.py:259
  3.2 13.4 %collective-permute-start.7 = (bf16[128,1024]{1,0:T(8,128)(2,1)S(1)}, bf16[128,1024]{1,0:T(8,128)(2,1)S(1)}, u32[]{:S(2)}, u32[]{:S(2)}) collective-permute-start(bf16[128,1024]{1,0:T(8,128)(2,1)S(1)} %pad_maximum_fusion.refs_0_), channel_id=1, source_target_pairs={{0,16},{4,20},{8,24},{12,28},{16,0},{20,4},{24,8},{28,12},{1,17},{... | collective-permute-start | bytes 786440 | tf_op jit(solution)/shard_map/ppermute | solution.py:259
  10.5 32.2 %collective-permute-start.16 = (bf16[2,2,4,64,512]{4,3,2,1,0:T(8,128)(2,1)S(1)}, bf16[2,2,4,64,512]{4,3,2,1,0:T(8,128)(2,1)S(1)}, u32[]{:S(2)}, u32[]{:S(2)}) collective-permute-start(bf16[2,2,4,64,512]{4,3,2,1,0:T(8,128)(2,1)S(1)} %get-tuple-element.26), channel_id=1, source_target_pairs={{0,2},{1,3},{2,0},{3,1},{4,6},{5,7},{6,4},{7,5},{8,10},{9,11},{10,... | collective-permute-start | bytes 3145736 | tf_op jit(solution)/shard_map/ppermute | solution.py:259
  13.2 5.8 %collective-permute-start.5 = (bf16[128,1024]{1,0:T(8,128)(2,1)S(1)}, bf16[128,1024]{1,0:T(8,128)(2,1)S(1)}, u32[]{:S(2)}, u32[]{:S(2)}) collective-permute-start(bf16[128,1024]{1,0:T(8,128)(2,1)S(1)} %collective-permute-done.3.refs_4_), channel_id=1, source_target_pairs={{0,4},{4,0},{8,12},{12,8},{16,20},{20,16},{24,28},{28,24},{1,5},{5... | collective-permute-start | bytes 786440 | tf_op jit(solution)/shard_map/ppermute | solution.py:259
  16.5 3.1 %collective-permute-start.8 = (bf16[128,1024]{1,0:T(8,128)(2,1)S(1)}, bf16[128,1024]{1,0:T(8,128)(2,1)S(1)}, u32[]{:S(2)}, u32[]{:S(2)}) collective-permute-start(bf16[128,1024]{1,0:T(8,128)(2,1)S(1)} %collective-permute-done.7.refs_8_), channel_id=1, source_target_pairs={{0,1},{1,0},{2,3},{3,2},{4,5},{5,4},{6,7},{7,6},{8,9},{9,8},{10,11... | collective-permute-start | bytes 786440 | tf_op jit(solution)/shard_map/ppermute | solution.py:259
  18.5 13.6 %collective-permute-start.11 = (bf16[128,1024]{1,0:T(8,128)(2,1)S(1)}, bf16[128,1024]{1,0:T(8,128)(2,1)S(1)}, u32[]{:S(2)}, u32[]{:S(2)}) collective-permute-start(bf16[128,1024]{1,0:T(8,128)(2,1)S(1)} %pad_maximum_fusion.refs_0_), channel_id=1, source_target_pairs={{0,24},{4,28},{8,16},{12,20},{16,8},{20,12},{24,0},{28,4},{1,25},{... | collective-permute-start | bytes 786440 | tf_op jit(solution)/shard_map/ppermute | solution.py:259
  19.6 13.2 %collective-permute-start.9 = (bf16[128,1024]{1,0:T(8,128)(2,1)S(1)}, bf16[128,1024]{1,0:T(8,128)(2,1)S(1)}, u32[]{:S(2)}, u32[]{:S(2)}) collective-permute-start(bf16[128,1024]{1,0:T(8,128)(2,1)S(1)} %collective-permute-done.7.refs_8_), channel_id=1, source_target_pairs={{0,4},{4,0},{8,12},{12,8},{16,20},{20,16},{24,28},{28,24},{1,5},{5... | collective-permute-start | bytes 786440 | tf_op jit(solution)/shard_map/ppermute | solution.py:259
  19.9 12.9 %collective-permute-start = (bf16[128,1024]{1,0:T(8,128)(2,1)S(1)}, bf16[128,1024]{1,0:T(8,128)(2,1)S(1)}, u32[]{:S(2)}, u32[]{:S(2)}) collective-permute-start(bf16[128,1024]{1,0:T(8,128)(2,1)S(1)} %pad_maximum_fusion.refs_0_), channel_id=1, source_target_pairs={{0,1},{1,0},{2,3},{3,2},{4,5},{5,4},{6,7},{7,6},{8,9},{9,8},{10,11... | collective-permute-start | bytes 786440 | tf_op jit(solution)/shard_map/ppermute | solution.py:259
  22.6 10.7 %collective-permute-start.2 = (bf16[128,1024]{1,0:T(8,128)(2,1)S(1)}, bf16[128,1024]{1,0:T(8,128)(2,1)S(1)}, u32[]{:S(2)}, u32[]{:S(2)}) collective-permute-start(bf16[128,1024]{1,0:T(8,128)(2,1)S(1)} %collective-permute-done.1.refs_2_), channel_id=1, source_target_pairs={{0,1},{1,0},{2,3},{3,2},{4,5},{5,4},{6,7},{7,6},{8,9},{9,8},{10,11... | collective-permute-start | bytes 786440 | tf_op jit(solution)/shard_map/ppermute | solution.py:259
  32.0 1.9 %collective-permute-start.4 = (bf16[128,1024]{1,0:T(8,128)(2,1)S(1)}, bf16[128,1024]{1,0:T(8,128)(2,1)S(1)}, u32[]{:S(2)}, u32[]{:S(2)}) collective-permute-start(bf16[128,1024]{1,0:T(8,128)(2,1)S(1)} %collective-permute-done.3.refs_4_), channel_id=1, source_target_pairs={{0,1},{1,0},{2,3},{3,2},{4,5},{5,4},{6,7},{7,6},{8,9},{9,8},{10,11... | collective-permute-start | bytes 786440 | tf_op jit(solution)/shard_map/ppermute | solution.py:259
  32.8 1.5 %collective-permute-start.12 = (bf16[128,1024]{1,0:T(8,128)(2,1)S(1)}, bf16[128,1024]{1,0:T(8,128)(2,1)S(1)}, u32[]{:S(2)}, u32[]{:S(2)}) collective-permute-start(bf16[128,1024]{1,0:T(8,128)(2,1)S(1)} %collective-permute-done.11.refs_12_), channel_id=1, source_target_pairs={{0,1},{1,0},{2,3},{3,2},{4,5},{5,4},{6,7},{7,6},{8,9},{9,8},{10,11... | collective-permute-start | bytes 786440 | tf_op jit(solution)/shard_map/ppermute | solution.py:259
  32.8 2.7 %collective-permute-start.6 = (bf16[128,1024]{1,0:T(8,128)(2,1)S(1)}, bf16[128,1024]{1,0:T(8,128)(2,1)S(1)}, u32[]{:S(2)}, u32[]{:S(2)}) collective-permute-start(bf16[128,1024]{1,0:T(8,128)(2,1)S(1)} %collective-permute-done.5.refs_6_), channel_id=1, source_target_pairs={{0,1},{1,0},{2,3},{3,2},{4,5},{5,4},{6,7},{7,6},{8,9},{9,8},{10,11... | collective-permute-start | bytes 786440 | tf_op jit(solution)/shard_map/ppermute | solution.py:259
  33.3 2.2 %collective-permute-start.10 = (bf16[128,1024]{1,0:T(8,128)(2,1)S(1)}, bf16[128,1024]{1,0:T(8,128)(2,1)S(1)}, u32[]{:S(2)}, u32[]{:S(2)}) collective-permute-start(bf16[128,1024]{1,0:T(8,128)(2,1)S(1)} %collective-permute-done.9.refs_10_), channel_id=1, source_target_pairs={{0,1},{1,0},{2,3},{3,2},{4,5},{5,4},{6,7},{7,6},{8,9},{9,8},{10,11... | collective-permute-start | bytes 786440 | tf_op jit(solution)/shard_map/ppermute | solution.py:259
  34.0 7.5 %collective-permute-start.13 = (bf16[128,1024]{1,0:T(8,128)(2,1)S(1)}, bf16[128,1024]{1,0:T(8,128)(2,1)S(1)}, u32[]{:S(2)}, u32[]{:S(2)}) collective-permute-start(bf16[128,1024]{1,0:T(8,128)(2,1)S(1)} %collective-permute-done.11.refs_12_), channel_id=1, source_target_pairs={{0,4},{4,0},{8,12},{12,8},{16,20},{20,16},{24,28},{28,24},{1,5},{5... | collective-permute-start | bytes 786440 | tf_op jit(solution)/shard_map/ppermute | solution.py:259
  34.3 9.0 %collective-permute-start.15 = (bf16[1,2,4,64,512]{4,3,2,1,0:T(8,128)(2,1)S(1)}, bf16[1,2,4,64,512]{4,3,2,1,0:T(8,128)(2,1)S(1)}, u32[]{:S(2)}, u32[]{:S(2)}) collective-permute-start(bf16[1,2,4,64,512]{4,3,2,1,0:T(8,128)(2,1)S(1)} %get-tuple-element.25), channel_id=1, source_target_pairs={{0,1},{1,0},{2,3},{3,2},{4,5},{5,4},{6,7},{7,6},{8,9},{9,8},{10,11... | collective-permute-start | bytes 1572872 | tf_op jit(solution)/shard_map/ppermute | solution.py:259
  41.5 2.4 %collective-permute-start.14 = (bf16[128,1024]{1,0:T(8,128)(2,1)S(1)}, bf16[128,1024]{1,0:T(8,128)(2,1)S(1)}, u32[]{:S(2)}, u32[]{:S(2)}) collective-permute-start(bf16[128,1024]{1,0:T(8,128)(2,1)S(1)} %collective-permute-done.13.refs_0_), channel_id=1, source_target_pairs={{0,1},{1,0},{2,3},{3,2},{4,5},{5,4},{6,7},{7,6},{8,9},{9,8},{10,11... | collective-permute-start | bytes 786440 | tf_op jit(solution)/shard_map/ppermute | solution.py:259
  42.7 1.6 %collective-permute-start.17 = (bf16[1,1,4,64,512]{4,3,2,1,0:T(8,128)(2,1)S(1)}, bf16[1,1,4,64,512]{4,3,2,1,0:T(8,128)(2,1)S(1)}, u32[]{:S(2)}, u32[]{:S(2)}) collective-permute-start(bf16[1,1,4,64,512]{4,3,2,1,0:T(8,128)(2,1)S(1)} %get-tuple-element.28), channel_id=1, source_target_pairs={{0,1},{1,0},{2,3},{3,2},{4,5},{5,4},{6,7},{7,6},{8,9},{9,8},{10,11... | collective-permute-start | bytes 786440 | tf_op jit(solution)/shard_map/ppermute | solution.py:259
  42.8 1.9 %collective-permute-start.18 = (bf16[1,1,4,64,512]{4,3,2,1,0:T(8,128)(2,1)S(1)}, bf16[1,1,4,64,512]{4,3,2,1,0:T(8,128)(2,1)S(1)}, u32[]{:S(2)}, u32[]{:S(2)}) collective-permute-start(bf16[1,1,4,64,512]{4,3,2,1,0:T(8,128)(2,1)S(1)} %get-tuple-element.27), channel_id=1, source_target_pairs={{0,1},{1,0},{2,3},{3,2},{4,5},{5,4},{6,7},{7,6},{8,9},{9,8},{10,11... | collective-permute-start | bytes 786440 | tf_op jit(solution)/shard_map/ppermute | solution.py:259

commit v5 on v4

--- a/solution.py
+++ b/solution.py
@@ -109,7 +109,7 @@
     nops = slot_ref.shape[0] // blocks // 2
     pair, side = lax.axis_index("tpair"), lax.axis_index("col") % 2
     cols = []
-    for k in range(products):
+    for k in products:
         op = source_ref[0] * nops + op_ref[k, 1]
         cols += [
             column(slot_ref[pl.ds(op * blocks + b, 1), :]) for b in range(blocks)
@@ -137,7 +137,7 @@
 def assemble_kernel(places, counts, source_ref, op_ref, slot_ref, *refs):
     pieces, (out_ref,) = grouped(counts, refs)
     products, eigen = out_ref.shape[0], out_ref.shape[2]
-    total = add_pieces(places, (source_ref, op_ref), slot_ref, pieces, products, eigen)
+    total = add_pieces(places, (source_ref, op_ref), slot_ref, pieces, range(products), eigen)
     total = total.astype(BF16)
     for k in range(products):
         rows = slice(k * eigen, (k + 1) * eigen)
@@ -169,90 +169,129 @@
     return jnp.concatenate([f.reshape(-1, f.shape[-1]) for f in found], axis=0)
 
 
-def contract_kernel(places, counts, source_ref, op_ref, slot_ref, partial_ref, *refs):
-    groups, (out_ref, right, done, sems) = grouped(counts, refs)
-    pieces, blocks = groups[: len(places)], groups[len(places) :]
-    n_cols = len(blocks)
-    own2, local_cols = blocks[0][0].shape[3:]
-    products, eigen = right.shape[0], right.shape[2]
-    rows = NS * own2
-    total = add_pieces(places, (source_ref, op_ref), slot_ref, pieces, products, eigen)
-    total = total.astype(BF16)
-    for p in range(products):
-        some = slice(p * eigen, (p + 1) * eigen)
-        right[p, :eigen] = partial_ref[p, :eigen] + total[some, :eigen]
-        right[p, eigen:] = partial_ref[p, eigen:] + total[some, eigen:]
+def times_right(blocks, masks, right, k):
+    eigen = right.shape[2]
+    local_cols = blocks[0][0].shape[4]
     me = lax.axis_index("col")
     per_time = eigen // local_cols
-    times = n_cols // per_time
+    direct = [block_rows(parts, k) for parts in blocks]
+    rows = direct[0].shape[0]
     odd = iota((rows, local_cols), 0) % 2 == 1
+    turned = []
+    for x in direct:
+        wide = x.astype(F32)
+        y = jnp.where(odd, pltpu.roll(wide, 1, 0), -pltpu.roll(wide, rows - 1, 0))
+        turned.append(y.astype(BF16))
+    if per_time == 1:
+        lhs = jnp.concatenate(
+            [jnp.concatenate(direct, axis=0), jnp.concatenate(turned, axis=0)], axis=1
+        )
+        whole = dot(lhs, right[k]).astype(BF16)
+        results = [whole[n * rows : (n + 1) * rows] for n in range(len(masks))]
+    else:
+        results = []
+        for n, mask in enumerate(masks):
+            first = pl.multiple_of(((me ^ mask) % per_time) * local_cols, local_cols)
+            second = pl.multiple_of(eigen + first, local_cols)
+            part = dot(direct[n], right[k, pl.ds(first, local_cols), :])
+            part += dot(turned[n], right[k, pl.ds(second, local_cols), :])
+            if n % per_time:
+                results[-1] += part
+            else:
+                results.append(part)
+        results = [result.astype(BF16) for result in results]
+    times = [(me ^ mask) // per_time for mask in masks[::per_time]]
+    return list(zip(times, results))
+
+
+def near_kernel(places, masks, counts, source_ref, op_ref, slot_ref, partial_ref, *refs):
+    groups, (right, done) = grouped(counts, refs)
+    pieces, blocks = groups[: len(places)], groups[len(places) :]
+    products, eigen = right.shape[0], right.shape[2]
+    scalars = (source_ref, op_ref)
+    for k in range(products):
+        total = add_pieces(places, scalars, slot_ref, pieces, [k], eigen).astype(BF16)
+        right[k, :eigen] = partial_ref[k, :eigen] + total[:, :eigen]
+        right[k, eigen:] = partial_ref[k, eigen:] + total[:, eigen:]
+    for k in range(products):
+        for n, (_, result) in enumerate(times_right(blocks, masks, right, k)):
+            done[k, n] = result.reshape(done.shape[2:])
+
+
+def far_kernel(near_masks, masks, counts, right, near_ref, *refs):
+    blocks, (out_ref, done, near_sems, sems) = grouped(counts, refs)
+    products, eigen = right.shape[0], right.shape[2]
+    near_times, times = near_ref.shape[1], done.shape[1]
+    per_time = len(masks) // times
+    me = lax.axis_index("col")
+
+    def send(source, k, time, sem):
+        at = pl.multiple_of(time * eigen, eigen)
+        copy = pltpu.make_async_copy(source, out_ref.at[k, :, :, :, pl.ds(at, eigen)], sem)
+        copy.start()
+        return copy
+
     copies = []
     for k in range(products):
-        direct, turned = [], []
-        for j in range(n_cols):
-            x = block_rows(blocks[j], k)
-            wide = x.astype(F32)
-            y = jnp.where(odd, pltpu.roll(wide, 1, 0), -pltpu.roll(wide, rows - 1, 0))
-            direct.append(x)
-            turned.append(y.astype(BF16))
-        if per_time == 1:
-            lhs = jnp.concatenate(
-                [jnp.concatenate(direct, axis=0), jnp.concatenate(turned, axis=0)], axis=1
-            )
-            result = dot(lhs, right[k])
-        else:
-            result = []
-            for j in range(n_cols):
-                first = pl.multiple_of(((me ^ j) % per_time) * local_cols, local_cols)
-                second = pl.multiple_of(eigen + first, local_cols)
-                part = dot(direct[j], right[k, pl.ds(first, local_cols), :])
-                part += dot(turned[j], right[k, pl.ds(second, local_cols), :])
-                if j % per_time:
-                    result[-1] += part
-                else:
-                    result.append(part)
-            result = jnp.concatenate(result, axis=0)
-        result = result.astype(BF16)
-        for g in range(times):
-            slot = k * times + g
-            block = result[g * rows : (g + 1) * rows]
-            done[slot] = block.reshape(NS, own2 // 2, 2, eigen)
-            at = pl.multiple_of(((me ^ (g * per_time)) // per_time) * eigen, eigen)
-            copy = pltpu.make_async_copy(
-                done.at[slot], out_ref.at[k, :, :, :, pl.ds(at, eigen)], sems.at[slot]
-            )
-            copy.start()
-            copies.append(copy)
+        for n in range(near_times):
+            time = (me ^ near_masks[n * per_time]) // per_time
+            copies.append(send(near_ref.at[k, n], k, time, near_sems.at[k, n]))
+    for k in range(products):
+        for n, (time, result) in enumerate(times_right(blocks, masks, right, k)):
+            done[k, n] = result.reshape(done.shape[2:])
+            copies.append(send(done.at[k, n], k, time, sems.at[k, n]))
     for copy in copies:
         copy.wait()
+
+
+def flat(groups):
+    return [part for group in groups for part in group]
 
 
 def contract(places, pieces, partial, source, op_index, slots, blocks):
     _, products, _, own2, local_cols = blocks[0][0].shape
     n_cols = len(blocks)
-    groups = pieces + blocks
-    parts = [part for group in groups for part in group]
     eigen = partial.shape[2]
-    order = n_cols * local_cols
-    times = order // eigen
+    times = n_cols * local_cols // eigen
+    near = n_cols // 2
+    near_masks, far_masks = list(range(near)), list(range(near, n_cols))
     vmem = pl.BlockSpec(memory_space=pltpu.VMEM)
     smem = pl.BlockSpec(memory_space=pltpu.SMEM)
+    params = pltpu.CompilerParams(vmem_limit_bytes=VMEM_LIMIT)
+    cost = pl.CostEstimate(
+        flops=2 * products * eigen * NS * own2 * n_cols * local_cols,
+        bytes_accessed=1000,
+        transcendentals=0,
+    )
+    half = (products, times // 2, NS, own2 // 2, 2, eigen)
+    groups = pieces + blocks[:near]
+    right, done = pl.pallas_call(
+        functools.partial(near_kernel, places, near_masks, [len(g) for g in groups]),
+        in_specs=[smem, smem] + [vmem] * (2 + len(flat(groups))),
+        out_specs=[vmem, vmem],
+        out_shape=[
+            jax.ShapeDtypeStruct((products, 2 * eigen, eigen), BF16),
+            jax.ShapeDtypeStruct(half, BF16),
+        ],
+        compiler_params=params,
+        cost_estimate=cost,
+        name="near",
+    )(source, op_index, slots, partial, *flat(groups))
+    groups = blocks[near:]
     return pl.pallas_call(
-        functools.partial(contract_kernel, places, [len(group) for group in groups]),
-        in_specs=[smem, smem] + [vmem] * (2 + len(parts)),
+        functools.partial(far_kernel, near_masks, far_masks, [len(g) for g in groups]),
+        in_specs=[vmem] * (2 + len(flat(groups))),
         out_specs=pl.BlockSpec(memory_space=pl.ANY),
-        out_shape=jax.ShapeDtypeStruct((products, NS, own2 // 2, 2, order), BF16),
+        out_shape=jax.ShapeDtypeStruct((products, NS, own2 // 2, 2, times * eigen), BF16),
         scratch_shapes=[
-            pltpu.VMEM((products, 2 * eigen, eigen), BF16),
-            pltpu.VMEM((products * times, NS, own2 // 2, 2, eigen), BF16),
-            pltpu.SemaphoreType.DMA((products * times,)),
+            pltpu.VMEM(half, BF16),
+            pltpu.SemaphoreType.DMA(half[:2]),
+            pltpu.SemaphoreType.DMA(half[:2]),
         ],
-        compiler_params=pltpu.CompilerParams(vmem_limit_bytes=VMEM_LIMIT),
-        cost_estimate=pl.CostEstimate(
-            flops=4 * products * eigen * NS * own2 * order, bytes_accessed=0, transcendentals=0
-        ),
-        name="contract",
-    )(source, op_index, slots, partial, *parts)
+        compiler_params=params,
+        cost_estimate=cost,
+        name="far",
+    )(right, done, *flat(groups))
 
 
 def swap(array, axis, size, mask):
@@ -288,19 +327,23 @@
     half = rows // 2
     own = lax.dynamic_slice_in_dim(op_table, lax.axis_index("col") % 2 * half, half, 0)
     own = jnp.concatenate([own[:, 0], own[:, 1]], axis=1)
-    held = {(0, 0): own}
-    for mask in (4, 2, 1):
+    held = {(0, 0): own, (0, 1): beside(own)}
+    for mask in (2, 4):
         held[mask, 0] = across(own, mask)
+    held[1, 0] = across(after(own, held[0, 1]), 1)
     mixed = mix(op_index, listed_rows, sink_ops, peramb, [1, 1, 2])
     crossed = swap(mixed[2], "col", n_cols, 2)
     halves = [beside(crossed[1:, k : k + 1]) for k in range(mixed[2].shape[1])]
-    blocks = [[mixed[0]], [beside(mixed[1])], [crossed], halves]
-    for mask in (0, 1, 2, 4):
+    beside_me = beside(mixed[1])
+    blocks = [[mixed[0]], [beside_me], [crossed], halves]
+    for mask in (1, 2, 4):
         held[mask, 1] = beside(after(held[mask, 0], mixed[0]))
     held[3, 0] = across(after(held[2, 0], mixed[0], held[1, 0]), 1)
     held[6, 0] = across(after(own, mixed[0]), 6)
     held[6, 1] = beside(held[6, 0])
-    held[5, 0] = across(after(held[4, 0], held[4, 1], held[3, 0]), 1)
+    held[5, 0] = across(
+        after(held[4, 0], held[4, 1], held[3, 0], held[1, 1], beside_me), 1
+    )
     held[7, 0] = across(after(held[6, 0], held[5, 0]), 1)
     for mask in (3, 5):
         held[mask, 1] = beside(held[mask, 0])

time: 49.3 us -> 49.8 us (1.010)
  the two profiles are of different devices: /device:TPU:9 before, /device:TPU:0 now
where the time goes in v5:
time: 49.8 us; the launch traced here: 49.6 us
  starting transfers between devices  18.7 us (38%)
  waiting for transfers between devices  14.3 us (29%)
  Pallas kernels  14.1 us (28%)
  local copies, waits for them, and re-layouts  1.69 us (3%)
  between operations  0.78 us (2%)
    ppermute x19, starting transfers between devices, swap(): return lax.ppermute(array, axis, [(i, i ^ mask) for i in range(size)])  18.7 us
    ppermute x19, waiting for transfers between devices, swap(): return lax.ppermute(array, axis, [(i, i ^ mask) for i in range(size)])  14.3 us
    pallas_call x1, Pallas kernels, mix(): pl.pallas_call(mix_kernel, in_specs=[pl.BlockSpec(memory_space=pltpu.SMEM...  4.99 us
    pallas_call x1, Pallas kernels, assemble(): pl.pallas_call(functools.partial(assemble_kernel, places, [len(group) for...  4.57 us
    pallas_call x1, Pallas kernels, contract(): pl.pallas_call(functools.partial(near_kernel, places, near_masks, [len(g)...  2.44 us
    pallas_call x1, Pallas kernels, contract(): pl.pallas_call(functools.partial(far_kernel, near_masks, far_masks, [len(...  2.12 us
    slice x1, local copies, waits for them, and re-layouts, per_device(): own = jnp.concatenate([own[:, 0], own[:, 1]], axis=1)  1.6 us
  transfers between devices with their start and end apart: 19, of which 6 were waited for; matrix products, arithmetic and copies ran while one was open for 0% of the time, Pallas kernels for 24%

profile of v5, /device:TPU:0, one launch (start us, length us, event | category | flops | bytes accessed | tf_op | source)
XLA Modules:
  0.0 49.6 jit_solution(6647724398785035067)
XLA Ops:
  0.0 1.6 %constant_dynamic-slice_fusion = (bf16[128,1,512]{2,1,0:T(2,128)(2,1)S(1)}, bf16[128,1,512]{2,1,0:T(2,128)(2,1)S(1)}) fusion(bf16[256,2,512]{2,1,0:T(2,128)(2,1)} %param.9, s32[]{:T(128)S(6)} %select_n.11, s32[]{:T(128)S(6)} %add.9), kind=kLoop, calls=%fused_computation.3 | loop fusion | bytes 524296 | tf_op jit(solution)/shard_map/slice | solution.py:329
  1.7 0.0 copy-start.1
  1.7 0.5 %collective-permute-start = (bf16[128,1024]{1,0:T(8,128)(2,1)S(1)}, bf16[128,1024]{1,0:T(8,128)(2,1)S(1)}, u32[]{:S(2)}, u32[]{:S(2)}) collective-permute-start(bf16[128,1024]{1,0:T(8,128)(2,1)S(1)} %pad_maximum_fusion.refs_0_), channel_id=1, source_target_pairs={{0,1},{1,0},{2,3},{3,2},{4,5},{5,4},{6,7},{7,6},{8,9},{9,8},{10,11... | collective-permute-start | bytes 786440 | tf_op jit(solution)/shard_map/ppermute | solution.py:298
  2.2 3.7 %collective-permute-start.7 = (bf16[128,1024]{1,0:T(8,128)(2,1)S(1)}, bf16[128,1024]{1,0:T(8,128)(2,1)S(1)}, u32[]{:S(2)}, u32[]{:S(2)}) collective-permute-start(bf16[128,1024]{1,0:T(8,128)(2,1)S(1)} %pad_maximum_fusion.refs_0_), channel_id=1, source_target_pairs={{0,16},{4,20},{8,24},{12,28},{16,0},{20,4},{24,8},{28,12},{1,17},{... | collective-permute-start | bytes 786440 | tf_op jit(solution)/shard_map/ppermute | solution.py:298
  5.9 1.6 %collective-permute-start.3 = (bf16[128,1024]{1,0:T(8,128)(2,1)S(1)}, bf16[128,1024]{1,0:T(8,128)(2,1)S(1)}, u32[]{:S(2)}, u32[]{:S(2)}) collective-permute-start(bf16[128,1024]{1,0:T(8,128)(2,1)S(1)} %pad_maximum_fusion.refs_0_), channel_id=1, source_target_pairs={{0,8},{4,12},{8,0},{12,4},{16,24},{20,28},{24,16},{28,20},{1,9},{5... | collective-permute-start | bytes 786440 | tf_op jit(solution)/shard_map/ppermute | solution.py:298
  7.5 0.0 collective-permute-done.refs_1_
  7.5 1.5 %collective-permute-start.1 = (bf16[128,1024]{1,0:T(8,128)(2,1)S(1)}, bf16[128,1024]{1,0:T(8,128)(2,1)S(1)}, u32[]{:S(2)}, u32[]{:S(2)}) collective-permute-start(bf16[128,1024]{1,0:T(8,128)(2,1)S(1)} %pad_maximum_fusion.refs_0_), channel_id=1, source_target_pairs={{0,4},{4,0},{8,12},{12,8},{16,20},{20,16},{24,28},{28,24},{1,5},{5... | collective-permute-start | bytes 786440 | tf_op jit(solution)/shard_map/ppermute | solution.py:298
  9.0 5.0 %mix.1 = (bf16[1,2,4,64,512]{4,3,2,1,0:T(8,128)(2,1)S(1)}, bf16[1,2,4,64,512]{4,3,2,1,0:T(8,128)(2,1)S(1)}, bf16[2,2,4,64,512]{4,3,2,1,0:T(8,128)(2,1)S(1)}) custom-call(s32[2,2]{1,0:T(2,128)S(1)} %copy-done.2, s32[2,128]{1,0:T(2,128)S(1)} %copy-done.3, bf16[1,2,2,512,512]{4,3,2,1,0:T(8,128)(2,1)S(1)} %copy-done, bf16[1,2,2048,512]{3,2,1,0:T(8,128)(2,1)} %peramb_ref.1), custom_call_target="tpu_custom_call" | custom-call | flops 1000 | bytes 1000 | tf_op jit(solution)/shard_map/mix/pallas_call | solution.py:88
  14.0 0.1 collective-permute-start.9
  14.1 1.6 %collective-permute-start.16 = (bf16[2,2,4,64,512]{4,3,2,1,0:T(8,128)(2,1)S(1)}, bf16[2,2,4,64,512]{4,3,2,1,0:T(8,128)(2,1)S(1)}, u32[]{:S(2)}, u32[]{:S(2)}) collective-permute-start(bf16[2,2,4,64,512]{4,3,2,1,0:T(8,128)(2,1)S(1)} %get-tuple-element.32), channel_id=1, source_target_pairs={{0,2},{1,3},{2,0},{3,1},{4,6},{5,7},{6,4},{7,5},{8,10},{9,11},{10,... | collective-permute-start | bytes 3145736 | tf_op jit(solution)/shard_map/ppermute | solution.py:298
  15.7 2.9 %collective-permute-done.7.refs_8_ = bf16[128,1024]{1,0:T(8,128)(2,1)S(1)} collective-permute-done((bf16[128,1024]{1,0:T(8,128)(2,1)S(1)}, bf16[128,1024]{1,0:T(8,128)(2,1)S(1)}, u32[]{:S(2)}, u32[]{:S(2)}) %collective-permute-start.7) | collective-permute-done | bytes 262176 | tf_op jit(solution)/shard_map/ppermute | solution.py:298
  18.5 0.0 collective-permute-done.1.refs_2_
  18.5 0.5 %collective-permute-start.2 = (bf16[128,1024]{1,0:T(8,128)(2,1)S(1)}, bf16[128,1024]{1,0:T(8,128)(2,1)S(1)}, u32[]{:S(2)}, u32[]{:S(2)}) collective-permute-start(bf16[128,1024]{1,0:T(8,128)(2,1)S(1)} %collective-permute-done.1.refs_2_), channel_id=1, source_target_pairs={{0,1},{1,0},{2,3},{3,2},{4,5},{5,4},{6,7},{7,6},{8,9},{9,8},{10,11... | collective-permute-start | bytes 786440 | tf_op jit(solution)/shard_map/ppermute | solution.py:298
  19.0 0.0 collective-permute-done.3.refs_4_
  19.0 1.6 %collective-permute-start.5 = (bf16[128,1024]{1,0:T(8,128)(2,1)S(1)}, bf16[128,1024]{1,0:T(8,128)(2,1)S(1)}, u32[]{:S(2)}, u32[]{:S(2)}) collective-permute-start(bf16[128,1024]{1,0:T(8,128)(2,1)S(1)} %collective-permute-done.3.refs_4_), channel_id=1, source_target_pairs={{0,4},{4,0},{8,12},{12,8},{16,20},{20,16},{24,28},{28,24},{1,5},{5... | collective-permute-start | bytes 786440 | tf_op jit(solution)/shard_map/ppermute | solution.py:298
  20.6 0.0 collective-permute-done.8.refs_9_
  20.6 3.4 %collective-permute-start.12 = (bf16[128,1024]{1,0:T(8,128)(2,1)S(1)}, bf16[128,1024]{1,0:T(8,128)(2,1)S(1)}, u32[]{:S(2)}, u32[]{:S(2)}) collective-permute-start(bf16[128,1024]{1,0:T(8,128)(2,1)S(1)} %pad_maximum_fusion.refs_0_), channel_id=1, source_target_pairs={{0,24},{4,28},{8,16},{12,20},{16,8},{20,12},{24,0},{28,4},{1,25},{... | collective-permute-start | bytes 786440 | tf_op jit(solution)/shard_map/ppermute | solution.py:298
  24.0 0.0 collective-permute-done.9.refs_3_
  24.0 0.0 collective-permute-done.2.refs_3_
  24.0 3.3 %collective-permute-done.5.refs_6_ = bf16[128,1024]{1,0:T(8,128)(2,1)S(1)} collective-permute-done((bf16[128,1024]{1,0:T(8,128)(2,1)S(1)}, bf16[128,1024]{1,0:T(8,128)(2,1)S(1)}, u32[]{:S(2)}, u32[]{:S(2)}) %collective-permute-start.5) | collective-permute-done | bytes 262176 | tf_op jit(solution)/shard_map/ppermute | solution.py:298
  27.3 1.6 %collective-permute-start.10 = (bf16[128,1024]{1,0:T(8,128)(2,1)S(1)}, bf16[128,1024]{1,0:T(8,128)(2,1)S(1)}, u32[]{:S(2)}, u32[]{:S(2)}) collective-permute-start(bf16[128,1024]{1,0:T(8,128)(2,1)S(1)} %collective-permute-done.7.refs_8_), channel_id=1, source_target_pairs={{0,4},{4,0},{8,12},{12,8},{16,20},{20,16},{24,28},{28,24},{1,5},{5... | collective-permute-start | bytes 786440 | tf_op jit(solution)/shard_map/ppermute | solution.py:298
  28.9 1.6 %collective-permute-done.12.refs_12_ = bf16[128,1024]{1,0:T(8,128)(2,1)S(1)} collective-permute-done((bf16[128,1024]{1,0:T(8,128)(2,1)S(1)}, bf16[128,1024]{1,0:T(8,128)(2,1)S(1)}, u32[]{:S(2)}, u32[]{:S(2)}) %collective-permute-start.12) | collective-permute-done | bytes 262176 | tf_op jit(solution)/shard_map/ppermute | solution.py:298
  30.5 0.5 %collective-permute-start.6 = (bf16[128,1024]{1,0:T(8,128)(2,1)S(1)}, bf16[128,1024]{1,0:T(8,128)(2,1)S(1)}, u32[]{:S(2)}, u32[]{:S(2)}) collective-permute-start(bf16[128,1024]{1,0:T(8,128)(2,1)S(1)} %collective-permute-done.5.refs_6_), channel_id=1, source_target_pairs={{0,1},{1,0},{2,3},{3,2},{4,5},{5,4},{6,7},{7,6},{8,9},{9,8},{10,11... | collective-permute-start | bytes 786440 | tf_op jit(solution)/shard_map/ppermute | solution.py:298
  31.0 3.7 %collective-permute-done.10.refs_10_ = bf16[128,1024]{1,0:T(8,128)(2,1)S(1)} collective-permute-done((bf16[128,1024]{1,0:T(8,128)(2,1)S(1)}, bf16[128,1024]{1,0:T(8,128)(2,1)S(1)}, u32[]{:S(2)}, u32[]{:S(2)}) %collective-permute-start.10) | collective-permute-done | bytes 262176 | tf_op jit(solution)/shard_map/ppermute | solution.py:298
  34.8 1.6 %collective-permute-start.14 = (bf16[128,1024]{1,0:T(8,128)(2,1)S(1)}, bf16[128,1024]{1,0:T(8,128)(2,1)S(1)}, u32[]{:S(2)}, u32[]{:S(2)}) collective-permute-start(bf16[128,1024]{1,0:T(8,128)(2,1)S(1)} %collective-permute-done.12.refs_12_), channel_id=1, source_target_pairs={{0,4},{4,0},{8,12},{12,8},{16,20},{20,16},{24,28},{28,24},{1,5},{5... | collective-permute-start | bytes 786440 | tf_op jit(solution)/shard_map/ppermute | solution.py:298
  37.0 4.6 %assemble.1.partial_ref = bf16[2,1024,512]{2,1,0:T(8,128)(2,1)S(1)} custom-call(s32[1]{0:T(128)S(6)} %copy.14.source_ref, s32[2,2]{1,0:T(2,128)S(1)} %copy-done.2, s32[16,128]{1,0:T(8,128)S(1)} %bitcast.5, bf16[128,1024]{1,0:T(8,128)(2,1)S(1)} %pad_maximum_fusion.refs_0_, bf16[128,1024]{1,0:T(8,128)(2,1)S(1)} %collective-permute-done.refs_1_, ...), custom_call_target="tpu_custom_call" | custom-call | flops 1000 | bytes 1000 | tf_op jit(solution)/shard_map/assemble/pallas_call | solution.py:152
  41.6 1.9 %collective-permute-done.14.refs_0_ = bf16[128,1024]{1,0:T(8,128)(2,1)S(1)} collective-permute-done((bf16[128,1024]{1,0:T(8,128)(2,1)S(1)}, bf16[128,1024]{1,0:T(8,128)(2,1)S(1)}, u32[]{:S(2)}, u32[]{:S(2)}) %collective-permute-start.14) | collective-permute-done | bytes 262176 | tf_op jit(solution)/shard_map/ppermute | solution.py:298
  43.5 0.6 %collective-permute-start.17 = (bf16[1,1,4,64,512]{4,3,2,1,0:T(8,128)(2,1)S(1)}, bf16[1,1,4,64,512]{4,3,2,1,0:T(8,128)(2,1)S(1)}, u32[]{:S(2)}, u32[]{:S(2)}) collective-permute-start(bf16[1,1,4,64,512]{4,3,2,1,0:T(8,128)(2,1)S(1)} %get-tuple-element.34), channel_id=1, source_target_pairs={{0,1},{1,0},{2,3},{3,2},{4,5},{5,4},{6,7},{7,6},{8,9},{9,8},{10,11... | collective-permute-start | bytes 786440 | tf_op jit(solution)/shard_map/ppermute | solution.py:298
  44.1 0.1 collective-permute-start.18
  44.2 0.8 %collective-permute-done.15.refs_1_ = bf16[128,1024]{1,0:T(8,128)(2,1)S(1)} collective-permute-done((bf16[128,1024]{1,0:T(8,128)(2,1)S(1)}, bf16[128,1024]{1,0:T(8,128)(2,1)S(1)}, u32[]{:S(2)}, u32[]{:S(2)}) %collective-permute-start.15) | collective-permute-done | bytes 262176 | tf_op jit(solution)/shard_map/ppermute | solution.py:298
  45.0 2.4 %near.1 = (bf16[2,1024,512]{2,1,0:T(8,128)(2,1)S(1)}, bf16[2,2,4,32,2,512]{5,4,3,2,1,0:T(2,128)(2,1)S(1)}) custom-call(s32[1]{0:T(128)S(6)} %copy.14.source_ref, s32[2,2]{1,0:T(2,128)S(1)} %copy-done.2, s32[16,128]{1,0:T(8,128)S(1)} %bitcast.6, bf16[2,1024,512]{2,1,0:T(8,128)(2,1)S(1)} %assemble.1.partial_ref, ...), custom_call_target="tpu_custom_call" | custom-call | flops 1073741824 | bytes 1000 | tf_op jit(solution)/shard_map/near/pallas_call | solution.py:268
  47.5 2.1 %far.1 = bf16[2,4,32,2,2048]{4,3,2,1,0:T(2,128)(2,1)} custom-call(bf16[2,1024,512]{2,1,0:T(8,128)(2,1)S(1)} %get-tuple-element.30.right, bf16[2,2,4,32,2,512]{5,4,3,2,1,0:T(2,128)(2,1)S(1)} %get-tuple-element.31.near_ref, bf16[2,2,4,64,512]{4,3,2,1,0:T(8,128)(2,1)S(1)} %collective-permute-done.16.refs_0_, ...), custom_call_target="tpu_custom_call" | custom-call | flops 1073741824 | bytes 1000 | tf_op jit(solution)/shard_map/far/pallas_call | solution.py:281
  (22 shorter events, 0.1 us)
Async XLA Ops:
  0.0 9.0 %copy-start.2 = (s32[2,2]{1,0:T(2,128)S(1)}, s32[2,2]{1,0:T(2,128)}, u32[]{:S(2)}) copy-start(s32[2,2]{1,0:T(2,128)} %op_ref.5) | copy-start | bytes 52
  0.0 9.0 %copy-start.3 = (s32[2,128]{1,0:T(2,128)S(1)}, s32[2,128]{1,0:T(2,128)}, u32[]{:S(2)}) copy-start(s32[2,128]{1,0:T(2,128)} %listed_ref.1) | copy-start | bytes 3076
  0.0 9.0 %copy-start = (bf16[1,2,2,512,512]{4,3,2,1,0:T(8,128)(2,1)S(1)}, bf16[1,2,2,512,512]{4,3,2,1,0:T(8,128)(2,1)}, u32[]{:S(2)}) copy-start(bf16[1,2,2,512,512]{4,3,2,1,0:T(8,128)(2,1)} %sink_ref.1) | copy-start | bytes 6291460
  1.7 35.3 %copy-start.1 = (s32[2048]{0:T(1024)S(1)}, s32[2048]{0:T(1024)}, u32[]{:S(2)}) copy-start(s32[2048]{0:T(1024)} %param.10) | copy-start | bytes 24580
  1.7 5.8 %collective-permute-start = (bf16[128,1024]{1,0:T(8,128)(2,1)S(1)}, bf16[128,1024]{1,0:T(8,128)(2,1)S(1)}, u32[]{:S(2)}, u32[]{:S(2)}) collective-permute-start(bf16[128,1024]{1,0:T(8,128)(2,1)S(1)} %pad_maximum_fusion.refs_0_), channel_id=1, source_target_pairs={{0,1},{1,0},{2,3},{3,2},{4,5},{5,4},{6,7},{7,6},{8,9},{9,8},{10,11... | collective-permute-start | bytes 786440 | tf_op jit(solution)/shard_map/ppermute | solution.py:298
  2.2 16.3 %collective-permute-start.7 = (bf16[128,1024]{1,0:T(8,128)(2,1)S(1)}, bf16[128,1024]{1,0:T(8,128)(2,1)S(1)}, u32[]{:S(2)}, u32[]{:S(2)}) collective-permute-start(bf16[128,1024]{1,0:T(8,128)(2,1)S(1)} %pad_maximum_fusion.refs_0_), channel_id=1, source_target_pairs={{0,16},{4,20},{8,24},{12,28},{16,0},{20,4},{24,8},{28,12},{1,17},{... | collective-permute-start | bytes 786440 | tf_op jit(solution)/shard_map/ppermute | solution.py:298
  5.9 13.1 %collective-permute-start.3 = (bf16[128,1024]{1,0:T(8,128)(2,1)S(1)}, bf16[128,1024]{1,0:T(8,128)(2,1)S(1)}, u32[]{:S(2)}, u32[]{:S(2)}) collective-permute-start(bf16[128,1024]{1,0:T(8,128)(2,1)S(1)} %pad_maximum_fusion.refs_0_), channel_id=1, source_target_pairs={{0,8},{4,12},{8,0},{12,4},{16,24},{20,28},{24,16},{28,20},{1,9},{5... | collective-permute-start | bytes 786440 | tf_op jit(solution)/shard_map/ppermute | solution.py:298
  7.5 11.0 %collective-permute-start.1 = (bf16[128,1024]{1,0:T(8,128)(2,1)S(1)}, bf16[128,1024]{1,0:T(8,128)(2,1)S(1)}, u32[]{:S(2)}, u32[]{:S(2)}) collective-permute-start(bf16[128,1024]{1,0:T(8,128)(2,1)S(1)} %pad_maximum_fusion.refs_0_), channel_id=1, source_target_pairs={{0,4},{4,0},{8,12},{12,8},{16,20},{20,16},{24,28},{28,24},{1,5},{5... | collective-permute-start | bytes 786440 | tf_op jit(solution)/shard_map/ppermute | solution.py:298
  14.0 10.0 %collective-permute-start.9 = (bf16[1,2,4,64,512]{4,3,2,1,0:T(8,128)(2,1)S(1)}, bf16[1,2,4,64,512]{4,3,2,1,0:T(8,128)(2,1)S(1)}, u32[]{:S(2)}, u32[]{:S(2)}) collective-permute-start(bf16[1,2,4,64,512]{4,3,2,1,0:T(8,128)(2,1)S(1)} %get-tuple-element.25), channel_id=1, source_target_pairs={{0,1},{1,0},{2,3},{3,2},{4,5},{5,4},{6,7},{7,6},{8,9},{9,8},{10,11... | collective-permute-start | bytes 1572872 | tf_op jit(solution)/shard_map/ppermute | solution.py:298
  14.1 29.4 %collective-permute-start.16 = (bf16[2,2,4,64,512]{4,3,2,1,0:T(8,128)(2,1)S(1)}, bf16[2,2,4,64,512]{4,3,2,1,0:T(8,128)(2,1)S(1)}, u32[]{:S(2)}, u32[]{:S(2)}) collective-permute-start(bf16[2,2,4,64,512]{4,3,2,1,0:T(8,128)(2,1)S(1)} %get-tuple-element.32), channel_id=1, source_target_pairs={{0,2},{1,3},{2,0},{3,1},{4,6},{5,7},{6,4},{7,5},{8,10},{9,11},{10,... | collective-permute-start | bytes 3145736 | tf_op jit(solution)/shard_map/ppermute | solution.py:298
  18.5 2.1 %collective-permute-start.8 = (bf16[128,1024]{1,0:T(8,128)(2,1)S(1)}, bf16[128,1024]{1,0:T(8,128)(2,1)S(1)}, u32[]{:S(2)}, u32[]{:S(2)}) collective-permute-start(bf16[128,1024]{1,0:T(8,128)(2,1)S(1)} %collective-permute-done.7.refs_8_), channel_id=1, source_target_pairs={{0,1},{1,0},{2,3},{3,2},{4,5},{5,4},{6,7},{7,6},{8,9},{9,8},{10,11... | collective-permute-start | bytes 786440 | tf_op jit(solution)/shard_map/ppermute | solution.py:298
  18.5 5.5 %collective-permute-start.2 = (bf16[128,1024]{1,0:T(8,128)(2,1)S(1)}, bf16[128,1024]{1,0:T(8,128)(2,1)S(1)}, u32[]{:S(2)}, u32[]{:S(2)}) collective-permute-start(bf16[128,1024]{1,0:T(8,128)(2,1)S(1)} %collective-permute-done.1.refs_2_), channel_id=1, source_target_pairs={{0,1},{1,0},{2,3},{3,2},{4,5},{5,4},{6,7},{7,6},{8,9},{9,8},{10,11... | collective-permute-start | bytes 786440 | tf_op jit(solution)/shard_map/ppermute | solution.py:298
  19.0 8.3 %collective-permute-start.5 = (bf16[128,1024]{1,0:T(8,128)(2,1)S(1)}, bf16[128,1024]{1,0:T(8,128)(2,1)S(1)}, u32[]{:S(2)}, u32[]{:S(2)}) collective-permute-start(bf16[128,1024]{1,0:T(8,128)(2,1)S(1)} %collective-permute-done.3.refs_4_), channel_id=1, source_target_pairs={{0,4},{4,0},{8,12},{12,8},{16,20},{20,16},{24,28},{28,24},{1,5},{5... | collective-permute-start | bytes 786440 | tf_op jit(solution)/shard_map/ppermute | solution.py:298
  20.6 9.9 %collective-permute-start.12 = (bf16[128,1024]{1,0:T(8,128)(2,1)S(1)}, bf16[128,1024]{1,0:T(8,128)(2,1)S(1)}, u32[]{:S(2)}, u32[]{:S(2)}) collective-permute-start(bf16[128,1024]{1,0:T(8,128)(2,1)S(1)} %pad_maximum_fusion.refs_0_), channel_id=1, source_target_pairs={{0,24},{4,28},{8,16},{12,20},{16,8},{20,12},{24,0},{28,4},{1,25},{... | collective-permute-start | bytes 786440 | tf_op jit(solution)/shard_map/ppermute | solution.py:298
  27.3 7.4 %collective-permute-start.10 = (bf16[128,1024]{1,0:T(8,128)(2,1)S(1)}, bf16[128,1024]{1,0:T(8,128)(2,1)S(1)}, u32[]{:S(2)}, u32[]{:S(2)}) collective-permute-start(bf16[128,1024]{1,0:T(8,128)(2,1)S(1)} %collective-permute-done.7.refs_8_), channel_id=1, source_target_pairs={{0,4},{4,0},{8,12},{12,8},{16,20},{20,16},{24,28},{28,24},{1,5},{5... | collective-permute-start | bytes 786440 | tf_op jit(solution)/shard_map/ppermute | solution.py:298
  28.9 5.9 %collective-permute-start.4 = (bf16[128,1024]{1,0:T(8,128)(2,1)S(1)}, bf16[128,1024]{1,0:T(8,128)(2,1)S(1)}, u32[]{:S(2)}, u32[]{:S(2)}) collective-permute-start(bf16[128,1024]{1,0:T(8,128)(2,1)S(1)} %collective-permute-done.3.refs_4_), channel_id=1, source_target_pairs={{0,1},{1,0},{2,3},{3,2},{4,5},{5,4},{6,7},{7,6},{8,9},{9,8},{10,11... | collective-permute-start | bytes 786440 | tf_op jit(solution)/shard_map/ppermute | solution.py:298
  30.5 6.5 %collective-permute-start.13 = (bf16[128,1024]{1,0:T(8,128)(2,1)S(1)}, bf16[128,1024]{1,0:T(8,128)(2,1)S(1)}, u32[]{:S(2)}, u32[]{:S(2)}) collective-permute-start(bf16[128,1024]{1,0:T(8,128)(2,1)S(1)} %collective-permute-done.12.refs_12_), channel_id=1, source_target_pairs={{0,1},{1,0},{2,3},{3,2},{4,5},{5,4},{6,7},{7,6},{8,9},{9,8},{10,11... | collective-permute-start | bytes 786440 | tf_op jit(solution)/shard_map/ppermute | solution.py:298
  30.5 6.5 %collective-permute-start.6 = (bf16[128,1024]{1,0:T(8,128)(2,1)S(1)}, bf16[128,1024]{1,0:T(8,128)(2,1)S(1)}, u32[]{:S(2)}, u32[]{:S(2)}) collective-permute-start(bf16[128,1024]{1,0:T(8,128)(2,1)S(1)} %collective-permute-done.5.refs_6_), channel_id=1, source_target_pairs={{0,1},{1,0},{2,3},{3,2},{4,5},{5,4},{6,7},{7,6},{8,9},{9,8},{10,11... | collective-permute-start | bytes 786440 | tf_op jit(solution)/shard_map/ppermute | solution.py:298
  34.8 2.2 %collective-permute-start.11 = (bf16[128,1024]{1,0:T(8,128)(2,1)S(1)}, bf16[128,1024]{1,0:T(8,128)(2,1)S(1)}, u32[]{:S(2)}, u32[]{:S(2)}) collective-permute-start(bf16[128,1024]{1,0:T(8,128)(2,1)S(1)} %collective-permute-done.10.refs_10_), channel_id=1, source_target_pairs={{0,1},{1,0},{2,3},{3,2},{4,5},{5,4},{6,7},{7,6},{8,9},{9,8},{10,11... | collective-permute-start | bytes 786440 | tf_op jit(solution)/shard_map/ppermute | solution.py:298
  34.8 8.7 %collective-permute-start.14 = (bf16[128,1024]{1,0:T(8,128)(2,1)S(1)}, bf16[128,1024]{1,0:T(8,128)(2,1)S(1)}, u32[]{:S(2)}, u32[]{:S(2)}) collective-permute-start(bf16[128,1024]{1,0:T(8,128)(2,1)S(1)} %collective-permute-done.12.refs_12_), channel_id=1, source_target_pairs={{0,4},{4,0},{8,12},{12,8},{16,20},{20,16},{24,28},{28,24},{1,5},{5... | collective-permute-start | bytes 786440 | tf_op jit(solution)/shard_map/ppermute | solution.py:298
  43.5 1.5 %collective-permute-start.15 = (bf16[128,1024]{1,0:T(8,128)(2,1)S(1)}, bf16[128,1024]{1,0:T(8,128)(2,1)S(1)}, u32[]{:S(2)}, u32[]{:S(2)}) collective-permute-start(bf16[128,1024]{1,0:T(8,128)(2,1)S(1)} %collective-permute-done.14.refs_0_), channel_id=1, source_target_pairs={{0,1},{1,0},{2,3},{3,2},{4,5},{5,4},{6,7},{7,6},{8,9},{9,8},{10,11... | collective-permute-start | bytes 786440 | tf_op jit(solution)/shard_map/ppermute | solution.py:298
  43.5 3.9 %collective-permute-start.17 = (bf16[1,1,4,64,512]{4,3,2,1,0:T(8,128)(2,1)S(1)}, bf16[1,1,4,64,512]{4,3,2,1,0:T(8,128)(2,1)S(1)}, u32[]{:S(2)}, u32[]{:S(2)}) collective-permute-start(bf16[1,1,4,64,512]{4,3,2,1,0:T(8,128)(2,1)S(1)} %get-tuple-element.34), channel_id=1, source_target_pairs={{0,1},{1,0},{2,3},{3,2},{4,5},{5,4},{6,7},{7,6},{8,9},{9,8},{10,11... | collective-permute-start | bytes 786440 | tf_op jit(solution)/shard_map/ppermute | solution.py:298
  44.1 3.4 %collective-permute-start.18 = (bf16[1,1,4,64,512]{4,3,2,1,0:T(8,128)(2,1)S(1)}, bf16[1,1,4,64,512]{4,3,2,1,0:T(8,128)(2,1)S(1)}, u32[]{:S(2)}, u32[]{:S(2)}) collective-permute-start(bf16[1,1,4,64,512]{4,3,2,1,0:T(8,128)(2,1)S(1)} %get-tuple-element.33), channel_id=1, source_target_pairs={{0,1},{1,0},{2,3},{3,2},{4,5},{5,4},{6,7},{7,6},{8,9},{9,8},{10,11... | collective-permute-start | bytes 786440 | tf_op jit(solution)/shard_map/ppermute | solution.py:298

commit v6 on v5

--- a/solution.py
+++ b/solution.py
@@ -116,12 +116,13 @@
         ]
     col = jnp.concatenate(cols, axis=0)
     tiles, tables = [], []
-    for place, parts in zip(places, pieces):
-        height = sum(part.shape[0] for part in parts)
-        first = place
-        if isinstance(place, tuple):
-            first = (2 * (pair ^ place[0]) + (side ^ place[1])) * height
-        tiles.append(one_hot(col, first, height))
+    for owners, parts in zip(places, pieces):
+        height = sum(part.shape[0] for part in parts) // len(owners)
+        for owner in owners:
+            first = owner
+            if isinstance(owner, tuple):
+                first = (2 * (pair ^ owner[0]) + (side ^ owner[1])) * height
+            tiles.append(one_hot(col, first, height))
         tables += [part[...] for part in parts]
     return dot(jnp.concatenate(tiles, axis=1), jnp.concatenate(tables, axis=0))
 
@@ -320,41 +321,38 @@
         half = whole.shape[0] // 2
         mixed = mix(op_index, listed_rows, sink_ops, peramb, [1] * n_cols)
         blocks = [[mixed[0]]] + [[swap(mixed[j], "col", n_cols, j)] for j in range(1, n_cols)]
-        partial = assemble([0], [[whole[:half]]], pair_source, op_index, slots, eigen)
+        partial = assemble([[0]], [[whole[:half]]], pair_source, op_index, slots, eigen)
         return contract(
-            [half], [[whole[half:]]], partial, pair_source, op_index, slots, blocks
+            [[half]], [[whole[half:]]], partial, pair_source, op_index, slots, blocks
         )
     half = rows // 2
     own = lax.dynamic_slice_in_dim(op_table, lax.axis_index("col") % 2 * half, half, 0)
     own = jnp.concatenate([own[:, 0], own[:, 1]], axis=1)
-    held = {(0, 0): own, (0, 1): beside(own)}
-    for mask in (2, 4):
-        held[mask, 0] = across(own, mask)
-    held[1, 0] = across(after(own, held[0, 1]), 1)
+    beside_own = beside(own)
+    z2 = across(own, 4)
+    z1 = across(own, 2)
+    x0 = across(after(own, beside_own), 1)
     mixed = mix(op_index, listed_rows, sink_ops, peramb, [1, 1, 2])
     crossed = swap(mixed[2], "col", n_cols, 2)
-    halves = [beside(crossed[1:, k : k + 1]) for k in range(mixed[2].shape[1])]
-    beside_me = beside(mixed[1])
-    blocks = [[mixed[0]], [beside_me], [crossed], halves]
-    for mask in (1, 2, 4):
-        held[mask, 1] = beside(after(held[mask, 0], mixed[0]))
-    held[3, 0] = across(after(held[2, 0], mixed[0], held[1, 0]), 1)
-    held[6, 0] = across(after(own, mixed[0]), 6)
-    held[6, 1] = beside(held[6, 0])
-    held[5, 0] = across(
-        after(held[4, 0], held[4, 1], held[3, 0], held[1, 1], beside_me), 1
-    )
-    held[7, 0] = across(after(held[6, 0], held[5, 0]), 1)
-    for mask in (3, 5):
-        held[mask, 1] = beside(held[mask, 0])
-    early = [(mask, side) for mask in range(7) for side in (0, 1)]
-    held = {p: pieces if isinstance(pieces, list) else [pieces] for p, pieces in held.items()}
-    partial = assemble(early, [held[p] for p in early], pair_source, op_index, slots, eigen)
-    held[7, 1] = [beside(after(held[7, 0][0], partial))]
-    late = [(7, 0), (7, 1)]
-    return contract(
-        late, [held[p] for p in late], partial, pair_source, op_index, slots, blocks
-    )
+    beside_mixed = beside(mixed[1])
+    blocks = [[mixed[0]], [beside_mixed], [crossed], [beside(crossed[1:])]]
+    beside_x0 = beside(after(x0, mixed[0]))
+    z3 = across(after(own, mixed[0]), 6)
+    z12 = after(jnp.concatenate([z1, z2]), mixed[0], x0)
+    x12 = across(z12, 1)
+    x3 = across(after(z3, x12, beside_x0, beside_mixed), 1)
+    early = [
+        ([(0, 0)], own), ([(0, 1)], beside_own),
+        ([(1, 0)], x0), ([(1, 1)], beside_x0),
+        ([(2, 0), (4, 0)], z12), ([(2, 1), (4, 1)], beside(z12)),
+        ([(6, 0)], z3), ([(6, 1)], beside(z3)),
+        ([(3, 0), (5, 0)], x12), ([(3, 1), (5, 1)], beside(x12)),
+    ]
+    places, pieces = [p for p, _ in early], [[piece] for _, piece in early]
+    partial = assemble(places, pieces, pair_source, op_index, slots, eigen)
+    late = [[x3], [beside(after(x3, partial))]]
+    places = [[(7, 0)], [(7, 1)]]
+    return contract(places, late, partial, pair_source, op_index, slots, blocks)
 
 
 def solution(mesh):

time: 49.8 us -> 50.6 us (1.016)
  waiting for transfers between devices: 14.3 us -> 17.1 us
  starting transfers between devices: 18.7 us -> 16.7 us
    ppermute x19 -> x15, waiting for transfers between devices: 14.3 us -> 17.1 us  [swap(): return lax.ppermute(array, axis, [(i, i ^ mask) for i in range(size)])]
    ppermute x19 -> x15, starting transfers between devices: 18.7 us -> 16.7 us  [swap(): return lax.ppermute(array, axis, [(i, i ^ mask) for i in range(size)])]
  transfers between devices with their start and end apart: 19 -> 15, of which waited for: 6 -> 6; matrix products, arithmetic and copies ran while one was open for 0% -> 0% of each run, Pallas kernels for 24% -> 24%
where the time goes in v6:
time: 50.6 us; the launch traced here: 50.4 us
  waiting for transfers between devices  17.1 us (34%)
  starting transfers between devices  16.7 us (33%)
  Pallas kernels  14.1 us (28%)
  local copies, waits for them, and re-layouts  1.69 us (3%)
  between operations  0.78 us (2%)
    ppermute x15, waiting for transfers between devices, swap(): return lax.ppermute(array, axis, [(i, i ^ mask) for i in range(size)])  17.1 us
    ppermute x15, starting transfers between devices, swap(): return lax.ppermute(array, axis, [(i, i ^ mask) for i in range(size)])  16.7 us
    pallas_call x1, Pallas kernels, mix(): pl.pallas_call(mix_kernel, in_specs=[pl.BlockSpec(memory_space=pltpu.SMEM...  4.99 us
    pallas_call x1, Pallas kernels, assemble(): pl.pallas_call(functools.partial(assemble_kernel, places, [len(group) for...  4.55 us
    pallas_call x1, Pallas kernels, contract(): pl.pallas_call(functools.partial(near_kernel, places, near_masks, [len(g)...  2.44 us
    pallas_call x1, Pallas kernels, contract(): pl.pallas_call(functools.partial(far_kernel, near_masks, far_masks, [len(...  2.12 us
    slice x1, local copies, waits for them, and re-layouts, per_device(): own = jnp.concatenate([own[:, 0], own[:, 1]], axis=1)  1.6 us
  transfers between devices with their start and end apart: 15, of which 6 were waited for; matrix products, arithmetic and copies ran while one was open for 0% of the time, Pallas kernels for 24%

profile of v6, /device:TPU:0, one launch (start us, length us, event | category | flops | bytes accessed | tf_op | source)
XLA Modules:
  0.0 50.4 jit_solution(12400886629420956874)
XLA Ops:
  0.0 1.6 %constant_dynamic-slice_fusion = (bf16[128,1,512]{2,1,0:T(2,128)(2,1)S(1)}, bf16[128,1,512]{2,1,0:T(2,128)(2,1)S(1)}) fusion(bf16[256,2,512]{2,1,0:T(2,128)(2,1)} %param.9, s32[]{:T(128)S(6)} %select_n.11, s32[]{:T(128)S(6)} %add.9), kind=kLoop, calls=%fused_computation.4 | loop fusion | bytes 524296 | tf_op jit(solution)/shard_map/slice | solution.py:330
  1.7 0.5 %collective-permute-start = (bf16[128,1024]{1,0:T(8,128)(2,1)S(1)}, bf16[128,1024]{1,0:T(8,128)(2,1)S(1)}, u32[]{:S(2)}, u32[]{:S(2)}) collective-permute-start(bf16[128,1024]{1,0:T(8,128)(2,1)S(1)} %pad_maximum_fusion.1.refs_0_), channel_id=1, source_target_pairs={{0,1},{1,0},{2,3},{3,2},{4,5},{5,4},{6,7},{7,6},{8,9},{9,8},{10,11... | collective-permute-start | bytes 786440 | tf_op jit(solution)/shard_map/ppermute | solution.py:299
  2.2 3.7 %collective-permute-start.4 = (bf16[128,1024]{1,0:T(8,128)(2,1)S(1)}, bf16[128,1024]{1,0:T(8,128)(2,1)S(1)}, u32[]{:S(2)}, u32[]{:S(2)}) collective-permute-start(bf16[128,1024]{1,0:T(8,128)(2,1)S(1)} %pad_maximum_fusion.1.refs_0_), channel_id=1, source_target_pairs={{0,16},{4,20},{8,24},{12,28},{16,0},{20,4},{24,8},{28,12},{1,17},{... | collective-permute-start | bytes 786440 | tf_op jit(solution)/shard_map/ppermute | solution.py:299
  5.9 1.6 %collective-permute-start.3 = (bf16[128,1024]{1,0:T(8,128)(2,1)S(1)}, bf16[128,1024]{1,0:T(8,128)(2,1)S(1)}, u32[]{:S(2)}, u32[]{:S(2)}) collective-permute-start(bf16[128,1024]{1,0:T(8,128)(2,1)S(1)} %pad_maximum_fusion.1.refs_0_), channel_id=1, source_target_pairs={{0,8},{4,12},{8,0},{12,4},{16,24},{20,28},{24,16},{28,20},{1,9},{5... | collective-permute-start | bytes 786440 | tf_op jit(solution)/shard_map/ppermute | solution.py:299
  7.5 0.0 collective-permute-done.refs_1_
  7.5 1.5 %collective-permute-start.1 = (bf16[128,1024]{1,0:T(8,128)(2,1)S(1)}, bf16[128,1024]{1,0:T(8,128)(2,1)S(1)}, u32[]{:S(2)}, u32[]{:S(2)}) collective-permute-start(bf16[128,1024]{1,0:T(8,128)(2,1)S(1)} %pad_maximum_fusion.1.refs_0_), channel_id=1, source_target_pairs={{0,4},{4,0},{8,12},{12,8},{16,20},{20,16},{24,28},{28,24},{1,5},{5... | collective-permute-start | bytes 786440 | tf_op jit(solution)/shard_map/ppermute | solution.py:299
  9.0 5.0 %mix.1 = (bf16[1,2,4,64,512]{4,3,2,1,0:T(8,128)(2,1)S(1)}, bf16[1,2,4,64,512]{4,3,2,1,0:T(8,128)(2,1)S(1)}, bf16[2,2,4,64,512]{4,3,2,1,0:T(8,128)(2,1)S(1)}) custom-call(s32[2,2]{1,0:T(2,128)S(1)} %copy-done.2, s32[2,128]{1,0:T(2,128)S(1)} %copy-done.3, bf16[1,2,2,512,512]{4,3,2,1,0:T(8,128)(2,1)S(1)} %copy-done, bf16[1,2,2048,512]{3,2,1,0:T(8,128)(2,1)} %peramb_ref.1), custom_call_target="tpu_custom_call" | custom-call | flops 1000 | bytes 1000 | tf_op jit(solution)/shard_map/mix/pallas_call | solution.py:88
  14.0 0.0 copy-start.1
  14.0 1.6 %collective-permute-start.13 = (bf16[2,2,4,64,512]{4,3,2,1,0:T(8,128)(2,1)S(1)}, bf16[2,2,4,64,512]{4,3,2,1,0:T(8,128)(2,1)S(1)}, u32[]{:S(2)}, u32[]{:S(2)}) collective-permute-start(bf16[2,2,4,64,512]{4,3,2,1,0:T(8,128)(2,1)S(1)} %get-tuple-element.26), channel_id=1, source_target_pairs={{0,2},{1,3},{2,0},{3,1},{4,6},{5,7},{6,4},{7,5},{8,10},{9,11},{10,... | collective-permute-start | bytes 3145736 | tf_op jit(solution)/shard_map/ppermute | solution.py:299
  15.6 2.9 %collective-permute-done.4 = bf16[128,1024]{1,0:T(8,128)(2,1)S(1)} collective-permute-done((bf16[128,1024]{1,0:T(8,128)(2,1)S(1)}, bf16[128,1024]{1,0:T(8,128)(2,1)S(1)}, u32[]{:S(2)}, u32[]{:S(2)}) %collective-permute-start.4) | collective-permute-done | bytes 262176 | tf_op jit(solution)/shard_map/ppermute | solution.py:299
  18.5 0.2 collective-permute-done.3
  18.7 0.0 collective-permute-done.1.refs_2_
  18.8 1.6 %collective-permute-start.8 = (bf16[256,1024]{1,0:T(8,128)(2,1)S(1)}, bf16[256,1024]{1,0:T(8,128)(2,1)S(1)}, u32[]{:S(2)}, u32[]{:S(2)}) collective-permute-start(bf16[256,1024]{1,0:T(8,128)(2,1)S(1)} %pad_maximum_fusion.refs_4_), channel_id=1, source_target_pairs={{0,4},{4,0},{8,12},{12,8},{16,20},{20,16},{24,28},{28,24},{1,5},{5... | collective-permute-start | bytes 1572872 | tf_op jit(solution)/shard_map/ppermute | solution.py:299
  20.4 3.2 %collective-permute-start.6 = (bf16[128,1024]{1,0:T(8,128)(2,1)S(1)}, bf16[128,1024]{1,0:T(8,128)(2,1)S(1)}, u32[]{:S(2)}, u32[]{:S(2)}) collective-permute-start(bf16[128,1024]{1,0:T(8,128)(2,1)S(1)} %pad_maximum_fusion.1.refs_0_), channel_id=1, source_target_pairs={{0,24},{4,28},{8,16},{12,20},{16,8},{20,12},{24,0},{28,4},{1,25},{... | collective-permute-start | bytes 786440 | tf_op jit(solution)/shard_map/ppermute | solution.py:299
  23.6 0.5 %collective-permute-start.5 = (bf16[256,1024]{1,0:T(8,128)(2,1)S(1)}, bf16[256,1024]{1,0:T(8,128)(2,1)S(1)}, u32[]{:S(2)}, u32[]{:S(2)}) collective-permute-start(bf16[256,1024]{1,0:T(8,128)(2,1)S(1)} %pad_maximum_fusion.refs_4_), channel_id=1, source_target_pairs={{0,1},{1,0},{2,3},{3,2},{4,5},{5,4},{6,7},{7,6},{8,9},{9,8},{10,11... | collective-permute-start | bytes 1572872 | tf_op jit(solution)/shard_map/ppermute | solution.py:299
  24.1 5.8 %collective-permute-done.6.refs_6_ = bf16[128,1024]{1,0:T(8,128)(2,1)S(1)} collective-permute-done((bf16[128,1024]{1,0:T(8,128)(2,1)S(1)}, bf16[128,1024]{1,0:T(8,128)(2,1)S(1)}, u32[]{:S(2)}, u32[]{:S(2)}) %collective-permute-start.6) | collective-permute-done | bytes 262176 | tf_op jit(solution)/shard_map/ppermute | solution.py:299
  29.9 2.3 %collective-permute-done.8.refs_8_ = bf16[256,1024]{1,0:T(8,128)(2,1)S(1)} collective-permute-done((bf16[256,1024]{1,0:T(8,128)(2,1)S(1)}, bf16[256,1024]{1,0:T(8,128)(2,1)S(1)}, u32[]{:S(2)}, u32[]{:S(2)}) %collective-permute-start.8) | collective-permute-done | bytes 524320 | tf_op jit(solution)/shard_map/ppermute | solution.py:299
  32.3 0.0 collective-permute-start.9
  32.3 0.0 collective-permute-done.10.refs_3_
  32.3 0.5 %collective-permute-start.7 = (bf16[128,1024]{1,0:T(8,128)(2,1)S(1)}, bf16[128,1024]{1,0:T(8,128)(2,1)S(1)}, u32[]{:S(2)}, u32[]{:S(2)}) collective-permute-start(bf16[128,1024]{1,0:T(8,128)(2,1)S(1)} %collective-permute-done.6.refs_6_), channel_id=1, source_target_pairs={{0,1},{1,0},{2,3},{3,2},{4,5},{5,4},{6,7},{7,6},{8,9},{9,8},{10,11... | collective-permute-start | bytes 786440 | tf_op jit(solution)/shard_map/ppermute | solution.py:299
  32.8 0.0 collective-permute-done.2.refs_3_
  32.8 1.4 %collective-permute-start.11 = (bf16[128,1024]{1,0:T(8,128)(2,1)S(1)}, bf16[128,1024]{1,0:T(8,128)(2,1)S(1)}, u32[]{:S(2)}, u32[]{:S(2)}) collective-permute-start(bf16[128,1024]{1,0:T(8,128)(2,1)S(1)} %collective-permute-done.6.refs_6_), channel_id=1, source_target_pairs={{0,4},{4,0},{8,12},{12,8},{16,20},{20,16},{24,28},{28,24},{1,5},{5... | collective-permute-start | bytes 786440 | tf_op jit(solution)/shard_map/ppermute | solution.py:299
  34.1 4.6 %collective-permute-done.13.refs_0_ = bf16[2,2,4,64,512]{4,3,2,1,0:T(8,128)(2,1)S(1)} collective-permute-done((bf16[2,2,4,64,512]{4,3,2,1,0:T(8,128)(2,1)S(1)}, bf16[2,2,4,64,512]{4,3,2,1,0:T(8,128)(2,1)S(1)}, u32[]{:S(2)}, u32[]{:S(2)}) %collective-permute-start.13) | collective-permute-done | bytes 1048608 | tf_op jit(solution)/shard_map/ppermute | solution.py:299
  38.8 0.1 collective-permute-start.14
  39.5 0.0 collective-permute-done.5.refs_5_
  39.5 0.0 collective-permute-done.9.refs_9_
  39.5 4.6 %assemble.1.partial_ref = bf16[2,1024,512]{2,1,0:T(8,128)(2,1)S(1)} custom-call(s32[1]{0:T(128)S(6)} %copy.14.source_ref, s32[2,2]{1,0:T(2,128)S(1)} %copy-done.2, s32[16,128]{1,0:T(8,128)S(1)} %bitcast.5, bf16[128,1024]{1,0:T(8,128)(2,1)S(1)} %pad_maximum_fusion.1.refs_0_, bf16[128,1024]{1,0:T(8,128)(2,1)S(1)} %collective-permute-done.refs_1_, ...), custom_call_target="tpu_custom_call" | custom-call | flops 1000 | bytes 1000 | tf_op jit(solution)/shard_map/assemble/pallas_call | solution.py:153
  44.1 0.0 collective-permute-done.11.refs_0_
  44.1 0.6 %collective-permute-start.12 = (bf16[128,1024]{1,0:T(8,128)(2,1)S(1)}, bf16[128,1024]{1,0:T(8,128)(2,1)S(1)}, u32[]{:S(2)}, u32[]{:S(2)}) collective-permute-start(bf16[128,1024]{1,0:T(8,128)(2,1)S(1)} %collective-permute-done.11.refs_0_), channel_id=1, source_target_pairs={{0,1},{1,0},{2,3},{3,2},{4,5},{5,4},{6,7},{7,6},{8,9},{9,8},{10,11... | collective-permute-start | bytes 786440 | tf_op jit(solution)/shard_map/ppermute | solution.py:299
  44.7 1.2 %collective-permute-done.12.refs_1_ = bf16[128,1024]{1,0:T(8,128)(2,1)S(1)} collective-permute-done((bf16[128,1024]{1,0:T(8,128)(2,1)S(1)}, bf16[128,1024]{1,0:T(8,128)(2,1)S(1)}, u32[]{:S(2)}, u32[]{:S(2)}) %collective-permute-start.12) | collective-permute-done | bytes 262176 | tf_op jit(solution)/shard_map/ppermute | solution.py:299
  45.8 2.4 %near.1 = (bf16[2,1024,512]{2,1,0:T(8,128)(2,1)S(1)}, bf16[2,2,4,32,2,512]{5,4,3,2,1,0:T(2,128)(2,1)S(1)}) custom-call(s32[1]{0:T(128)S(6)} %copy.14.source_ref, s32[2,2]{1,0:T(2,128)S(1)} %copy-done.2, s32[16,128]{1,0:T(8,128)S(1)} %bitcast.6, bf16[2,1024,512]{2,1,0:T(8,128)(2,1)S(1)} %assemble.1.partial_ref, ...), custom_call_target="tpu_custom_call" | custom-call | flops 1073741824 | bytes 1000 | tf_op jit(solution)/shard_map/near/pallas_call | solution.py:269
  48.3 2.1 %far.1 = bf16[2,4,32,2,2048]{4,3,2,1,0:T(2,128)(2,1)} custom-call(bf16[2,1024,512]{2,1,0:T(8,128)(2,1)S(1)} %get-tuple-element.24.right, bf16[2,2,4,32,2,512]{5,4,3,2,1,0:T(2,128)(2,1)S(1)} %get-tuple-element.25.near_ref, bf16[2,2,4,64,512]{4,3,2,1,0:T(8,128)(2,1)S(1)} %collective-permute-done.13.refs_0_, ...), custom_call_target="tpu_custom_call" | custom-call | flops 1073741824 | bytes 1000 | tf_op jit(solution)/shard_map/far/pallas_call | solution.py:282
  (15 shorter events, 0.2 us)
Async XLA Ops:
  0.0 9.0 %copy-start.2 = (s32[2,2]{1,0:T(2,128)S(1)}, s32[2,2]{1,0:T(2,128)}, u32[]{:S(2)}) copy-start(s32[2,2]{1,0:T(2,128)} %op_ref.5) | copy-start | bytes 52
  0.0 9.0 %copy-start.3 = (s32[2,128]{1,0:T(2,128)S(1)}, s32[2,128]{1,0:T(2,128)}, u32[]{:S(2)}) copy-start(s32[2,128]{1,0:T(2,128)} %listed_ref.1) | copy-start | bytes 3076
  0.0 9.0 %copy-start = (bf16[1,2,2,512,512]{4,3,2,1,0:T(8,128)(2,1)S(1)}, bf16[1,2,2,512,512]{4,3,2,1,0:T(8,128)(2,1)}, u32[]{:S(2)}) copy-start(bf16[1,2,2,512,512]{4,3,2,1,0:T(8,128)(2,1)} %sink_ref.1) | copy-start | bytes 6291460
  1.7 5.8 %collective-permute-start = (bf16[128,1024]{1,0:T(8,128)(2,1)S(1)}, bf16[128,1024]{1,0:T(8,128)(2,1)S(1)}, u32[]{:S(2)}, u32[]{:S(2)}) collective-permute-start(bf16[128,1024]{1,0:T(8,128)(2,1)S(1)} %pad_maximum_fusion.1.refs_0_), channel_id=1, source_target_pairs={{0,1},{1,0},{2,3},{3,2},{4,5},{5,4},{6,7},{7,6},{8,9},{9,8},{10,11... | collective-permute-start | bytes 786440 | tf_op jit(solution)/shard_map/ppermute | solution.py:299
  2.2 16.3 %collective-permute-start.4 = (bf16[128,1024]{1,0:T(8,128)(2,1)S(1)}, bf16[128,1024]{1,0:T(8,128)(2,1)S(1)}, u32[]{:S(2)}, u32[]{:S(2)}) collective-permute-start(bf16[128,1024]{1,0:T(8,128)(2,1)S(1)} %pad_maximum_fusion.1.refs_0_), channel_id=1, source_target_pairs={{0,16},{4,20},{8,24},{12,28},{16,0},{20,4},{24,8},{28,12},{1,17},{... | collective-permute-start | bytes 786440 | tf_op jit(solution)/shard_map/ppermute | solution.py:299
  5.9 12.8 %collective-permute-start.3 = (bf16[128,1024]{1,0:T(8,128)(2,1)S(1)}, bf16[128,1024]{1,0:T(8,128)(2,1)S(1)}, u32[]{:S(2)}, u32[]{:S(2)}) collective-permute-start(bf16[128,1024]{1,0:T(8,128)(2,1)S(1)} %pad_maximum_fusion.1.refs_0_), channel_id=1, source_target_pairs={{0,8},{4,12},{8,0},{12,4},{16,24},{20,28},{24,16},{28,20},{1,9},{5... | collective-permute-start | bytes 786440 | tf_op jit(solution)/shard_map/ppermute | solution.py:299
  7.5 11.3 %collective-permute-start.1 = (bf16[128,1024]{1,0:T(8,128)(2,1)S(1)}, bf16[128,1024]{1,0:T(8,128)(2,1)S(1)}, u32[]{:S(2)}, u32[]{:S(2)}) collective-permute-start(bf16[128,1024]{1,0:T(8,128)(2,1)S(1)} %pad_maximum_fusion.1.refs_0_), channel_id=1, source_target_pairs={{0,4},{4,0},{8,12},{12,8},{16,20},{20,16},{24,28},{28,24},{1,5},{5... | collective-permute-start | bytes 786440 | tf_op jit(solution)/shard_map/ppermute | solution.py:299
  14.0 25.5 %copy-start.1 = (s32[2048]{0:T(1024)S(1)}, s32[2048]{0:T(1024)}, u32[]{:S(2)}) copy-start(s32[2048]{0:T(1024)} %param.10) | copy-start | bytes 24580
  14.0 24.7 %collective-permute-start.13 = (bf16[2,2,4,64,512]{4,3,2,1,0:T(8,128)(2,1)S(1)}, bf16[2,2,4,64,512]{4,3,2,1,0:T(8,128)(2,1)S(1)}, u32[]{:S(2)}, u32[]{:S(2)}) collective-permute-start(bf16[2,2,4,64,512]{4,3,2,1,0:T(8,128)(2,1)S(1)} %get-tuple-element.26), channel_id=1, source_target_pairs={{0,2},{1,3},{2,0},{3,1},{4,6},{5,7},{6,4},{7,5},{8,10},{9,11},{10,... | collective-permute-start | bytes 3145736 | tf_op jit(solution)/shard_map/ppermute | solution.py:299
  18.8 13.5 %collective-permute-start.8 = (bf16[256,1024]{1,0:T(8,128)(2,1)S(1)}, bf16[256,1024]{1,0:T(8,128)(2,1)S(1)}, u32[]{:S(2)}, u32[]{:S(2)}) collective-permute-start(bf16[256,1024]{1,0:T(8,128)(2,1)S(1)} %pad_maximum_fusion.refs_4_), channel_id=1, source_target_pairs={{0,4},{4,0},{8,12},{12,8},{16,20},{20,16},{24,28},{28,24},{1,5},{5... | collective-permute-start | bytes 1572872 | tf_op jit(solution)/shard_map/ppermute | solution.py:299
  20.4 9.6 %collective-permute-start.6 = (bf16[128,1024]{1,0:T(8,128)(2,1)S(1)}, bf16[128,1024]{1,0:T(8,128)(2,1)S(1)}, u32[]{:S(2)}, u32[]{:S(2)}) collective-permute-start(bf16[128,1024]{1,0:T(8,128)(2,1)S(1)} %pad_maximum_fusion.1.refs_0_), channel_id=1, source_target_pairs={{0,24},{4,28},{8,16},{12,20},{16,8},{20,12},{24,0},{28,4},{1,25},{... | collective-permute-start | bytes 786440 | tf_op jit(solution)/shard_map/ppermute | solution.py:299
  23.6 8.7 %collective-permute-start.10 = (bf16[1,2,4,64,512]{4,3,2,1,0:T(8,128)(2,1)S(1)}, bf16[1,2,4,64,512]{4,3,2,1,0:T(8,128)(2,1)S(1)}, u32[]{:S(2)}, u32[]{:S(2)}) collective-permute-start(bf16[1,2,4,64,512]{4,3,2,1,0:T(8,128)(2,1)S(1)} %get-tuple-element.21), channel_id=1, source_target_pairs={{0,1},{1,0},{2,3},{3,2},{4,5},{5,4},{6,7},{7,6},{8,9},{9,8},{10,11... | collective-permute-start | bytes 1572872 | tf_op jit(solution)/shard_map/ppermute | solution.py:299
  23.6 15.9 %collective-permute-start.5 = (bf16[256,1024]{1,0:T(8,128)(2,1)S(1)}, bf16[256,1024]{1,0:T(8,128)(2,1)S(1)}, u32[]{:S(2)}, u32[]{:S(2)}) collective-permute-start(bf16[256,1024]{1,0:T(8,128)(2,1)S(1)} %pad_maximum_fusion.refs_4_), channel_id=1, source_target_pairs={{0,1},{1,0},{2,3},{3,2},{4,5},{5,4},{6,7},{7,6},{8,9},{9,8},{10,11... | collective-permute-start | bytes 1572872 | tf_op jit(solution)/shard_map/ppermute | solution.py:299
  29.9 2.8 %collective-permute-start.2 = (bf16[128,1024]{1,0:T(8,128)(2,1)S(1)}, bf16[128,1024]{1,0:T(8,128)(2,1)S(1)}, u32[]{:S(2)}, u32[]{:S(2)}) collective-permute-start(bf16[128,1024]{1,0:T(8,128)(2,1)S(1)} %collective-permute-done.1.refs_2_), channel_id=1, source_target_pairs={{0,1},{1,0},{2,3},{3,2},{4,5},{5,4},{6,7},{7,6},{8,9},{9,8},{10,11... | collective-permute-start | bytes 786440 | tf_op jit(solution)/shard_map/ppermute | solution.py:299
  32.3 7.3 %collective-permute-start.9 = (bf16[256,1024]{1,0:T(8,128)(2,1)S(1)}, bf16[256,1024]{1,0:T(8,128)(2,1)S(1)}, u32[]{:S(2)}, u32[]{:S(2)}) collective-permute-start(bf16[256,1024]{1,0:T(8,128)(2,1)S(1)} %collective-permute-done.8.refs_8_), channel_id=1, source_target_pairs={{0,1},{1,0},{2,3},{3,2},{4,5},{5,4},{6,7},{7,6},{8,9},{9,8},{10,11... | collective-permute-start | bytes 1572872 | tf_op jit(solution)/shard_map/ppermute | solution.py:299
  32.3 7.2 %collective-permute-start.7 = (bf16[128,1024]{1,0:T(8,128)(2,1)S(1)}, bf16[128,1024]{1,0:T(8,128)(2,1)S(1)}, u32[]{:S(2)}, u32[]{:S(2)}) collective-permute-start(bf16[128,1024]{1,0:T(8,128)(2,1)S(1)} %collective-permute-done.6.refs_6_), channel_id=1, source_target_pairs={{0,1},{1,0},{2,3},{3,2},{4,5},{5,4},{6,7},{7,6},{8,9},{9,8},{10,11... | collective-permute-start | bytes 786440 | tf_op jit(solution)/shard_map/ppermute | solution.py:299
  32.8 11.3 %collective-permute-start.11 = (bf16[128,1024]{1,0:T(8,128)(2,1)S(1)}, bf16[128,1024]{1,0:T(8,128)(2,1)S(1)}, u32[]{:S(2)}, u32[]{:S(2)}) collective-permute-start(bf16[128,1024]{1,0:T(8,128)(2,1)S(1)} %collective-permute-done.6.refs_6_), channel_id=1, source_target_pairs={{0,4},{4,0},{8,12},{12,8},{16,20},{20,16},{24,28},{28,24},{1,5},{5... | collective-permute-start | bytes 786440 | tf_op jit(solution)/shard_map/ppermute | solution.py:299
  38.8 9.5 %collective-permute-start.14 = (bf16[1,2,4,64,512]{4,3,2,1,0:T(8,128)(2,1)S(1)}, bf16[1,2,4,64,512]{4,3,2,1,0:T(8,128)(2,1)S(1)}, u32[]{:S(2)}, u32[]{:S(2)}) collective-permute-start(bf16[1,2,4,64,512]{4,3,2,1,0:T(8,128)(2,1)S(1)} %slice.12), channel_id=1, source_target_pairs={{0,1},{1,0},{2,3},{3,2},{4,5},{5,4},{6,7},{7,6},{8,9},{9,8},{10,11... | collective-permute-start | bytes 1572872 | tf_op jit(solution)/shard_map/ppermute | solution.py:299
  44.1 1.7 %collective-permute-start.12 = (bf16[128,1024]{1,0:T(8,128)(2,1)S(1)}, bf16[128,1024]{1,0:T(8,128)(2,1)S(1)}, u32[]{:S(2)}, u32[]{:S(2)}) collective-permute-start(bf16[128,1024]{1,0:T(8,128)(2,1)S(1)} %collective-permute-done.11.refs_0_), channel_id=1, source_target_pairs={{0,1},{1,0},{2,3},{3,2},{4,5},{5,4},{6,7},{7,6},{8,9},{9,8},{10,11... | collective-permute-start | bytes 786440 | tf_op jit(solution)/shard_map/ppermute | solution.py:299
